TPU v7x, 32 devices: a whole 2x2x4 slice. The times are simulated.
32 devices in a mesh: parts: 2 (over y), beam: 8 (over z, x), head: 2 (over core).
Axes of the slice: x: 2, y: 2, z: 4, core: 2. Of those that a mesh axis runs over, the one named last changes fastest.
Arguments:
- states: float32 [32, 128, 4096], P(('parts', 'beam'), None, 'head'), parts along dimension 0, may hold values from -6 to 6
- decay_rates: float32 [32], P('head'), may hold values from 0.05 to 2
- queries: bfloat16 [2, 32, 4096], P(None, ('parts', 'beam'), 'head'), parts along dimension 1, may hold values from -0.59765625 to 0.59765625
- key_vectors: bfloat16 [2, 32, 4096], P(None, ('parts', 'beam'), 'head'), parts along dimension 1, may hold values from -6 to 6
- values: bfloat16 [2, 32, 4096], P(None, ('parts', 'beam'), 'head'), parts along dimension 1, may hold values from -6 to 6
- gate_logits: bfloat16 [2, 32, 4096], P(None, ('parts', 'beam'), 'head'), parts along dimension 1, may hold values from -6 to 6
- parents: int32 [2, 32], P(None, 'parts'), parts along dimension 1, may hold values from 0 to 15, as said below
- out_weight: bfloat16 [4096, 6144], P('head', 'beam'), may hold values from -0.09375 to 0.09375
Outputs:
- projected: bfloat16 [2, 32, 6144], P(None, ('parts', 'head'), 'beam'), parts along dimension 1
- final_states: float32 [32, 128, 4096], P(('parts', 'beam'), None, 'head'), parts along dimension 0
There are 2 independent parts, one for each index of `parts`. A program takes and returns all parts, laid end to end along the dimension named above; an argument that names none is the same for every part. Nothing has to cross between parts.
Inputs may be any that keep to these rules, and one draw needn't show every extreme that they name: Beam j of request r sits in slot j * 2 + r; a parent is a slot of the same request (parents[t, c] % 2 == c % 2); beam 0 of every request is the child of beam 0, and the last slot is the child of itself at each step.
All inputs are finite; a program needn't handle non-finite values.
Results may differ from a plain program's by a relative error of at most 0.0049.
Values may be sent and summed in bfloat16 or wider, within the bound.
No kernel may reach another device: no remote copies, remote signals or barrier semaphores. Data moves between devices by JAX's collectives and lax.ppermute only.
A program may use at most 64 MiB of HBM per device.

v0:
```python
import jax
import jax.numpy as jnp
from jax import lax
from jax.sharding import PartitionSpec as P


def fork(state, parent_list):
    row_state = lax.all_to_all(state, "beam", split_axis=1, concat_axis=0, tiled=True)
    picked = jnp.take(row_state, parent_list, axis=0)
    return lax.all_to_all(picked, "beam", split_axis=0, concat_axis=1, tiled=True)


def shards(states, decay_rates, queries, key_vectors, values, gate_logits, parents, out_weight):
    slot_count, head_dim, columns = states.shape
    groups = columns // head_dim
    decay = jnp.exp(-decay_rates)
    current = states
    readouts = []
    for step in range(parents.shape[0]):
        forked = fork(current, parents[step])
        query_f = queries[step].astype(jnp.float32).reshape(slot_count, groups, head_dim)
        key_f = key_vectors[step].astype(jnp.float32).reshape(slot_count, groups, head_dim)
        value_f = values[step].astype(jnp.float32).reshape(slot_count, groups, head_dim)
        grid = forked.reshape(slot_count, head_dim, groups, head_dim)
        updated = decay[None, None, :, None] * grid + jnp.einsum("shi,shj->sihj", key_f, value_f)
        readout = jnp.einsum("shi,sihj->shj", query_f, updated, precision=lax.Precision.HIGHEST)
        current, readout = (
            updated.reshape(slot_count, head_dim, columns),
            readout.reshape(slot_count, columns),
        )
        readouts.append(readout)
    stacked = jnp.stack(readouts)
    attn = (jax.nn.sigmoid(gate_logits.astype(jnp.float32)) * stacked).astype(jnp.bfloat16)
    terms = jnp.einsum(
        "tsc,cd->tsd",
        lax.all_gather(attn, "beam", axis=1, tiled=True),
        out_weight,
        preferred_element_type=jnp.float32,
    )
    projected = lax.psum_scatter(terms, "head", scatter_dimension=1, tiled=True).astype(
        jnp.bfloat16
    )
    return (projected, current)


def solution(mesh):
    in_specs = (
        P(("parts", "beam"), None, "head"),
        P("head"),
        P(None, ("parts", "beam"), "head"),
        P(None, ("parts", "beam"), "head"),
        P(None, ("parts", "beam"), "head"),
        P(None, ("parts", "beam"), "head"),
        P(None, "parts"),
        P("head", "beam"),
    )
    out_specs = (P(None, ("parts", "head"), "beam"), P(("parts", "beam"), None, "head"))
    return jax.shard_map(shards, mesh=mesh, in_specs=in_specs, out_specs=out_specs, check_vma=False)
```

profile of v0, /device:TPU:0, one launch (start us, length us, event | category | flops | bytes accessed | tf_op | source)
XLA Modules:
  0.0 310.4 jit_solution(6478587944526209887)
XLA Ops:
  7.2 0.0 copy-start
  7.2 4.7 %copy.21 = f32[2,128,2048]{2,0,1:T(2,128)} copy(f32[2,128,2048]{2,1,0:T(8,128)} %param.10) | data formatting | bytes 4194304 | tf_op args[0]
  11.9 0.0 copy-start.6
  11.9 7.4 %all-to-all-start = ((f32[2,128,2048]{2,0,1:T(2,128)}), f32[2,128,2048]{2,0,1:T(2,128)}, u32[]{:S(2)}, u32[]{:S(2)}) async-start(f32[2,128,2048]{2,0,1:T(2,128)} %copy.21), calls=%async_computation | async-start | bytes 4194304 | tf_op jit(solution)/shard_map/all_to_all | solution.py:8
  19.2 0.0 copy-done.6
  19.3 48.3 %all-to-all-done = f32[2,128,2048]{2,0,1:T(2,128)} async-done(((f32[2,128,2048]{2,0,1:T(2,128)}), f32[2,128,2048]{2,0,1:T(2,128)}, u32[]{:S(2)}, u32[]{:S(2)}) %all-to-all-start) | async-done | bytes 2097184 | tf_op jit(solution)/shard_map/all_to_all | solution.py:8
  67.6 2.8 copy.22
  70.4 1.5 copy.23
  71.9 3.6 %gather_fusion = f32[16,16,2048]{2,1,0:T(8,128)} fusion(f32[16,16,2048]{2,1,0:T(8,128)} %bitcast.83, s32[1024]{0:T(1024)S(1)} %pad_clamp_fusion.1), kind=kCustom, calls=%fused_computation.clone | custom fusion | bytes 4194368 | tf_op jit(solution)/shard_map/jit(_take)/gather | solution.py:9
  75.5 3.2 %broadcast_select_fusion.1 = f32[16,16,2048]{2,1,0:T(8,128)} fusion(f32[16,16,2048]{2,1,0:T(8,128)} %gather_fusion, pred[16]{0:T(512)(128)(4,1)S(1)} %get-tuple-element.13), kind=kLoop, calls=%fused_computation.13 | loop fusion | flops 524288 | bytes 4194320 | tf_op jit(solution)/shard_map/jit(_take)/select_n | solution.py:9
  78.7 0.0 copy-start.2
  78.7 0.0 copy-start.7
  78.7 0.0 copy-start.3
  78.7 4.5 %all-to-all-start.1 = ((f32[16,16,2048]{2,1,0:T(8,128)}), f32[16,16,2048]{2,1,0:T(8,128)}, u32[]{:S(2)}, u32[]{:S(2)}) async-start(f32[16,16,2048]{2,1,0:T(8,128)} %broadcast_select_fusion.1), calls=%async_computation.1 | async-start | bytes 4194304 | tf_op jit(solution)/shard_map/all_to_all | solution.py:10
  83.2 0.0 copy-done.2
  83.2 0.1 copy.25
  83.3 0.0 copy-done.7
  83.4 0.0 copy-done.3
  83.4 47.6 %all-to-all-done.1 = f32[16,16,2048]{2,1,0:T(8,128)} async-done(((f32[16,16,2048]{2,1,0:T(8,128)}), f32[16,16,2048]{2,1,0:T(8,128)}, u32[]{:S(2)}, u32[]{:S(2)}) %all-to-all-start.1) | async-done | bytes 2097184 | tf_op jit(solution)/shard_map/all_to_all | solution.py:10
  131.0 1.7 copy.24
  132.8 0.4 copy.38
  133.1 1.7 fusion.3
  134.8 2.7 reshape.60
  137.5 4.5 %copy.26 = f32[2,128,2048]{2,0,1:T(2,128)} copy(f32[2,128,2048]{2,1,0:T(8,128)} %reshape.60) | data formatting | bytes 4194304 | tf_op jit(solution)/shard_map/reshape | solution.py:28
  142.1 4.4 %all-to-all-start.2 = ((f32[2,128,2048]{2,0,1:T(2,128)}), f32[2,128,2048]{2,0,1:T(2,128)}, u32[]{:S(2)}, u32[]{:S(2)}) async-start(f32[2,128,2048]{2,0,1:T(2,128)} %copy.26), calls=%async_computation.2 | async-start | bytes 4194304 | tf_op jit(solution)/shard_map/all_to_all | solution.py:8
  146.4 47.8 %all-to-all-done.2 = f32[2,128,2048]{2,0,1:T(2,128)} async-done(((f32[2,128,2048]{2,0,1:T(2,128)}), f32[2,128,2048]{2,0,1:T(2,128)}, u32[]{:S(2)}, u32[]{:S(2)}) %all-to-all-start.2) | async-done | bytes 2097184 | tf_op jit(solution)/shard_map/all_to_all | solution.py:8
  194.2 2.8 copy.27
  197.0 1.5 copy.28
  198.5 3.6 %gather_fusion.1 = f32[16,16,2048]{2,1,0:T(8,128)} fusion(f32[16,16,2048]{2,1,0:T(8,128)} %bitcast.84, s32[1024]{0:T(1024)S(1)} %pad_clamp_fusion), kind=kCustom, calls=%fused_computation.1.clone | custom fusion | bytes 4194368 | tf_op jit(solution)/shard_map/jit(_take)/gather | solution.py:9
  202.1 3.2 %broadcast_select_fusion = f32[16,16,2048]{2,1,0:T(8,128)} fusion(f32[16,16,2048]{2,1,0:T(8,128)} %gather_fusion.1, pred[16]{0:T(512)(128)(4,1)S(1)} %get-tuple-element.3), kind=kLoop, calls=%fused_computation.12 | loop fusion | flops 524288 | bytes 4194320 | tf_op jit(solution)/shard_map/jit(_take)/select_n | solution.py:9
  205.3 0.0 copy-start.4
  205.3 4.5 %all-to-all-start.3 = ((f32[16,16,2048]{2,1,0:T(8,128)}), f32[16,16,2048]{2,1,0:T(8,128)}, u32[]{:S(2)}, u32[]{:S(2)}) async-start(f32[16,16,2048]{2,1,0:T(8,128)} %broadcast_select_fusion), calls=%async_computation.3 | async-start | bytes 4194304 | tf_op jit(solution)/shard_map/all_to_all | solution.py:10
  209.8 0.2 reduce-scatter.2.cloned.1.call-start
  210.0 0.0 copy-done.4
  210.1 0.1 copy.30
  210.2 3.1 %convolution_bitcast_fusion.1 = f32[1,2,2048]{2,0,1:T(1,128)S(1)} fusion(bf16[2,16,128,1]{2,3,1,0:T(2,128)(2,1)S(1)} %reshape.98, f32[2,128,16,128]{3,2,1,0:T(8,128)} %fusion.3), kind=kOutput, calls=%fused_computation.5 | convolution fusion | flops 6291456 | bytes 2121728 | tf_op jit(solution)/shard_map/shi,sihj->shj/dot_general | solution.py:26
  213.3 44.3 %all-to-all-done.3 = f32[16,16,2048]{2,1,0:T(8,128)} async-done(((f32[16,16,2048]{2,1,0:T(8,128)}), f32[16,16,2048]{2,1,0:T(8,128)}, u32[]{:S(2)}, u32[]{:S(2)}) %all-to-all-start.3) | async-done | bytes 2097184 | tf_op jit(solution)/shard_map/all_to_all | solution.py:10
  257.6 1.8 copy.29
  259.4 0.4 copy.41
  259.8 0.7 fusion.2
  260.5 0.0 copy-start.1
  260.6 1.3 copy-done.1
  261.9 0.0 copy-start.5
  261.9 1.6 convolution_bitcast_fusion
  263.5 0.0 copy-done.5
  263.5 0.1 fusion.7
  263.5 30.5 %all_gather.3 = bf16[2,16,2048]{2,0,1:T(2,128)(2,1)S(1)} all-gather(bf16[2,2,2048]{2,0,1:T(2,128)(2,1)S(1)} %fusion.7), channel_id=1, replica_groups=mesh['parts'=2,'beam'=8,'head'=2] {'beam'}, dimensions={1}, use_global_device_ids=true | all-gather | bytes 147456 | tf_op jit(solution)/shard_map/all_gather | solution.py:36
  294.1 0.0 copy-done
  294.1 1.3 fusion
  295.3 0.0 reduce-scatter.2.cloned.1.call-update
  295.4 2.7 reshape.65
  298.1 4.0 %reduce-scatter.2.cloned.1.call-done = f32[2,8,768]{2,1,0:T(8,128)} async-done(((f32[2,16,768]{2,1,0:T(8,128)}), f32[2,8,768]{2,1,0:T(8,128)}) %reduce-scatter.2.cloned.1.call-update) | async-done | bytes 49168 | tf_op jit(solution)/shard_map/reduce_scatter | solution.py:40
  302.1 1.4 convert_element_type.8
  (11 shorter events, 0.1 us)
Async XLA Ops:
  7.2 286.9 %copy-start = (bf16[2048,768]{1,0:T(8,128)(2,1)S(1)}, bf16[2048,768]{1,0:T(8,128)(2,1)}, u32[]{:S(2)}) copy-start(bf16[2048,768]{1,0:T(8,128)(2,1)} %param.17) | copy-start | bytes 9437188
  11.9 7.4 %copy-start.6 = (s32[2,16]{1,0:T(2,128)S(1)}, s32[2,16]{1,0:T(2,128)}, u32[]{:S(2)}) copy-start(s32[2,16]{1,0:T(2,128)} %param.16) | copy-start | bytes 388
  11.9 55.7 %all-to-all-start = ((f32[2,128,2048]{2,0,1:T(2,128)}), f32[2,128,2048]{2,0,1:T(2,128)}, u32[]{:S(2)}, u32[]{:S(2)}) async-start(f32[2,128,2048]{2,0,1:T(2,128)} %copy.21), calls=%async_computation | async-start | bytes 4194304 | tf_op jit(solution)/shard_map/all_to_all | solution.py:8
  78.7 4.5 %copy-start.2 = (bf16[2,2,2048]{2,1,0:T(2,128)(2,1)S(1)}, bf16[2,2,2048]{2,1,0:T(2,128)(2,1)}, u32[]{:S(2)}) copy-start(bf16[2,2,2048]{2,1,0:T(2,128)(2,1)} %param.13) | copy-start | bytes 49156
  78.7 4.6 %copy-start.7 = (f32[16]{0:T(128)S(1)}, f32[16]{0:T(128)}, u32[]{:S(2)}) copy-start(f32[16]{0:T(128)} %param.11) | copy-start | bytes 196
  78.7 4.7 %copy-start.3 = (bf16[2,2,2048]{2,1,0:T(2,128)(2,1)S(1)}, bf16[2,2,2048]{2,1,0:T(2,128)(2,1)}, u32[]{:S(2)}) copy-start(bf16[2,2,2048]{2,1,0:T(2,128)(2,1)} %param.14) | copy-start | bytes 49156
  78.7 52.3 %all-to-all-start.1 = ((f32[16,16,2048]{2,1,0:T(8,128)}), f32[16,16,2048]{2,1,0:T(8,128)}, u32[]{:S(2)}, u32[]{:S(2)}) async-start(f32[16,16,2048]{2,1,0:T(8,128)} %broadcast_select_fusion.1), calls=%async_computation.1 | async-start | bytes 4194304 | tf_op jit(solution)/shard_map/all_to_all | solution.py:10
  142.1 52.2 %all-to-all-start.2 = ((f32[2,128,2048]{2,0,1:T(2,128)}), f32[2,128,2048]{2,0,1:T(2,128)}, u32[]{:S(2)}, u32[]{:S(2)}) async-start(f32[2,128,2048]{2,0,1:T(2,128)} %copy.26), calls=%async_computation.2 | async-start | bytes 4194304 | tf_op jit(solution)/shard_map/all_to_all | solution.py:8
  205.3 4.7 %copy-start.4 = (bf16[2,2,2048]{2,1,0:T(2,128)(2,1)S(1)}, bf16[2,2,2048]{2,1,0:T(2,128)(2,1)}, u32[]{:S(2)}) copy-start(bf16[2,2,2048]{2,1,0:T(2,128)(2,1)} %param.12) | copy-start | bytes 49156
  205.3 52.3 %all-to-all-start.3 = ((f32[16,16,2048]{2,1,0:T(8,128)}), f32[16,16,2048]{2,1,0:T(8,128)}, u32[]{:S(2)}, u32[]{:S(2)}) async-start(f32[16,16,2048]{2,1,0:T(8,128)} %broadcast_select_fusion), calls=%async_computation.3 | async-start | bytes 4194304 | tf_op jit(solution)/shard_map/all_to_all | solution.py:10
  209.8 92.3 %reduce-scatter.2.cloned.1.call-start = ((), (), s32[]{:S(2)}) async-start(), calls=%async_computation.5 | async-start | bytes 147456 | tf_op jit(solution)/shard_map/reduce_scatter | solution.py:40
  260.5 1.3 copy-start.1
  261.9 1.6 copy-start.5
Sparse Core Ops, SparseCore 0:
  295.5 6.5 reduce-scatter.1
where the time goes:
time: 311 us; the launch traced here: 310 us
  waiting for transfers between devices  192 us (62%)
  local copies, waits for them, and re-layouts  36.2 us (12%)
  blocking collectives  30.5 us (10%)
  starting transfers between devices  20.9 us (7%)
  between operations  14.2 us (5%)
  other arithmetic  10.4 us (3%)
  matrix products  6.02 us (2%)
    all_to_all x2, waiting for transfers between devices, fork(): lax.all_to_all(state, 'beam', split_axis=1, concat_axis=0, tiled=True)  96.1 us
    all_to_all x2, waiting for transfers between devices, fork(): lax.all_to_all(picked, 'beam', split_axis=0, concat_axis=1, tiled=True)  91.9 us
    all_gather x1, blocking collectives, shards(): lax.all_gather(attn, 'beam', axis=1, tiled=True)  30.5 us
    all_to_all x2, starting transfers between devices, fork(): lax.all_to_all(state, 'beam', split_axis=1, concat_axis=0, tiled=True)  11.7 us
    reshape x3, local copies, waits for them, and re-layouts, shards(): updated.reshape(slot_count, head_dim, columns)  9.93 us
    all_to_all x2, starting transfers between devices, fork(): lax.all_to_all(picked, 'beam', split_axis=0, concat_axis=1, tiled=True)  8.95 us
    all_to_all x4, local copies, waits for them, and re-layouts, fork(): lax.all_to_all(state, 'beam', split_axis=1, concat_axis=0, tiled=True)  8.55 us
    gather x2, local copies, waits for them, and re-layouts, fork(): picked = jnp.take(row_state, parent_list, axis=0)  7.17 us
  transfers between devices with their start and end apart: 5, of which 5 were waited for; matrix products, arithmetic and copies ran while one was open for 2% of the time, Pallas kernels for 0%

commit v1 on v0

v1 whole, which is shorter than its diff:
```python
import functools

import jax
import jax.numpy as jnp
from jax import lax
from jax.experimental import pallas as pl
from jax.experimental.pallas import tpu as pltpu
from jax.sharding import PartitionSpec as P

F32, BF16 = jnp.float32, jnp.bfloat16
VMEM = pl.BlockSpec(memory_space=pltpu.VMEM)
SMEM = pl.BlockSpec(memory_space=pltpu.SMEM)
ANY = pl.BlockSpec(memory_space=pl.ANY)
STEPS, ARRAYS = 2, 4
Q, K, V, G = range(ARRAYS)
EXTRA = 16


def params(limit=48):
    return pltpu.CompilerParams(vmem_limit_bytes=limit << 20)


def cost(flops, moved):
    return pl.CostEstimate(flops=flops, bytes_accessed=moved, transcendentals=0)


def row_of(head, array, step):
    return head * ARRAYS * STEPS + array * STEPS + step


def pack_kernel(n, st, q, k, v, g, *rest):
    outs, rows = rest[:n], rest[n]
    slots, dim, columns = st.shape
    heads = columns // dim // n
    me = lax.axis_index("beam")
    for a, ref in enumerate((q, k, v, g)):
        whole = ref[...].astype(F32)
        for t in range(STEPS):
            for j in range(slots):
                rows[j, a * STEPS + t : a * STEPS + t + 1, :] = whole[t, j : j + 1]
    for x in range(n):
        first = (me ^ x) * heads
        for j in range(slots):
            extra = []
            for i in range(heads):
                at = pl.ds(pl.multiple_of((first + i) * dim, dim), dim)
                outs[x][j, i * dim : (i + 1) * dim, :] = st[j, :, at].astype(BF16)
                extra.append(rows[j, :, at])
            outs[x][j, heads * dim :, :] = jnp.concatenate(extra, 0).astype(BF16)


def pick_kernel(n, parents, *rest):
    ins, outs, (buf, sem_in, sem_out) = rest[:n], rest[n : 2 * n], rest[2 * n :]
    slots, rows, _ = ins[0].shape
    depth = rows - EXTRA
    me = lax.axis_index("beam")
    copies = []
    for x in range(n):
        at = pl.multiple_of((me ^ x) * slots, slots)
        copies.append(pltpu.make_async_copy(ins[x], buf.at[pl.ds(at, slots)], sem_in.at[x]))
        copies[-1].start()
    for c in copies:
        c.wait()
    copies = []
    for x in range(n):
        for j in range(slots):
            middle = parents[1, (me ^ x) * slots + j]
            root = parents[0, middle]
            copies.append(
                pltpu.make_async_copy(
                    buf.at[root, pl.ds(0, depth)], outs[x].at[j, pl.ds(0, depth)], sem_out.at[x, j, 0]
                )
            )
            copies.append(
                pltpu.make_async_copy(
                    buf.at[middle, pl.ds(depth, EXTRA)], outs[x].at[j, pl.ds(depth, EXTRA)], sem_out.at[x, j, 1]
                )
            )
            copies[-2].start()
            copies[-1].start()
    for c in copies:
        c.wait()


def readout_kernel(n, parents, decay, *rest):
    ins, out, vectors = rest[:n], rest[n], rest[n + 1]
    slots, rows, dim = ins[0].shape
    heads = (rows - EXTRA) // dim
    total = n * slots
    me = lax.axis_index("beam")
    for x in range(n):
        for j in range(slots):
            at = pl.multiple_of(((me ^ x) * slots + j) * EXTRA, EXTRA)
            vectors[pl.ds(at, EXTRA), :] = ins[x][j, heads * dim :, :].astype(F32)
    line = lax.broadcasted_iota(jnp.int32, (STEPS * total, dim), 0)
    mid_line = lax.broadcasted_iota(jnp.int32, (total, total), 0)
    source = jnp.zeros((STEPS * total, dim), jnp.int32)
    chosen = jnp.zeros((total, total), jnp.int32)
    for c in range(total):
        middle = parents[1, c]
        source = jnp.where(line == c, parents[0, c], source)
        source = jnp.where(line == total + c, parents[0, middle], source)
        chosen = jnp.where(mid_line == c, middle, chosen)
    pick = (chosen == lax.broadcasted_iota(jnp.int32, (total, total), 1)).astype(BF16)
    for i in range(heads):
        d = decay[me * heads + i]

        def get(array, step):
            return vectors[pl.ds(row_of(i, array, step), total, stride=EXTRA), :]

        q1, q2, k1, k2 = get(Q, 0), get(Q, 1), get(K, 0), get(K, 1)
        v1, v2 = get(V, 0), get(V, 1)
        queries = jnp.concatenate([q1, q2], 0)
        acc = jnp.zeros((STEPS * total, dim), F32)
        for x in range(n):
            for j in range(slots):
                slot = (me ^ x) * slots + j
                mine = jnp.where(source == slot, queries, 0.0).astype(BF16)
                acc += jnp.dot(mine, ins[x][j, i * dim : (i + 1) * dim, :], preferred_element_type=F32)
        k1m = jnp.dot(pick, k1.astype(BF16), preferred_element_type=F32)
        v1m = jnp.dot(pick, v1.astype(BF16), preferred_element_type=F32)
        r1 = d * acc[:total] + jnp.sum(q1 * k1, -1, keepdims=True) * v1
        r2 = d * (d * acc[total:] + jnp.sum(q2 * k1m, -1, keepdims=True) * v1m)
        r2 = r2 + jnp.sum(q2 * k2, -1, keepdims=True) * v2
        lanes = slice(i * dim, (i + 1) * dim)
        out[:total, lanes] = (jax.nn.sigmoid(get(G, 0)) * r1).astype(BF16)
        out[total:, lanes] = (jax.nn.sigmoid(get(G, 1)) * r2).astype(BF16)


def project_kernel(order, head_count, mine, theirs, weight, keep, send, terms):
    me, head = lax.axis_index("beam"), lax.axis_index("head")
    half, lines, depth = mine.shape
    acc = None
    for at, x in enumerate(order):
        rows = pl.ds(pl.multiple_of((me ^ x) * depth, depth), depth)
        lhs = mine[at] if at < half else theirs[at - half]
        term = jnp.dot(lhs, weight[rows, :], preferred_element_type=F32)
        acc = term if acc is None else acc + term
    terms[...] = acc
    part = lines // STEPS // head_count
    for t in range(STEPS):
        own = pl.multiple_of(t * part * head_count + head * part, part)
        other = pl.multiple_of(t * part * head_count + (1 - head) * part, part)
        keep[t] = terms[pl.ds(own, part), :]
        send[t] = terms[pl.ds(other, part), :]


def final_kernel(n, decay, k, v, *rest):
    ins, out, ks, vs = rest[:n], rest[n], rest[n + 1], rest[n + 2]
    slots, rows, dim = ins[0].shape
    heads = (rows - EXTRA) // dim
    me = lax.axis_index("beam")
    ks[...] = k[1].astype(F32)
    vs[...] = v[1].astype(F32)
    line = lax.broadcasted_iota(jnp.int32, (16, dim), 0)
    for x in range(n):
        for j in range(slots):
            extra = ins[x][j, heads * dim :, :].astype(F32)
            for i in range(heads):
                h = (me ^ x) * heads + i
                d = decay[h]
                at = pl.ds(pl.multiple_of(h * dim, dim), dim)
                at_k, at_v = row_of(i, K, 0), row_of(i, V, 0)
                k1, v1 = extra[at_k : at_k + 1], extra[at_v : at_v + 1]
                scaled = d * v1
                high = scaled.astype(BF16).astype(F32)
                low = scaled - high
                lhs = jnp.where(line < 2, k1, jnp.where(line == 2, ks[j : j + 1, at], 0.0))
                rhs = jnp.where(line == 0, high, jnp.where(line == 1, low, vs[j : j + 1, at]))
                outer = lax.dot_general(
                    lhs.astype(BF16), rhs.astype(BF16), (((0,), (0,)), ((), ())), preferred_element_type=F32
                )
                out[j, :, at] = (d * d) * ins[x][j, i * dim : (i + 1) * dim, :].astype(F32) + outer


def fast(n, head_count, states, decay_rates, queries, key_vectors, values, gate_logits, parents, out_weight):
    slots, dim, columns = states.shape
    heads = columns // dim // n
    total = n * slots
    rows = heads * dim + EXTRA
    chunk = jax.ShapeDtypeStruct((slots, rows, dim), BF16)
    decay = jnp.exp(-decay_rates)

    def swap(array, x):
        return lax.ppermute(array, "beam", [(j, j ^ x) for j in range(n)])

    packed = pl.pallas_call(
        functools.partial(pack_kernel, n),
        out_shape=[chunk] * n,
        in_specs=[VMEM] * 5,
        out_specs=[VMEM] * n,
        scratch_shapes=[pltpu.VMEM((slots, ARRAYS * STEPS, columns), F32)],
        compiler_params=params(),
    )(states, queries, key_vectors, values, gate_logits)
    middle = [packed[0]] + [swap(packed[x], x) for x in range(1, n)]
    picked = pl.pallas_call(
        functools.partial(pick_kernel, n),
        out_shape=[chunk] * n,
        in_specs=[SMEM] + [ANY] * n,
        out_specs=[ANY] * n,
        scratch_shapes=[
            pltpu.VMEM((total, rows, dim), BF16),
            pltpu.SemaphoreType.DMA((n,)),
            pltpu.SemaphoreType.DMA((n, slots, 2)),
        ],
        compiler_params=params(),
    )(parents, *middle)
    forked = [picked[0]] + [swap(picked[x], x) for x in range(1, n)]
    attn = pl.pallas_call(
        functools.partial(readout_kernel, n),
        out_shape=jax.ShapeDtypeStruct((STEPS * total, heads * dim), BF16),
        in_specs=[SMEM, SMEM] + [VMEM] * n,
        out_specs=VMEM,
        scratch_shapes=[pltpu.VMEM((total * EXTRA, dim), F32)],
        compiler_params=params(),
    )(parents, decay, *middle)
    have, order, hop = attn[None], [0], n // 2
    while hop:
        got = swap(have, hop)
        order = order + [x ^ hop for x in order]
        if hop > 1:
            have = jnp.concatenate([have, got], 0)
        hop //= 2
    part = total // head_count
    piece = jax.ShapeDtypeStruct((STEPS, part, out_weight.shape[1]), F32)
    keep, send = pl.pallas_call(
        functools.partial(project_kernel, order, head_count),
        out_shape=[piece, piece],
        in_specs=[VMEM] * 3,
        out_specs=[VMEM] * 2,
        scratch_shapes=[pltpu.VMEM((STEPS * total, out_weight.shape[1]), F32)],
        compiler_params=params(),
    )(have, got, out_weight)
    other = lax.ppermute(send, "head", [(0, 1), (1, 0)])
    projected = (keep + other).astype(BF16)
    final = pl.pallas_call(
        functools.partial(final_kernel, n),
        out_shape=jax.ShapeDtypeStruct(states.shape, F32),
        in_specs=[SMEM] + [VMEM] * (n + 2),
        out_specs=VMEM,
        scratch_shapes=[pltpu.VMEM((slots, columns), F32)] * 2,
        compiler_params=params(),
    )(decay, key_vectors, values, *forked)
    return projected, final


def fork(state, parent_list):
    row_state = lax.all_to_all(state, "beam", split_axis=1, concat_axis=0, tiled=True)
    picked = jnp.take(row_state, parent_list, axis=0)
    return lax.all_to_all(picked, "beam", split_axis=0, concat_axis=1, tiled=True)


def general(states, decay_rates, queries, key_vectors, values, gate_logits, parents, out_weight):
    slot_count, head_dim, columns = states.shape
    groups = columns // head_dim
    decay = jnp.exp(-decay_rates)
    current = states
    readouts = []
    for step in range(parents.shape[0]):
        forked = fork(current, parents[step])
        query_f = queries[step].astype(F32).reshape(slot_count, groups, head_dim)
        key_f = key_vectors[step].astype(F32).reshape(slot_count, groups, head_dim)
        value_f = values[step].astype(F32).reshape(slot_count, groups, head_dim)
        grid = forked.reshape(slot_count, head_dim, groups, head_dim)
        updated = decay[None, None, :, None] * grid + jnp.einsum("shi,shj->sihj", key_f, value_f)
        readout = jnp.einsum("shi,sihj->shj", query_f, updated, precision=lax.Precision.HIGHEST)
        current = updated.reshape(slot_count, head_dim, columns)
        readouts.append(readout.reshape(slot_count, columns))
    stacked = jnp.stack(readouts)
    attn = (jax.nn.sigmoid(gate_logits.astype(F32)) * stacked).astype(BF16)
    terms = jnp.einsum(
        "tsc,cd->tsd",
        lax.all_gather(attn, "beam", axis=1, tiled=True),
        out_weight,
        preferred_element_type=F32,
    )
    projected = lax.psum_scatter(terms, "head", scatter_dimension=1, tiled=True).astype(BF16)
    return (projected, current)


def solution(mesh):
    n, head_count = mesh.shape["beam"], mesh.shape["head"]

    def shards(*args):
        columns, dim = args[0].shape[2], args[0].shape[1]
        if n & (n - 1) == 0 and columns // dim == 2 * n and head_count == 2:
            return fast(n, head_count, *args)
        return general(*args)

    in_specs = (
        P(("parts", "beam"), None, "head"),
        P("head"),
        P(None, ("parts", "beam"), "head"),
        P(None, ("parts", "beam"), "head"),
        P(None, ("parts", "beam"), "head"),
        P(None, ("parts", "beam"), "head"),
        P(None, "parts"),
        P("head", "beam"),
    )
    out_specs = (P(None, ("parts", "head"), "beam"), P(("parts", "beam"), None, "head"))
    return jax.shard_map(shards, mesh=mesh, in_specs=in_specs, out_specs=out_specs, check_vma=False)
```

time: 311 us -> 79.3 us (0.25)
  waiting for transfers between devices: 192 us -> 27.4 us
  local copies, waits for them, and re-layouts: 36.2 us -> 5.14 us
  blocking collectives: 30.5 us -> 0 us
  starting transfers between devices: 20.9 us -> 35.1 us
  between operations: 14.2 us -> 0.73 us
  other arithmetic: 10.4 us -> 1.29 us
  Pallas kernels: 0 us -> 8.49 us
  matrix products: 6.02 us -> 0 us
    all_to_all x4 -> x0, waiting for transfers between devices: 188 us -> none  [the longest x2 96.1 us: fork(): lax.all_to_all(state, 'beam', split_axis=1, concat_axis=0, tiled=True)]
    ppermute x0 -> x18, starting transfers between devices: none -> 35.1 us  [the longest x17 35 us: swap(): return lax.ppermute(array, 'beam', [(j, j ^ x) for j in range(n)])]
    all_gather x1 -> x0, blocking collectives: 30.5 us -> none  [shards(): lax.all_gather(attn, 'beam', axis=1, tiled=True)]
    ppermute x0 -> x18, waiting for transfers between devices: none -> 27.4 us  [the longest x17 27.4 us: swap(): return lax.ppermute(array, 'beam', [(j, j ^ x) for j in range(n)])]
    all_to_all x4 -> x0, starting transfers between devices: 20.7 us -> none  [the longest x2 11.7 us: fork(): lax.all_to_all(state, 'beam', split_axis=1, concat_axis=0, tiled=True)]
    all_to_all x6 -> x0, local copies, waits for them, and re-layouts: 12.1 us -> none  [the longest x4 8.55 us: fork(): lax.all_to_all(state, 'beam', split_axis=1, concat_axis=0, tiled=True)]
    reshape x5 -> x0, local copies, waits for them, and re-layouts: 9.96 us -> none  [the longest x3 9.93 us: shards(): updated.reshape(slot_count, head_dim, columns)]
    pallas_call x0 -> x5, Pallas kernels: none -> 8.49 us  [the longest x1 4.1 us: fast(): pl.pallas_call(functools.partial(pick_kernel, n), out_shape=[chunk] * n,...]
  transfers between devices with their start and end apart: 5 -> 18, of which waited for: 5 -> 6; matrix products, arithmetic and copies ran while one was open for 2% -> 1% of each run, Pallas kernels for 0% -> 9%
where the time goes in v1:
time: 79.3 us; the launch traced here: 78.1 us
  starting transfers between devices  35.1 us (44%)
  waiting for transfers between devices  27.4 us (35%)
  Pallas kernels  8.49 us (11%)
  local copies, waits for them, and re-layouts  5.14 us (6%)
  other arithmetic  1.29 us (2%)
    ppermute x17, starting transfers between devices, swap(): return lax.ppermute(array, 'beam', [(j, j ^ x) for j in range(n)])  35 us
    ppermute x17, waiting for transfers between devices, swap(): return lax.ppermute(array, 'beam', [(j, j ^ x) for j in range(n)])  27.4 us
    unnamed x18, local copies, waits for them, and re-layouts  5.14 us
    pallas_call x1, Pallas kernels, fast(): pl.pallas_call(functools.partial(pick_kernel, n), out_shape=[chunk] * n,...  4.1 us
    pallas_call x1, Pallas kernels, fast(): pl.pallas_call(functools.partial(final_kernel, n), out_shape=jax.ShapeDty...  2.39 us
  transfers between devices with their start and end apart: 18, of which 6 were waited for; matrix products, arithmetic and copies ran while one was open for 1% of the time, Pallas kernels for 9%

profile of v1, /device:TPU:0, one launch (start us, length us, event | category | flops | bytes accessed | tf_op | source)
XLA Modules:
  0.0 78.1 jit_solution(1755120096142820339)
XLA Ops:
  0.6 0.0 copy-start.1
  0.6 1.6 %copy-done.1 = f32[2,128,2048]{2,1,0:T(8,128)S(1)} copy-done((f32[2,128,2048]{2,1,0:T(8,128)S(1)}, f32[2,128,2048]{2,1,0:T(8,128)}, u32[]{:S(2)}) %copy-start.1) | copy-done | bytes 2097176
  2.2 0.0 copy-start.2
  2.2 0.7 copy-done.2
  2.9 0.0 copy-start.4
  2.9 0.7 copy-done.4
  3.7 0.0 copy-start.6
  3.7 0.7 copy-done.6
  4.4 0.0 copy-start.7
  4.4 0.7 copy-done.7
  5.1 0.0 copy-start
  5.1 0.3 shard_map.95
  5.4 3.0 %collective-permute-start = (bf16[2,272,128]{2,1,0:T(8,128)(2,1)S(1)}, bf16[2,272,128]{2,1,0:T(8,128)(2,1)S(1)}, u32[]{:S(2)}, u32[]{:S(2)}) collective-permute-start(bf16[2,272,128]{2,1,0:T(8,128)(2,1)S(1)} %get-tuple-element.21), channel_id=1, source_target_pairs={{0,2},{2,0},{4,6},{6,4},{8,10},{10,8},{12,14},{14,12},{1,3},{3,1},... | collective-permute-start | bytes 417800 | tf_op jit(solution)/shard_map/ppermute | solution.py:185
  8.4 1.6 %collective-permute-start.1 = (bf16[2,272,128]{2,1,0:T(8,128)(2,1)S(1)}, bf16[2,272,128]{2,1,0:T(8,128)(2,1)S(1)}, u32[]{:S(2)}, u32[]{:S(2)}) collective-permute-start(bf16[2,272,128]{2,1,0:T(8,128)(2,1)S(1)} %get-tuple-element.22), channel_id=1, source_target_pairs={{0,4},{2,6},{4,0},{6,2},{8,12},{10,14},{12,8},{14,10},{1,5},{3,7},... | collective-permute-start | bytes 417800 | tf_op jit(solution)/shard_map/ppermute | solution.py:185
  10.0 0.0 collective-permute-start.2
  10.0 3.0 %collective-permute-start.3 = (bf16[2,272,128]{2,1,0:T(8,128)(2,1)S(1)}, bf16[2,272,128]{2,1,0:T(8,128)(2,1)S(1)}, u32[]{:S(2)}, u32[]{:S(2)}) collective-permute-start(bf16[2,272,128]{2,1,0:T(8,128)(2,1)S(1)} %get-tuple-element.24), channel_id=1, source_target_pairs={{0,8},{2,10},{4,12},{6,14},{8,0},{10,2},{12,4},{14,6},{1,9},{3,11}... | collective-permute-start | bytes 417800 | tf_op jit(solution)/shard_map/ppermute | solution.py:185
  13.0 1.3 %collective-permute-start.4 = (bf16[2,272,128]{2,1,0:T(8,128)(2,1)S(1)}, bf16[2,272,128]{2,1,0:T(8,128)(2,1)S(1)}, u32[]{:S(2)}, u32[]{:S(2)}) collective-permute-start(bf16[2,272,128]{2,1,0:T(8,128)(2,1)S(1)} %get-tuple-element.25), channel_id=1, source_target_pairs={{0,10},{2,8},{4,14},{6,12},{8,2},{10,0},{12,6},{14,4},{1,11},{3,9}... | collective-permute-start | bytes 417800 | tf_op jit(solution)/shard_map/ppermute | solution.py:185
  14.3 0.0 collective-permute-done.rest_1_
  14.3 3.6 %collective-permute-start.5 = (bf16[2,272,128]{2,1,0:T(8,128)(2,1)S(1)}, bf16[2,272,128]{2,1,0:T(8,128)(2,1)S(1)}, u32[]{:S(2)}, u32[]{:S(2)}) collective-permute-start(bf16[2,272,128]{2,1,0:T(8,128)(2,1)S(1)} %get-tuple-element.26), channel_id=1, source_target_pairs={{0,12},{2,14},{4,8},{6,10},{8,4},{10,6},{12,0},{14,2},{1,13},{3,15... | collective-permute-start | bytes 417800 | tf_op jit(solution)/shard_map/ppermute | solution.py:185
  17.9 1.9 %collective-permute-done.1.rest_2_ = bf16[2,272,128]{2,1,0:T(8,128)(2,1)S(1)} collective-permute-done((bf16[2,272,128]{2,1,0:T(8,128)(2,1)S(1)}, bf16[2,272,128]{2,1,0:T(8,128)(2,1)S(1)}, u32[]{:S(2)}, u32[]{:S(2)}) %collective-permute-start.1) | collective-permute-done | bytes 139296 | tf_op jit(solution)/shard_map/ppermute | solution.py:185
  19.8 0.9 %collective-permute-start.6 = (bf16[2,272,128]{2,1,0:T(8,128)(2,1)S(1)}, bf16[2,272,128]{2,1,0:T(8,128)(2,1)S(1)}, u32[]{:S(2)}, u32[]{:S(2)}) collective-permute-start(bf16[2,272,128]{2,1,0:T(8,128)(2,1)S(1)} %get-tuple-element.27), channel_id=1, source_target_pairs={{0,14},{2,12},{4,10},{6,8},{8,6},{10,4},{12,2},{14,0},{1,15},{3,13... | collective-permute-start | bytes 417800 | tf_op jit(solution)/shard_map/ppermute | solution.py:185
  20.7 0.7 negate_exponential_fusion.decay
  21.3 0.0 collective-permute-done.2.rest_3_
  21.3 0.0 collective-permute-done.3.rest_4_
  21.3 12.1 %collective-permute-done.4.rest_5_ = bf16[2,272,128]{2,1,0:T(8,128)(2,1)S(1)} collective-permute-done((bf16[2,272,128]{2,1,0:T(8,128)(2,1)S(1)}, bf16[2,272,128]{2,1,0:T(8,128)(2,1)S(1)}, u32[]{:S(2)}, u32[]{:S(2)}) %collective-permute-start.4) | collective-permute-done | bytes 139296 | tf_op jit(solution)/shard_map/ppermute | solution.py:185
  33.4 0.0 collective-permute-done.5.rest_6_
  33.4 0.0 collective-permute-done.6.rest_7_
  33.4 0.0 copy-start.8
  33.4 0.7 copy-done.8
  34.1 1.0 %shard_map.96 = bf16[32,256]{1,0:T(8,128)(2,1)S(1)} custom-call(s32[2,16]{1,0:T(2,128)S(1)} %copy-done.8, f32[16]{0:T(128)S(1)} %negate_exponential_fusion.decay, bf16[2,272,128]{2,1,0:T(8,128)(2,1)S(1)} %get-tuple-element.20.rest_0_, bf16[2,272,128]{2,1,0:T(8,128)(2,1)S(1)} %collective-permute-done.rest_1_, ...), custom_call_target="tpu_custom_call" | custom-call | tf_op jit(solution)/shard_map/pallas_call | solution.py:209
  35.1 7.0 %collective-permute-start.7 = (bf16[1,32,256]{2,1,0:T(8,128)(2,1)S(1)}, bf16[1,32,256]{2,1,0:T(8,128)(2,1)S(1)}, u32[]{:S(2)}, u32[]{:S(2)}) collective-permute-start(bf16[1,32,256]{2,1,0:T(8,128)(2,1)S(1)} %bitcast.1), channel_id=1, source_target_pairs={{0,8},{2,10},{4,12},{6,14},{8,0},{10,2},{12,4},{14,6},{1,9},{3,11}... | collective-permute-start | bytes 49160 | tf_op jit(solution)/shard_map/ppermute | solution.py:185
  42.2 1.7 %collective-permute-done.7 = bf16[1,32,256]{2,1,0:T(8,128)(2,1)S(1)} collective-permute-done((bf16[1,32,256]{2,1,0:T(8,128)(2,1)S(1)}, bf16[1,32,256]{2,1,0:T(8,128)(2,1)S(1)}, u32[]{:S(2)}, u32[]{:S(2)}) %collective-permute-start.7) | collective-permute-done | bytes 16416 | tf_op jit(solution)/shard_map/ppermute | solution.py:185
  43.9 0.0 copy-start.3
  43.9 0.0 copy-start.5
  43.9 1.3 %collective-permute-start.8 = (bf16[2,32,256]{2,1,0:T(8,128)(2,1)S(1)}, bf16[2,32,256]{2,1,0:T(8,128)(2,1)S(1)}, u32[]{:S(2)}, u32[]{:S(2)}) collective-permute-start(bf16[2,32,256]{2,1,0:T(8,128)(2,1)S(1)} %pad_maximum_fusion.1), channel_id=1, source_target_pairs={{0,4},{2,6},{4,0},{6,2},{8,12},{10,14},{12,8},{14,10},{1,5},{3,7},... | collective-permute-start | bytes 98312 | tf_op jit(solution)/shard_map/ppermute | solution.py:185
  45.2 4.1 %shard_map.98 = (bf16[2,272,128]{2,1,0:T(8,128)(2,1)S(1)}, bf16[2,272,128]{2,1,0:T(8,128)(2,1)S(1)}, bf16[2,272,128]{2,1,0:T(8,128)(2,1)S(1)}, bf16[2,272,128]{2...) custom-call(s32[2,16]{1,0:T(2,128)S(1)} %copy-done.8, ...), custom_call_target="tpu_custom_call" | custom-call | tf_op jit(solution)/shard_map/pallas_call | solution.py:196
  49.3 0.4 collective-permute-start.11
  49.7 1.1 %collective-permute-start.12 = (bf16[2,272,128]{2,1,0:T(8,128)(2,1)S(1)}, bf16[2,272,128]{2,1,0:T(8,128)(2,1)S(1)}, u32[]{:S(2)}, u32[]{:S(2)}) collective-permute-start(bf16[2,272,128]{2,1,0:T(8,128)(2,1)S(1)} %get-tuple-element.32), channel_id=1, source_target_pairs={{0,4},{2,6},{4,0},{6,2},{8,12},{10,14},{12,8},{14,10},{1,5},{3,7},... | collective-permute-start | bytes 417800 | tf_op jit(solution)/shard_map/ppermute | solution.py:185
  50.8 0.0 collective-permute-done.8
  50.8 1.4 %collective-permute-start.9 = (bf16[4,32,256]{2,1,0:T(8,128)(2,1)S(1)}, bf16[4,32,256]{2,1,0:T(8,128)(2,1)S(1)}, u32[]{:S(2)}, u32[]{:S(2)}) collective-permute-start(bf16[4,32,256]{2,1,0:T(8,128)(2,1)S(1)} %pad_maximum_fusion.mine), channel_id=1, source_target_pairs={{0,2},{2,0},{4,6},{6,4},{8,10},{10,8},{12,14},{14,12},{1,3},{3,1},... | collective-permute-start | bytes 196616 | tf_op jit(solution)/shard_map/ppermute | solution.py:185
  52.3 1.0 %collective-permute-start.13 = (bf16[2,272,128]{2,1,0:T(8,128)(2,1)S(1)}, bf16[2,272,128]{2,1,0:T(8,128)(2,1)S(1)}, u32[]{:S(2)}, u32[]{:S(2)}) collective-permute-start(bf16[2,272,128]{2,1,0:T(8,128)(2,1)S(1)} %get-tuple-element.33), channel_id=1, source_target_pairs={{0,6},{2,4},{4,2},{6,0},{8,14},{10,12},{12,10},{14,8},{1,7},{3,5},... | collective-permute-start | bytes 417800 | tf_op jit(solution)/shard_map/ppermute | solution.py:185
  53.3 2.1 %collective-permute-start.14 = (bf16[2,272,128]{2,1,0:T(8,128)(2,1)S(1)}, bf16[2,272,128]{2,1,0:T(8,128)(2,1)S(1)}, u32[]{:S(2)}, u32[]{:S(2)}) collective-permute-start(bf16[2,272,128]{2,1,0:T(8,128)(2,1)S(1)} %get-tuple-element.34), channel_id=1, source_target_pairs={{0,8},{2,10},{4,12},{6,14},{8,0},{10,2},{12,4},{14,6},{1,9},{3,11}... | collective-permute-start | bytes 417800 | tf_op jit(solution)/shard_map/ppermute | solution.py:185
  55.4 0.5 collective-permute-done.9.theirs
  55.8 3.8 %collective-permute-start.15 = (bf16[2,272,128]{2,1,0:T(8,128)(2,1)S(1)}, bf16[2,272,128]{2,1,0:T(8,128)(2,1)S(1)}, u32[]{:S(2)}, u32[]{:S(2)}) collective-permute-start(bf16[2,272,128]{2,1,0:T(8,128)(2,1)S(1)} %get-tuple-element.35), channel_id=1, source_target_pairs={{0,10},{2,8},{4,14},{6,12},{8,2},{10,0},{12,6},{14,4},{1,11},{3,9}... | collective-permute-start | bytes 417800 | tf_op jit(solution)/shard_map/ppermute | solution.py:185
  59.6 0.0 collective-permute-done.11.rest_1_
  59.6 1.1 %collective-permute-start.16 = (bf16[2,272,128]{2,1,0:T(8,128)(2,1)S(1)}, bf16[2,272,128]{2,1,0:T(8,128)(2,1)S(1)}, u32[]{:S(2)}, u32[]{:S(2)}) collective-permute-start(bf16[2,272,128]{2,1,0:T(8,128)(2,1)S(1)} %get-tuple-element.36), channel_id=1, source_target_pairs={{0,12},{2,14},{4,8},{6,10},{8,4},{10,6},{12,0},{14,2},{1,13},{3,15... | collective-permute-start | bytes 417800 | tf_op jit(solution)/shard_map/ppermute | solution.py:185
  60.7 0.0 collective-permute-done.12.rest_2_
  60.7 2.5 %collective-permute-start.17 = (bf16[2,272,128]{2,1,0:T(8,128)(2,1)S(1)}, bf16[2,272,128]{2,1,0:T(8,128)(2,1)S(1)}, u32[]{:S(2)}, u32[]{:S(2)}) collective-permute-start(bf16[2,272,128]{2,1,0:T(8,128)(2,1)S(1)} %get-tuple-element.37), channel_id=1, source_target_pairs={{0,14},{2,12},{4,10},{6,8},{8,6},{10,4},{12,2},{14,0},{1,15},{3,13... | collective-permute-start | bytes 417800 | tf_op jit(solution)/shard_map/ppermute | solution.py:185
  63.1 0.0 copy-done
  63.1 0.7 shard_map.97
  63.8 0.0 collective-permute-done.13.rest_3_
  63.8 0.1 collective-permute-start.10
  63.9 7.1 %collective-permute-done.14.rest_4_ = bf16[2,272,128]{2,1,0:T(8,128)(2,1)S(1)} collective-permute-done((bf16[2,272,128]{2,1,0:T(8,128)(2,1)S(1)}, bf16[2,272,128]{2,1,0:T(8,128)(2,1)S(1)}, u32[]{:S(2)}, u32[]{:S(2)}) %collective-permute-start.14) | collective-permute-done | bytes 139296 | tf_op jit(solution)/shard_map/ppermute | solution.py:185
  71.0 4.1 %collective-permute-done.15.rest_5_ = bf16[2,272,128]{2,1,0:T(8,128)(2,1)S(1)} collective-permute-done((bf16[2,272,128]{2,1,0:T(8,128)(2,1)S(1)}, bf16[2,272,128]{2,1,0:T(8,128)(2,1)S(1)}, u32[]{:S(2)}, u32[]{:S(2)}) %collective-permute-start.15) | collective-permute-done | bytes 139296 | tf_op jit(solution)/shard_map/ppermute | solution.py:185
  75.1 0.0 collective-permute-done.16.rest_6_
  75.1 0.0 collective-permute-done.17.rest_7_
  75.1 0.0 copy-done.3
  75.1 0.0 copy-done.5
  75.1 2.4 %shard_map.99 = f32[2,128,2048]{2,1,0:T(8,128)} custom-call(f32[16]{0:T(128)S(1)} %negate_exponential_fusion.decay, bf16[2,2,2048]{2,1,0:T(2,128)(2,1)S(1)} %copy-done.3, bf16[2,2,2048]{2,1,0:T(2,128)(2,1)S(1)} %copy-done.5, bf16[2,272,128]{2,1,0:T(8,128)(2,1)S(1)} %get-tuple-element.30.rest_0_, bf16[2,272,128]{2,1,0:T(8,128)(2,1)S(1)} %collective-permute-done.11.rest_1_, ...), custom_call_target="tpu_custom_call" | custom-call | tf_op jit(solution)/shard_map/pallas_call | solution.py:236
  77.5 0.0 collective-permute-done.10
  77.5 0.6 add_convert_fusion
  (2 shorter events, 0.0 us)
Async XLA Ops:
  0.6 1.6 %copy-start.1 = (f32[2,128,2048]{2,1,0:T(8,128)S(1)}, f32[2,128,2048]{2,1,0:T(8,128)}, u32[]{:S(2)}) copy-start(f32[2,128,2048]{2,1,0:T(8,128)} %st.1) | copy-start | bytes 6291460
  2.2 0.7 copy-start.2
  2.9 0.7 copy-start.4
  3.7 0.7 copy-start.6
  4.4 0.7 copy-start.7
  5.1 58.1 %copy-start = (bf16[2048,768]{1,0:T(8,128)(2,1)S(1)}, bf16[2048,768]{1,0:T(8,128)(2,1)}, u32[]{:S(2)}) copy-start(bf16[2048,768]{1,0:T(8,128)(2,1)} %weight.1) | copy-start | bytes 9437188
  5.4 8.9 %collective-permute-start = (bf16[2,272,128]{2,1,0:T(8,128)(2,1)S(1)}, bf16[2,272,128]{2,1,0:T(8,128)(2,1)S(1)}, u32[]{:S(2)}, u32[]{:S(2)}) collective-permute-start(bf16[2,272,128]{2,1,0:T(8,128)(2,1)S(1)} %get-tuple-element.21), channel_id=1, source_target_pairs={{0,2},{2,0},{4,6},{6,4},{8,10},{10,8},{12,14},{14,12},{1,3},{3,1},... | collective-permute-start | bytes 417800 | tf_op jit(solution)/shard_map/ppermute | solution.py:185
  8.4 11.4 %collective-permute-start.1 = (bf16[2,272,128]{2,1,0:T(8,128)(2,1)S(1)}, bf16[2,272,128]{2,1,0:T(8,128)(2,1)S(1)}, u32[]{:S(2)}, u32[]{:S(2)}) collective-permute-start(bf16[2,272,128]{2,1,0:T(8,128)(2,1)S(1)} %get-tuple-element.22), channel_id=1, source_target_pairs={{0,4},{2,6},{4,0},{6,2},{8,12},{10,14},{12,8},{14,10},{1,5},{3,7},... | collective-permute-start | bytes 417800 | tf_op jit(solution)/shard_map/ppermute | solution.py:185
  10.0 11.3 %collective-permute-start.2 = (bf16[2,272,128]{2,1,0:T(8,128)(2,1)S(1)}, bf16[2,272,128]{2,1,0:T(8,128)(2,1)S(1)}, u32[]{:S(2)}, u32[]{:S(2)}) collective-permute-start(bf16[2,272,128]{2,1,0:T(8,128)(2,1)S(1)} %get-tuple-element.23), channel_id=1, source_target_pairs={{0,6},{2,4},{4,2},{6,0},{8,14},{10,12},{12,10},{14,8},{1,7},{3,5},... | collective-permute-start | bytes 417800 | tf_op jit(solution)/shard_map/ppermute | solution.py:185
  10.0 11.3 %collective-permute-start.3 = (bf16[2,272,128]{2,1,0:T(8,128)(2,1)S(1)}, bf16[2,272,128]{2,1,0:T(8,128)(2,1)S(1)}, u32[]{:S(2)}, u32[]{:S(2)}) collective-permute-start(bf16[2,272,128]{2,1,0:T(8,128)(2,1)S(1)} %get-tuple-element.24), channel_id=1, source_target_pairs={{0,8},{2,10},{4,12},{6,14},{8,0},{10,2},{12,4},{14,6},{1,9},{3,11}... | collective-permute-start | bytes 417800 | tf_op jit(solution)/shard_map/ppermute | solution.py:185
  13.0 20.4 %collective-permute-start.4 = (bf16[2,272,128]{2,1,0:T(8,128)(2,1)S(1)}, bf16[2,272,128]{2,1,0:T(8,128)(2,1)S(1)}, u32[]{:S(2)}, u32[]{:S(2)}) collective-permute-start(bf16[2,272,128]{2,1,0:T(8,128)(2,1)S(1)} %get-tuple-element.25), channel_id=1, source_target_pairs={{0,10},{2,8},{4,14},{6,12},{8,2},{10,0},{12,6},{14,4},{1,11},{3,9}... | collective-permute-start | bytes 417800 | tf_op jit(solution)/shard_map/ppermute | solution.py:185
  14.3 19.1 %collective-permute-start.5 = (bf16[2,272,128]{2,1,0:T(8,128)(2,1)S(1)}, bf16[2,272,128]{2,1,0:T(8,128)(2,1)S(1)}, u32[]{:S(2)}, u32[]{:S(2)}) collective-permute-start(bf16[2,272,128]{2,1,0:T(8,128)(2,1)S(1)} %get-tuple-element.26), channel_id=1, source_target_pairs={{0,12},{2,14},{4,8},{6,10},{8,4},{10,6},{12,0},{14,2},{1,13},{3,15... | collective-permute-start | bytes 417800 | tf_op jit(solution)/shard_map/ppermute | solution.py:185
  19.8 13.6 %collective-permute-start.6 = (bf16[2,272,128]{2,1,0:T(8,128)(2,1)S(1)}, bf16[2,272,128]{2,1,0:T(8,128)(2,1)S(1)}, u32[]{:S(2)}, u32[]{:S(2)}) collective-permute-start(bf16[2,272,128]{2,1,0:T(8,128)(2,1)S(1)} %get-tuple-element.27), channel_id=1, source_target_pairs={{0,14},{2,12},{4,10},{6,8},{8,6},{10,4},{12,2},{14,0},{1,15},{3,13... | collective-permute-start | bytes 417800 | tf_op jit(solution)/shard_map/ppermute | solution.py:185
  33.4 0.7 copy-start.8
  35.1 8.8 %collective-permute-start.7 = (bf16[1,32,256]{2,1,0:T(8,128)(2,1)S(1)}, bf16[1,32,256]{2,1,0:T(8,128)(2,1)S(1)}, u32[]{:S(2)}, u32[]{:S(2)}) collective-permute-start(bf16[1,32,256]{2,1,0:T(8,128)(2,1)S(1)} %bitcast.1), channel_id=1, source_target_pairs={{0,8},{2,10},{4,12},{6,14},{8,0},{10,2},{12,4},{14,6},{1,9},{3,11}... | collective-permute-start | bytes 49160 | tf_op jit(solution)/shard_map/ppermute | solution.py:185
  43.9 31.2 %copy-start.3 = (bf16[2,2,2048]{2,1,0:T(2,128)(2,1)S(1)}, bf16[2,2,2048]{2,1,0:T(2,128)(2,1)}, u32[]{:S(2)}) copy-start(bf16[2,2,2048]{2,1,0:T(2,128)(2,1)} %k.3) | copy-start | bytes 49156
  43.9 31.2 %copy-start.5 = (bf16[2,2,2048]{2,1,0:T(2,128)(2,1)S(1)}, bf16[2,2,2048]{2,1,0:T(2,128)(2,1)}, u32[]{:S(2)}) copy-start(bf16[2,2,2048]{2,1,0:T(2,128)(2,1)} %v.3) | copy-start | bytes 49156
  43.9 6.9 %collective-permute-start.8 = (bf16[2,32,256]{2,1,0:T(8,128)(2,1)S(1)}, bf16[2,32,256]{2,1,0:T(8,128)(2,1)S(1)}, u32[]{:S(2)}, u32[]{:S(2)}) collective-permute-start(bf16[2,32,256]{2,1,0:T(8,128)(2,1)S(1)} %pad_maximum_fusion.1), channel_id=1, source_target_pairs={{0,4},{2,6},{4,0},{6,2},{8,12},{10,14},{12,8},{14,10},{1,5},{3,7},... | collective-permute-start | bytes 98312 | tf_op jit(solution)/shard_map/ppermute | solution.py:185
  49.3 10.3 %collective-permute-start.11 = (bf16[2,272,128]{2,1,0:T(8,128)(2,1)S(1)}, bf16[2,272,128]{2,1,0:T(8,128)(2,1)S(1)}, u32[]{:S(2)}, u32[]{:S(2)}) collective-permute-start(bf16[2,272,128]{2,1,0:T(8,128)(2,1)S(1)} %get-tuple-element.31), channel_id=1, source_target_pairs={{0,2},{2,0},{4,6},{6,4},{8,10},{10,8},{12,14},{14,12},{1,3},{3,1},... | collective-permute-start | bytes 417800 | tf_op jit(solution)/shard_map/ppermute | solution.py:185
  49.7 11.0 %collective-permute-start.12 = (bf16[2,272,128]{2,1,0:T(8,128)(2,1)S(1)}, bf16[2,272,128]{2,1,0:T(8,128)(2,1)S(1)}, u32[]{:S(2)}, u32[]{:S(2)}) collective-permute-start(bf16[2,272,128]{2,1,0:T(8,128)(2,1)S(1)} %get-tuple-element.32), channel_id=1, source_target_pairs={{0,4},{2,6},{4,0},{6,2},{8,12},{10,14},{12,8},{14,10},{1,5},{3,7},... | collective-permute-start | bytes 417800 | tf_op jit(solution)/shard_map/ppermute | solution.py:185
  50.8 5.0 %collective-permute-start.9 = (bf16[4,32,256]{2,1,0:T(8,128)(2,1)S(1)}, bf16[4,32,256]{2,1,0:T(8,128)(2,1)S(1)}, u32[]{:S(2)}, u32[]{:S(2)}) collective-permute-start(bf16[4,32,256]{2,1,0:T(8,128)(2,1)S(1)} %pad_maximum_fusion.mine), channel_id=1, source_target_pairs={{0,2},{2,0},{4,6},{6,4},{8,10},{10,8},{12,14},{14,12},{1,3},{3,1},... | collective-permute-start | bytes 196616 | tf_op jit(solution)/shard_map/ppermute | solution.py:185
  52.3 11.5 %collective-permute-start.13 = (bf16[2,272,128]{2,1,0:T(8,128)(2,1)S(1)}, bf16[2,272,128]{2,1,0:T(8,128)(2,1)S(1)}, u32[]{:S(2)}, u32[]{:S(2)}) collective-permute-start(bf16[2,272,128]{2,1,0:T(8,128)(2,1)S(1)} %get-tuple-element.33), channel_id=1, source_target_pairs={{0,6},{2,4},{4,2},{6,0},{8,14},{10,12},{12,10},{14,8},{1,7},{3,5},... | collective-permute-start | bytes 417800 | tf_op jit(solution)/shard_map/ppermute | solution.py:185
  53.3 17.7 %collective-permute-start.14 = (bf16[2,272,128]{2,1,0:T(8,128)(2,1)S(1)}, bf16[2,272,128]{2,1,0:T(8,128)(2,1)S(1)}, u32[]{:S(2)}, u32[]{:S(2)}) collective-permute-start(bf16[2,272,128]{2,1,0:T(8,128)(2,1)S(1)} %get-tuple-element.34), channel_id=1, source_target_pairs={{0,8},{2,10},{4,12},{6,14},{8,0},{10,2},{12,4},{14,6},{1,9},{3,11}... | collective-permute-start | bytes 417800 | tf_op jit(solution)/shard_map/ppermute | solution.py:185
  55.8 19.3 %collective-permute-start.15 = (bf16[2,272,128]{2,1,0:T(8,128)(2,1)S(1)}, bf16[2,272,128]{2,1,0:T(8,128)(2,1)S(1)}, u32[]{:S(2)}, u32[]{:S(2)}) collective-permute-start(bf16[2,272,128]{2,1,0:T(8,128)(2,1)S(1)} %get-tuple-element.35), channel_id=1, source_target_pairs={{0,10},{2,8},{4,14},{6,12},{8,2},{10,0},{12,6},{14,4},{1,11},{3,9}... | collective-permute-start | bytes 417800 | tf_op jit(solution)/shard_map/ppermute | solution.py:185
  59.6 15.5 %collective-permute-start.16 = (bf16[2,272,128]{2,1,0:T(8,128)(2,1)S(1)}, bf16[2,272,128]{2,1,0:T(8,128)(2,1)S(1)}, u32[]{:S(2)}, u32[]{:S(2)}) collective-permute-start(bf16[2,272,128]{2,1,0:T(8,128)(2,1)S(1)} %get-tuple-element.36), channel_id=1, source_target_pairs={{0,12},{2,14},{4,8},{6,10},{8,4},{10,6},{12,0},{14,2},{1,13},{3,15... | collective-permute-start | bytes 417800 | tf_op jit(solution)/shard_map/ppermute | solution.py:185
  60.7 14.5 %collective-permute-start.17 = (bf16[2,272,128]{2,1,0:T(8,128)(2,1)S(1)}, bf16[2,272,128]{2,1,0:T(8,128)(2,1)S(1)}, u32[]{:S(2)}, u32[]{:S(2)}) collective-permute-start(bf16[2,272,128]{2,1,0:T(8,128)(2,1)S(1)} %get-tuple-element.37), channel_id=1, source_target_pairs={{0,14},{2,12},{4,10},{6,8},{8,6},{10,4},{12,2},{14,0},{1,15},{3,13... | collective-permute-start | bytes 417800 | tf_op jit(solution)/shard_map/ppermute | solution.py:185
  63.8 13.7 %collective-permute-start.10 = (f32[2,8,768]{2,1,0:T(8,128)S(1)}, f32[2,8,768]{2,1,0:T(8,128)S(1)}, u32[]{:S(2)}, u32[]{:S(2)}) collective-permute-start(f32[2,8,768]{2,1,0:T(8,128)S(1)} %get-tuple-element.29), channel_id=1, source_target_pairs={{0,1},{1,0},{2,3},{3,2},{4,5},{5,4},{6,7},{7,6},{8,9},{9,8},{10,11... | collective-permute-start | bytes 147464 | tf_op jit(solution)/shard_map/ppermute | solution.py:234

commit v2 on v1

v2 whole, which is shorter than its diff:
```python
import functools

import jax
import jax.numpy as jnp
from jax import lax
from jax.experimental import pallas as pl
from jax.experimental.pallas import tpu as pltpu
from jax.sharding import PartitionSpec as P

F32, BF16 = jnp.float32, jnp.bfloat16
VMEM = pl.BlockSpec(memory_space=pltpu.VMEM)
SMEM = pl.BlockSpec(memory_space=pltpu.SMEM)
ANY = pl.BlockSpec(memory_space=pl.ANY)
STEPS, ARRAYS = 2, 4
Q, K, V, G = range(ARRAYS)
EXTRA = 16
KEPT = 8


def params(limit=48):
    return pltpu.CompilerParams(vmem_limit_bytes=limit << 20)


def cost(flops, moved):
    return pl.CostEstimate(flops=flops, bytes_accessed=moved, transcendentals=0)


def row_of(head, array, step):
    return head * ARRAYS * STEPS + array * STEPS + step


def by_partner(order, refs):
    return [ref for _, ref in sorted(zip(order, refs), key=lambda pair: pair[0])]


def pack_kernel(n, order, st_hbm, q, k, v, g, parents_hbm, *rest):
    outs, (parents, st, vectors, rows, sem, sem_small) = by_partner(order, rest[:n]), rest[n:]
    slots, dim, columns = st.shape
    heads = columns // dim // n
    me = lax.axis_index("beam")

    def lanes(head, count):
        return pl.ds(pl.multiple_of(head * dim, dim), count * dim)

    small = [pltpu.make_async_copy(ref, vectors.at[a], sem_small.at[a]) for a, ref in enumerate((q, k, v, g))]
    small.append(pltpu.make_async_copy(parents_hbm, parents, sem_small.at[ARRAYS]))
    large = {}
    for x in order:
        at = lanes((me ^ x) * heads, heads)
        large[x] = pltpu.make_async_copy(st_hbm.at[:, :, at], st.at[:, :, at], sem.at[x])
    for c in small + list(large.values()):
        c.start()
    for a in range(ARRAYS):
        small[a].wait()
        whole = vectors[a].astype(F32)
        for t in range(STEPS):
            for j in range(slots):
                rows[j, a * STEPS + t : a * STEPS + t + 1, :] = whole[t, j : j + 1]
    for x in order:
        large[x].wait()
        first = (me ^ x) * heads
        for j in range(slots):
            extra = []
            for i in range(heads):
                at = lanes(first + i, 1)
                outs[x][j, i * dim : (i + 1) * dim, :] = st[j, :, at].astype(BF16)
                extra.append(rows[j, :, at])
            outs[x][j, heads * dim :, :] = jnp.concatenate(extra, 0).astype(BF16)
    small[ARRAYS].wait()


def middle_kernel(n, order, parents, decay, *rest):
    ins, outs, (buf, vectors, kept) = by_partner(order, rest[:n]), by_partner(order, rest[n : 2 * n]), rest[2 * n :]
    slots, rows, dim = ins[0].shape
    depth = rows - EXTRA
    heads = depth // dim
    total = n * slots
    me = lax.axis_index("beam")
    for x in range(n):
        for j in range(slots):
            slot = (me ^ x) * slots + j
            buf[slot] = ins[x][j, :depth, :]
            at = pl.multiple_of(slot * EXTRA, EXTRA)
            vectors[pl.ds(at, EXTRA), :] = ins[x][j, depth:, :].astype(F32)
    for x in range(n):
        for j in range(slots):
            middle = parents[1, (me ^ x) * slots + j]
            outs[x][j * depth : (j + 1) * depth, :] = buf[parents[0, middle]]
            for i in range(heads):
                for place, array in enumerate((K, V)):
                    to = j * KEPT + i * 2 + place
                    kept[to : to + 1, :] = vectors[pl.ds(middle * EXTRA + row_of(i, array, 0), 1), :]
        outs[x][slots * depth : slots * (depth + KEPT), :] = kept[...].astype(BF16)
    line = lax.broadcasted_iota(jnp.int32, (STEPS * total, dim), 0)
    mid_line = lax.broadcasted_iota(jnp.int32, (total, total), 0)
    source = jnp.zeros((STEPS * total, dim), jnp.int32)
    chosen = jnp.zeros((total, total), jnp.int32)
    for c in range(total):
        middle = parents[1, c]
        source = jnp.where(line == c, parents[0, c], source)
        source = jnp.where(line == total + c, parents[0, middle], source)
        chosen = jnp.where(mid_line == c, middle, chosen)
    pick = (chosen == lax.broadcasted_iota(jnp.int32, (total, total), 1)).astype(BF16)
    for i in range(heads):
        d = decay[pl.ds(me * heads + i, 1), :]

        def get(array, step):
            return vectors[pl.ds(row_of(i, array, step), total, stride=EXTRA), :]

        q1, q2, k1, k2 = get(Q, 0), get(Q, 1), get(K, 0), get(K, 1)
        v1, v2 = get(V, 0), get(V, 1)
        queries = jnp.concatenate([q1, q2], 0)
        acc = jnp.zeros((STEPS * total, dim), F32)
        for slot in range(total):
            mine = jnp.where(source == slot, queries, 0.0).astype(BF16)
            acc += jnp.dot(mine, buf[slot, i * dim : (i + 1) * dim, :], preferred_element_type=F32)
        k1m = jnp.dot(pick, k1.astype(BF16), preferred_element_type=F32)
        v1m = jnp.dot(pick, v1.astype(BF16), preferred_element_type=F32)
        r1 = d * acc[:total] + jnp.sum(q1 * k1, -1, keepdims=True) * v1
        r2 = d * (d * acc[total:] + jnp.sum(q2 * k1m, -1, keepdims=True) * v1m)
        r2 = r2 + jnp.sum(q2 * k2, -1, keepdims=True) * v2
        attn = [jax.nn.sigmoid(get(G, 0)) * r1, jax.nn.sigmoid(get(G, 1)) * r2]
        attn = jnp.concatenate(attn, 0).astype(BF16)
        at = slots * (depth + KEPT) + i * STEPS * total
        for x in range(n):
            outs[x][at : at + STEPS * total, :] = attn


def project_kernel(n, order, head_count, slots, weight, *rest):
    ins, (keep, send, terms) = by_partner(order, rest[:n]), rest[n:]
    me, head = lax.axis_index("beam"), lax.axis_index("head")
    lines, dim = terms.shape[0], ins[0].shape[1]
    heads = weight.shape[0] // dim // n
    first = slots * (heads * dim + KEPT)
    acc = None
    for x in range(n):
        rows = pl.ds(pl.multiple_of((me ^ x) * heads * dim, dim), heads * dim)
        lhs = [ins[x][first + i * lines : first + (i + 1) * lines, :] for i in range(heads)]
        term = jnp.dot(jnp.concatenate(lhs, 1), weight[rows, :], preferred_element_type=F32)
        acc = term if acc is None else acc + term
    terms[...] = acc
    part = lines // STEPS // head_count
    for t in range(STEPS):
        own = pl.multiple_of(t * part * head_count + head * part, part)
        other = pl.multiple_of(t * part * head_count + (1 - head) * part, part)
        keep[t] = terms[pl.ds(own, part), :]
        send[t] = terms[pl.ds(other, part), :]


def final_kernel(n, order, decay, k, v, *rest):
    ins, (out, ks, vs) = by_partner(order, rest[:n]), rest[n:]
    slots, dim, columns = out.shape
    heads = columns // dim // n
    depth = heads * dim
    me = lax.axis_index("beam")
    ks[...] = k[1].astype(F32)
    vs[...] = v[1].astype(F32)
    line = lax.broadcasted_iota(jnp.int32, (16, dim), 0)
    for x in range(n):
        extra = ins[x][slots * depth : slots * (depth + KEPT), :].astype(F32)
        for j in range(slots):
            for i in range(heads):
                h = (me ^ x) * heads + i
                d = decay[pl.ds(h, 1), :]
                at = pl.ds(pl.multiple_of(h * dim, dim), dim)
                row = j * KEPT + i * 2
                k1, v1 = extra[row : row + 1], extra[row + 1 : row + 2]
                scaled = d * v1
                high = scaled.astype(BF16).astype(F32)
                low = scaled - high
                lhs = jnp.where(line < 2, k1, jnp.where(line == 2, ks[j : j + 1, at], 0.0))
                rhs = jnp.where(line == 0, high, jnp.where(line == 1, low, vs[j : j + 1, at]))
                outer = lax.dot_general(
                    lhs.astype(BF16), rhs.astype(BF16), (((0,), (0,)), ((), ())), preferred_element_type=F32
                )
                first = j * depth + i * dim
                out[j, :, at] = (d * d) * ins[x][first : first + dim, :].astype(F32) + outer


def fast(n, head_count, states, decay_rates, queries, key_vectors, values, gate_logits, parents, out_weight):
    slots, dim, columns = states.shape
    heads = columns // dim // n
    total, depth = n * slots, heads * dim
    order = [1, 4, 5, 6, 7, 2, 3, 0]
    decay = jnp.broadcast_to(jnp.exp(-decay_rates)[:, None], (columns // dim, dim))

    def exchange(chunks):
        return [
            lax.ppermute(chunk, "beam", [(j, j ^ x) for j in range(n)]) if x else chunk
            for x, chunk in zip(order, chunks)
        ]

    *packed, table = pl.pallas_call(
        functools.partial(pack_kernel, n, order),
        out_shape=[jax.ShapeDtypeStruct((slots, depth + EXTRA, dim), BF16)] * n
        + [jax.ShapeDtypeStruct(parents.shape, jnp.int32)],
        in_specs=[ANY] * 6,
        out_specs=[VMEM] * n + [SMEM],
        scratch_shapes=[
            pltpu.VMEM((slots, dim, columns), F32),
            pltpu.VMEM((ARRAYS, *queries.shape), BF16),
            pltpu.VMEM((slots, ARRAYS * STEPS, columns), F32),
            pltpu.SemaphoreType.DMA((n,)),
            pltpu.SemaphoreType.DMA((ARRAYS + 1,)),
        ],
    )(states, queries, key_vectors, values, gate_logits, parents)
    lines = slots * (depth + KEPT) + heads * STEPS * total
    picked = pl.pallas_call(
        functools.partial(middle_kernel, n, order),
        out_shape=[jax.ShapeDtypeStruct((lines, dim), BF16)] * n,
        in_specs=[SMEM] + [VMEM] * (n + 1),
        out_specs=[VMEM] * n,
        scratch_shapes=[
            pltpu.VMEM((total, depth, dim), BF16),
            pltpu.VMEM((total * EXTRA, dim), F32),
            pltpu.VMEM((slots * KEPT, dim), F32),
        ],
        compiler_params=params(),
    )(table, decay, *exchange(packed))
    forked = exchange(picked)
    piece = jax.ShapeDtypeStruct((STEPS, total // head_count, out_weight.shape[1]), F32)
    keep, send = pl.pallas_call(
        functools.partial(project_kernel, n, order, head_count, slots),
        out_shape=[piece, piece],
        in_specs=[VMEM] * (n + 1),
        out_specs=[VMEM] * 2,
        scratch_shapes=[pltpu.VMEM((STEPS * total, out_weight.shape[1]), F32)],
        compiler_params=params(),
    )(out_weight, *forked)
    other = lax.ppermute(send, "head", [(0, 1), (1, 0)])
    projected = (keep + other).astype(BF16)
    final = pl.pallas_call(
        functools.partial(final_kernel, n, order),
        out_shape=jax.ShapeDtypeStruct(states.shape, F32),
        in_specs=[VMEM] + [VMEM] * (n + 2),
        out_specs=VMEM,
        scratch_shapes=[pltpu.VMEM((slots, columns), F32)] * 2,
        compiler_params=params(),
        cost_estimate=cost(1 << 31, 1 << 20),
    )(decay, key_vectors, values, *forked)
    return projected, final


def fork(state, parent_list):
    row_state = lax.all_to_all(state, "beam", split_axis=1, concat_axis=0, tiled=True)
    picked = jnp.take(row_state, parent_list, axis=0)
    return lax.all_to_all(picked, "beam", split_axis=0, concat_axis=1, tiled=True)


def general(states, decay_rates, queries, key_vectors, values, gate_logits, parents, out_weight):
    slot_count, head_dim, columns = states.shape
    groups = columns // head_dim
    decay = jnp.exp(-decay_rates)
    current = states
    readouts = []
    for step in range(parents.shape[0]):
        forked = fork(current, parents[step])
        query_f = queries[step].astype(F32).reshape(slot_count, groups, head_dim)
        key_f = key_vectors[step].astype(F32).reshape(slot_count, groups, head_dim)
        value_f = values[step].astype(F32).reshape(slot_count, groups, head_dim)
        grid = forked.reshape(slot_count, head_dim, groups, head_dim)
        updated = decay[None, None, :, None] * grid + jnp.einsum("shi,shj->sihj", key_f, value_f)
        readout = jnp.einsum("shi,sihj->shj", query_f, updated, precision=lax.Precision.HIGHEST)
        current = updated.reshape(slot_count, head_dim, columns)
        readouts.append(readout.reshape(slot_count, columns))
    stacked = jnp.stack(readouts)
    attn = (jax.nn.sigmoid(gate_logits.astype(F32)) * stacked).astype(BF16)
    terms = jnp.einsum(
        "tsc,cd->tsd",
        lax.all_gather(attn, "beam", axis=1, tiled=True),
        out_weight,
        preferred_element_type=F32,
    )
    projected = lax.psum_scatter(terms, "head", scatter_dimension=1, tiled=True).astype(BF16)
    return (projected, current)


def solution(mesh):
    n, head_count = mesh.shape["beam"], mesh.shape["head"]

    def shards(*args):
        columns, dim = args[0].shape[2], args[0].shape[1]
        if n & (n - 1) == 0 and columns // dim == 2 * n and head_count == 2:
            return fast(n, head_count, *args)
        return general(*args)

    in_specs = (
        P(("parts", "beam"), None, "head"),
        P("head"),
        P(None, ("parts", "beam"), "head"),
        P(None, ("parts", "beam"), "head"),
        P(None, ("parts", "beam"), "head"),
        P(None, ("parts", "beam"), "head"),
        P(None, "parts"),
        P("head", "beam"),
    )
    out_specs = (P(None, ("parts", "head"), "beam"), P(("parts", "beam"), None, "head"))
    return jax.shard_map(shards, mesh=mesh, in_specs=in_specs, out_specs=out_specs, check_vma=False)
```

time: 79.3 us -> 69.1 us (0.87); the launches traced: 78.1 us -> 68.8 us
  starting transfers between devices: 35.1 us -> 22.5 us
  waiting for transfers between devices: 27.4 us -> 36.2 us
  local copies, waits for them, and re-layouts: 5.14 us -> 1.67 us
  Pallas kernels: 8.49 us -> 6.51 us
    ppermute x17 -> x14, starting transfers between devices: 35 us -> 22.4 us  [exchange(): lax.ppermute(chunk, 'beam', [(j, j ^ x) for j in range(n)])]
    ppermute x17 -> x14, waiting for transfers between devices: 27.4 us -> 36.2 us  [exchange(): lax.ppermute(chunk, 'beam', [(j, j ^ x) for j in range(n)])]
    unnamed x18 -> x10, local copies, waits for them, and re-layouts: 5.14 us -> 1.6 us
    pallas_call x5 -> x4, Pallas kernels: 8.49 us -> 6.51 us  [the longest x1 2.87 us: fast(): pl.pallas_call(functools.partial(pack_kernel, n, order), out_shape=[jax.S...]
  transfers between devices with their start and end apart: 18 -> 15, of which waited for: 6 -> 8; matrix products, arithmetic and copies ran while one was open for 1% -> 1% of each run, Pallas kernels for 9% -> 3%
where the time goes in v2:
time: 69.1 us; the launch traced here: 68.8 us
  waiting for transfers between devices  36.2 us (52%)
  starting transfers between devices  22.5 us (33%)
  Pallas kernels  6.51 us (9%)
  local copies, waits for them, and re-layouts  1.67 us (2%)
  other arithmetic  1.27 us (2%)
  between operations  0.7 us (1%)
    ppermute x14, waiting for transfers between devices, exchange(): lax.ppermute(chunk, 'beam', [(j, j ^ x) for j in range(n)])  36.2 us
    ppermute x14, starting transfers between devices, exchange(): lax.ppermute(chunk, 'beam', [(j, j ^ x) for j in range(n)])  22.4 us
    pallas_call x1, Pallas kernels, fast(): pl.pallas_call(functools.partial(pack_kernel, n, order), out_shape=[jax.S...  2.87 us
    pallas_call x1, Pallas kernels, fast(): pl.pallas_call(functools.partial(final_kernel, n, order), out_shape=jax.S...  1.85 us
    unnamed x10, local copies, waits for them, and re-layouts  1.6 us
  transfers between devices with their start and end apart: 15, of which 8 were waited for; matrix products, arithmetic and copies ran while one was open for 1% of the time, Pallas kernels for 3%

profile of v2, /device:TPU:0, one launch (start us, length us, event | category | flops | bytes accessed | tf_op | source)
XLA Modules:
  0.0 68.8 jit_solution(16108026266722181111)
XLA Ops:
  0.6 0.0 copy-start
  0.6 2.9 %shard_map.95 = (bf16[2,272,128]{2,1,0:T(8,128)(2,1)}, bf16[2,272,128]{2,1,0:T(8,128)(2,1)}, bf16[2,272,128]{2,1,0:T(8,128)(2,1)}, bf16[2,272,128]{2,1,0:T(8,128...) custom-call(f32[2,128,2048]{2,1,0:T(8,128)} %st_hbm.1, ...), custom_call_target="tpu_custom_call" | custom-call | tf_op jit(solution)/shard_map/pallas_call | solution.py:193
  3.5 3.0 %collective-permute-start = (bf16[2,272,128]{2,1,0:T(8,128)(2,1)}, bf16[2,272,128]{2,1,0:T(8,128)(2,1)S(1)}, u32[]{:S(2)}, u32[]{:S(2)}) collective-permute-start(bf16[2,272,128]{2,1,0:T(8,128)(2,1)} %get-tuple-element.22), channel_id=1, source_target_pairs={{0,2},{2,0},{4,6},{6,4},{8,10},{10,8},{12,14},{14,12},{1,3},{3,1},... | collective-permute-start | bytes 417800 | tf_op jit(solution)/shard_map/ppermute | solution.py:189
  6.5 2.6 %collective-permute-start.1 = (bf16[2,272,128]{2,1,0:T(8,128)(2,1)}, bf16[2,272,128]{2,1,0:T(8,128)(2,1)S(1)}, u32[]{:S(2)}, u32[]{:S(2)}) collective-permute-start(bf16[2,272,128]{2,1,0:T(8,128)(2,1)} %get-tuple-element.23), channel_id=1, source_target_pairs={{0,8},{2,10},{4,12},{6,14},{8,0},{10,2},{12,4},{14,6},{1,9},{3,11}... | collective-permute-start | bytes 417800 | tf_op jit(solution)/shard_map/ppermute | solution.py:189
  9.1 0.0 collective-permute-start.2
  9.1 3.9 %collective-permute-start.3 = (bf16[2,272,128]{2,1,0:T(8,128)(2,1)}, bf16[2,272,128]{2,1,0:T(8,128)(2,1)S(1)}, u32[]{:S(2)}, u32[]{:S(2)}) collective-permute-start(bf16[2,272,128]{2,1,0:T(8,128)(2,1)} %get-tuple-element.25), channel_id=1, source_target_pairs={{0,12},{2,14},{4,8},{6,10},{8,4},{10,6},{12,0},{14,2},{1,13},{3,15... | collective-permute-start | bytes 417800 | tf_op jit(solution)/shard_map/ppermute | solution.py:189
  13.0 1.1 %collective-permute-start.4 = (bf16[2,272,128]{2,1,0:T(8,128)(2,1)}, bf16[2,272,128]{2,1,0:T(8,128)(2,1)S(1)}, u32[]{:S(2)}, u32[]{:S(2)}) collective-permute-start(bf16[2,272,128]{2,1,0:T(8,128)(2,1)} %get-tuple-element.26), channel_id=1, source_target_pairs={{0,14},{2,12},{4,10},{6,8},{8,6},{10,4},{12,2},{14,0},{1,15},{3,13... | collective-permute-start | bytes 417800 | tf_op jit(solution)/shard_map/ppermute | solution.py:189
  14.2 0.0 collective-permute-done.rest_0_
  14.2 0.0 collective-permute-start.5
  14.2 11.8 %collective-permute-done.1.rest_1_ = bf16[2,272,128]{2,1,0:T(8,128)(2,1)S(1)} collective-permute-done((bf16[2,272,128]{2,1,0:T(8,128)(2,1)}, bf16[2,272,128]{2,1,0:T(8,128)(2,1)S(1)}, u32[]{:S(2)}, u32[]{:S(2)}) %collective-permute-start.1) | collective-permute-done | bytes 139296 | tf_op jit(solution)/shard_map/ppermute | solution.py:189
  26.0 0.0 collective-permute-start.6
  26.0 0.7 negate_exponential_fusion
  26.6 2.1 %collective-permute-done.2.rest_2_ = bf16[2,272,128]{2,1,0:T(8,128)(2,1)S(1)} collective-permute-done((bf16[2,272,128]{2,1,0:T(8,128)(2,1)}, bf16[2,272,128]{2,1,0:T(8,128)(2,1)S(1)}, u32[]{:S(2)}, u32[]{:S(2)}) %collective-permute-start.2) | collective-permute-done | bytes 139296 | tf_op jit(solution)/shard_map/ppermute | solution.py:189
  28.7 0.0 collective-permute-done.3.rest_3_
  28.7 0.0 collective-permute-done.4.rest_4_
  28.8 2.0 %collective-permute-done.5.rest_5_ = bf16[2,272,128]{2,1,0:T(8,128)(2,1)S(1)} collective-permute-done((bf16[2,272,128]{2,1,0:T(8,128)(2,1)}, bf16[2,272,128]{2,1,0:T(8,128)(2,1)S(1)}, u32[]{:S(2)}, u32[]{:S(2)}) %collective-permute-start.5) | collective-permute-done | bytes 139296 | tf_op jit(solution)/shard_map/ppermute | solution.py:189
  30.8 1.4 %collective-permute-done.6.rest_6_ = bf16[2,272,128]{2,1,0:T(8,128)(2,1)S(1)} collective-permute-done((bf16[2,272,128]{2,1,0:T(8,128)(2,1)}, bf16[2,272,128]{2,1,0:T(8,128)(2,1)S(1)}, u32[]{:S(2)}, u32[]{:S(2)}) %collective-permute-start.6) | collective-permute-done | bytes 139296 | tf_op jit(solution)/shard_map/ppermute | solution.py:189
  32.1 0.1 broadcast_in_dim.2.decay
  32.2 0.0 copy-start.1
  32.2 0.9 %copy-done.1 = bf16[2,272,128]{2,1,0:T(8,128)(2,1)S(1)} copy-done((bf16[2,272,128]{2,1,0:T(8,128)(2,1)S(1)}, bf16[2,272,128]{2,1,0:T(8,128)(2,1)}, u32[]{:S(2)}) %copy-start.1) | copy-done | bytes 139288
  33.1 0.0 copy-start.4
  33.1 0.7 copy-done.4
  33.8 1.1 %shard_map.96 = (bf16[592,128]{1,0:T(8,128)(2,1)S(1)}, bf16[592,128]{1,0:T(8,128)(2,1)S(1)}, bf16[592,128]{1,0:T(8,128)(2,1)S(1)}, bf16[592,128]{1,0:T(8,128)(2,...) custom-call(s32[2,16]{1,0:T(2,128)S(1)} %copy-done.4, ...), custom_call_target="tpu_custom_call" | custom-call | tf_op jit(solution)/shard_map/pallas_call | solution.py:208
  34.9 1.6 %collective-permute-start.7 = (bf16[592,128]{1,0:T(8,128)(2,1)S(1)}, bf16[592,128]{1,0:T(8,128)(2,1)S(1)}, u32[]{:S(2)}, u32[]{:S(2)}) collective-permute-start(bf16[592,128]{1,0:T(8,128)(2,1)S(1)} %get-tuple-element.30), channel_id=1, source_target_pairs={{0,2},{2,0},{4,6},{6,4},{8,10},{10,8},{12,14},{14,12},{1,3},{3,1},... | collective-permute-start | bytes 454664 | tf_op jit(solution)/shard_map/ppermute | solution.py:189
  36.6 4.0 %collective-permute-start.8 = (bf16[592,128]{1,0:T(8,128)(2,1)S(1)}, bf16[592,128]{1,0:T(8,128)(2,1)S(1)}, u32[]{:S(2)}, u32[]{:S(2)}) collective-permute-start(bf16[592,128]{1,0:T(8,128)(2,1)S(1)} %get-tuple-element.31), channel_id=1, source_target_pairs={{0,8},{2,10},{4,12},{6,14},{8,0},{10,2},{12,4},{14,6},{1,9},{3,11}... | collective-permute-start | bytes 454664 | tf_op jit(solution)/shard_map/ppermute | solution.py:189
  40.6 0.0 collective-permute-start.9
  40.6 2.8 %collective-permute-start.10 = (bf16[592,128]{1,0:T(8,128)(2,1)S(1)}, bf16[592,128]{1,0:T(8,128)(2,1)S(1)}, u32[]{:S(2)}, u32[]{:S(2)}) collective-permute-start(bf16[592,128]{1,0:T(8,128)(2,1)S(1)} %get-tuple-element.33), channel_id=1, source_target_pairs={{0,12},{2,14},{4,8},{6,10},{8,4},{10,6},{12,0},{14,2},{1,13},{3,15... | collective-permute-start | bytes 454664 | tf_op jit(solution)/shard_map/ppermute | solution.py:189
  43.4 1.9 %collective-permute-start.11 = (bf16[592,128]{1,0:T(8,128)(2,1)S(1)}, bf16[592,128]{1,0:T(8,128)(2,1)S(1)}, u32[]{:S(2)}, u32[]{:S(2)}) collective-permute-start(bf16[592,128]{1,0:T(8,128)(2,1)S(1)} %get-tuple-element.34), channel_id=1, source_target_pairs={{0,14},{2,12},{4,10},{6,8},{8,6},{10,4},{12,2},{14,0},{1,15},{3,13... | collective-permute-start | bytes 454664 | tf_op jit(solution)/shard_map/ppermute | solution.py:189
  45.3 0.0 collective-permute-done.7.rest_0_
  45.3 0.0 collective-permute-start.12
  45.3 11.6 %collective-permute-done.8.rest_1_ = bf16[592,128]{1,0:T(8,128)(2,1)S(1)} collective-permute-done((bf16[592,128]{1,0:T(8,128)(2,1)S(1)}, bf16[592,128]{1,0:T(8,128)(2,1)S(1)}, u32[]{:S(2)}, u32[]{:S(2)}) %collective-permute-start.8) | collective-permute-done | bytes 151584 | tf_op jit(solution)/shard_map/ppermute | solution.py:189
  56.9 1.4 %collective-permute-start.13 = (bf16[592,128]{1,0:T(8,128)(2,1)S(1)}, bf16[592,128]{1,0:T(8,128)(2,1)S(1)}, u32[]{:S(2)}, u32[]{:S(2)}) collective-permute-start(bf16[592,128]{1,0:T(8,128)(2,1)S(1)} %get-tuple-element.36), channel_id=1, source_target_pairs={{0,6},{2,4},{4,2},{6,0},{8,14},{10,12},{12,10},{14,8},{1,7},{3,5},... | collective-permute-start | bytes 454664 | tf_op jit(solution)/shard_map/ppermute | solution.py:189
  58.3 2.7 %collective-permute-done.9.rest_2_ = bf16[592,128]{1,0:T(8,128)(2,1)S(1)} collective-permute-done((bf16[592,128]{1,0:T(8,128)(2,1)S(1)}, bf16[592,128]{1,0:T(8,128)(2,1)S(1)}, u32[]{:S(2)}, u32[]{:S(2)}) %collective-permute-start.9) | collective-permute-done | bytes 151584 | tf_op jit(solution)/shard_map/ppermute | solution.py:189
  61.0 0.0 collective-permute-done.10.rest_3_
  61.1 0.0 collective-permute-done.11.rest_4_
  61.1 2.2 %collective-permute-done.12.rest_5_ = bf16[592,128]{1,0:T(8,128)(2,1)S(1)} collective-permute-done((bf16[592,128]{1,0:T(8,128)(2,1)S(1)}, bf16[592,128]{1,0:T(8,128)(2,1)S(1)}, u32[]{:S(2)}, u32[]{:S(2)}) %collective-permute-start.12) | collective-permute-done | bytes 151584 | tf_op jit(solution)/shard_map/ppermute | solution.py:189
  63.3 2.3 %collective-permute-done.13.rest_6_ = bf16[592,128]{1,0:T(8,128)(2,1)S(1)} collective-permute-done((bf16[592,128]{1,0:T(8,128)(2,1)S(1)}, bf16[592,128]{1,0:T(8,128)(2,1)S(1)}, u32[]{:S(2)}, u32[]{:S(2)}) %collective-permute-start.13) | collective-permute-done | bytes 151584 | tf_op jit(solution)/shard_map/ppermute | solution.py:189
  65.6 0.0 copy-done
  65.6 0.0 copy-start.2
  65.6 0.0 copy-start.3
  65.6 0.7 shard_map.97
  66.3 0.1 collective-permute-start.14
  66.3 0.0 copy-done.2
  66.3 0.0 copy-done.3
  66.4 1.9 %shard_map.98 = f32[2,128,2048]{2,1,0:T(8,128)} custom-call(f32[16,128]{1,0:T(8,128)S(1)} %broadcast_in_dim.2.decay, bf16[2,2,2048]{2,1,0:T(2,128)(2,1)S(1)} %copy-done.2, bf16[2,2,2048]{2,1,0:T(2,128)(2,1)S(1)} %copy-done.3, bf16[592,128]{1,0:T(8,128)(2,1)S(1)} %collective-permute-done.7.rest_0_, bf16[592,128]{1,0:T(8,128)(2,1)S(1)} %collective-permute-done.8.rest_1_, ...), custom_call_target="tpu_custom_call" | custom-call | flops 2147483648 | bytes 1048576 | tf_op jit(solution)/shard_map/pallas_call | solution.py:232
  68.2 0.0 collective-permute-done.14
  68.2 0.6 add_convert_fusion
Async XLA Ops:
  0.6 65.0 %copy-start = (bf16[2048,768]{1,0:T(8,128)(2,1)S(1)}, bf16[2048,768]{1,0:T(8,128)(2,1)}, u32[]{:S(2)}) copy-start(bf16[2048,768]{1,0:T(8,128)(2,1)} %weight.1) | copy-start | bytes 9437188
  3.5 10.7 %collective-permute-start = (bf16[2,272,128]{2,1,0:T(8,128)(2,1)}, bf16[2,272,128]{2,1,0:T(8,128)(2,1)S(1)}, u32[]{:S(2)}, u32[]{:S(2)}) collective-permute-start(bf16[2,272,128]{2,1,0:T(8,128)(2,1)} %get-tuple-element.22), channel_id=1, source_target_pairs={{0,2},{2,0},{4,6},{6,4},{8,10},{10,8},{12,14},{14,12},{1,3},{3,1},... | collective-permute-start | bytes 417800 | tf_op jit(solution)/shard_map/ppermute | solution.py:189
  6.5 19.4 %collective-permute-start.1 = (bf16[2,272,128]{2,1,0:T(8,128)(2,1)}, bf16[2,272,128]{2,1,0:T(8,128)(2,1)S(1)}, u32[]{:S(2)}, u32[]{:S(2)}) collective-permute-start(bf16[2,272,128]{2,1,0:T(8,128)(2,1)} %get-tuple-element.23), channel_id=1, source_target_pairs={{0,8},{2,10},{4,12},{6,14},{8,0},{10,2},{12,4},{14,6},{1,9},{3,11}... | collective-permute-start | bytes 417800 | tf_op jit(solution)/shard_map/ppermute | solution.py:189
  9.1 19.6 %collective-permute-start.2 = (bf16[2,272,128]{2,1,0:T(8,128)(2,1)}, bf16[2,272,128]{2,1,0:T(8,128)(2,1)S(1)}, u32[]{:S(2)}, u32[]{:S(2)}) collective-permute-start(bf16[2,272,128]{2,1,0:T(8,128)(2,1)} %get-tuple-element.24), channel_id=1, source_target_pairs={{0,10},{2,8},{4,14},{6,12},{8,2},{10,0},{12,6},{14,4},{1,11},{3,9}... | collective-permute-start | bytes 417800 | tf_op jit(solution)/shard_map/ppermute | solution.py:189
  9.1 19.6 %collective-permute-start.3 = (bf16[2,272,128]{2,1,0:T(8,128)(2,1)}, bf16[2,272,128]{2,1,0:T(8,128)(2,1)S(1)}, u32[]{:S(2)}, u32[]{:S(2)}) collective-permute-start(bf16[2,272,128]{2,1,0:T(8,128)(2,1)} %get-tuple-element.25), channel_id=1, source_target_pairs={{0,12},{2,14},{4,8},{6,10},{8,4},{10,6},{12,0},{14,2},{1,13},{3,15... | collective-permute-start | bytes 417800 | tf_op jit(solution)/shard_map/ppermute | solution.py:189
  13.0 15.7 %collective-permute-start.4 = (bf16[2,272,128]{2,1,0:T(8,128)(2,1)}, bf16[2,272,128]{2,1,0:T(8,128)(2,1)S(1)}, u32[]{:S(2)}, u32[]{:S(2)}) collective-permute-start(bf16[2,272,128]{2,1,0:T(8,128)(2,1)} %get-tuple-element.26), channel_id=1, source_target_pairs={{0,14},{2,12},{4,10},{6,8},{8,6},{10,4},{12,2},{14,0},{1,15},{3,13... | collective-permute-start | bytes 417800 | tf_op jit(solution)/shard_map/ppermute | solution.py:189
  14.2 16.6 %collective-permute-start.5 = (bf16[2,272,128]{2,1,0:T(8,128)(2,1)}, bf16[2,272,128]{2,1,0:T(8,128)(2,1)S(1)}, u32[]{:S(2)}, u32[]{:S(2)}) collective-permute-start(bf16[2,272,128]{2,1,0:T(8,128)(2,1)} %get-tuple-element.27), channel_id=1, source_target_pairs={{0,4},{2,6},{4,0},{6,2},{8,12},{10,14},{12,8},{14,10},{1,5},{3,7},... | collective-permute-start | bytes 417800 | tf_op jit(solution)/shard_map/ppermute | solution.py:189
  26.0 6.2 %collective-permute-start.6 = (bf16[2,272,128]{2,1,0:T(8,128)(2,1)}, bf16[2,272,128]{2,1,0:T(8,128)(2,1)S(1)}, u32[]{:S(2)}, u32[]{:S(2)}) collective-permute-start(bf16[2,272,128]{2,1,0:T(8,128)(2,1)} %get-tuple-element.28), channel_id=1, source_target_pairs={{0,6},{2,4},{4,2},{6,0},{8,14},{10,12},{12,10},{14,8},{1,7},{3,5},... | collective-permute-start | bytes 417800 | tf_op jit(solution)/shard_map/ppermute | solution.py:189
  32.2 0.9 %copy-start.1 = (bf16[2,272,128]{2,1,0:T(8,128)(2,1)S(1)}, bf16[2,272,128]{2,1,0:T(8,128)(2,1)}, u32[]{:S(2)}) copy-start(bf16[2,272,128]{2,1,0:T(8,128)(2,1)} %get-tuple-element.29.rest_7_) | copy-start | bytes 417796
  33.1 0.7 copy-start.4
  34.9 10.4 %collective-permute-start.7 = (bf16[592,128]{1,0:T(8,128)(2,1)S(1)}, bf16[592,128]{1,0:T(8,128)(2,1)S(1)}, u32[]{:S(2)}, u32[]{:S(2)}) collective-permute-start(bf16[592,128]{1,0:T(8,128)(2,1)S(1)} %get-tuple-element.30), channel_id=1, source_target_pairs={{0,2},{2,0},{4,6},{6,4},{8,10},{10,8},{12,14},{14,12},{1,3},{3,1},... | collective-permute-start | bytes 454664 | tf_op jit(solution)/shard_map/ppermute | solution.py:189
  36.6 20.4 %collective-permute-start.8 = (bf16[592,128]{1,0:T(8,128)(2,1)S(1)}, bf16[592,128]{1,0:T(8,128)(2,1)S(1)}, u32[]{:S(2)}, u32[]{:S(2)}) collective-permute-start(bf16[592,128]{1,0:T(8,128)(2,1)S(1)} %get-tuple-element.31), channel_id=1, source_target_pairs={{0,8},{2,10},{4,12},{6,14},{8,0},{10,2},{12,4},{14,6},{1,9},{3,11}... | collective-permute-start | bytes 454664 | tf_op jit(solution)/shard_map/ppermute | solution.py:189
  40.6 20.5 %collective-permute-start.9 = (bf16[592,128]{1,0:T(8,128)(2,1)S(1)}, bf16[592,128]{1,0:T(8,128)(2,1)S(1)}, u32[]{:S(2)}, u32[]{:S(2)}) collective-permute-start(bf16[592,128]{1,0:T(8,128)(2,1)S(1)} %get-tuple-element.32), channel_id=1, source_target_pairs={{0,10},{2,8},{4,14},{6,12},{8,2},{10,0},{12,6},{14,4},{1,11},{3,9}... | collective-permute-start | bytes 454664 | tf_op jit(solution)/shard_map/ppermute | solution.py:189
  40.6 20.5 %collective-permute-start.10 = (bf16[592,128]{1,0:T(8,128)(2,1)S(1)}, bf16[592,128]{1,0:T(8,128)(2,1)S(1)}, u32[]{:S(2)}, u32[]{:S(2)}) collective-permute-start(bf16[592,128]{1,0:T(8,128)(2,1)S(1)} %get-tuple-element.33), channel_id=1, source_target_pairs={{0,12},{2,14},{4,8},{6,10},{8,4},{10,6},{12,0},{14,2},{1,13},{3,15... | collective-permute-start | bytes 454664 | tf_op jit(solution)/shard_map/ppermute | solution.py:189
  43.4 17.6 %collective-permute-start.11 = (bf16[592,128]{1,0:T(8,128)(2,1)S(1)}, bf16[592,128]{1,0:T(8,128)(2,1)S(1)}, u32[]{:S(2)}, u32[]{:S(2)}) collective-permute-start(bf16[592,128]{1,0:T(8,128)(2,1)S(1)} %get-tuple-element.34), channel_id=1, source_target_pairs={{0,14},{2,12},{4,10},{6,8},{8,6},{10,4},{12,2},{14,0},{1,15},{3,13... | collective-permute-start | bytes 454664 | tf_op jit(solution)/shard_map/ppermute | solution.py:189
  45.3 17.9 %collective-permute-start.12 = (bf16[592,128]{1,0:T(8,128)(2,1)S(1)}, bf16[592,128]{1,0:T(8,128)(2,1)S(1)}, u32[]{:S(2)}, u32[]{:S(2)}) collective-permute-start(bf16[592,128]{1,0:T(8,128)(2,1)S(1)} %get-tuple-element.35), channel_id=1, source_target_pairs={{0,4},{2,6},{4,0},{6,2},{8,12},{10,14},{12,8},{14,10},{1,5},{3,7},... | collective-permute-start | bytes 454664 | tf_op jit(solution)/shard_map/ppermute | solution.py:189
  56.9 8.6 %collective-permute-start.13 = (bf16[592,128]{1,0:T(8,128)(2,1)S(1)}, bf16[592,128]{1,0:T(8,128)(2,1)S(1)}, u32[]{:S(2)}, u32[]{:S(2)}) collective-permute-start(bf16[592,128]{1,0:T(8,128)(2,1)S(1)} %get-tuple-element.36), channel_id=1, source_target_pairs={{0,6},{2,4},{4,2},{6,0},{8,14},{10,12},{12,10},{14,8},{1,7},{3,5},... | collective-permute-start | bytes 454664 | tf_op jit(solution)/shard_map/ppermute | solution.py:189
  65.6 0.8 %copy-start.2 = (bf16[2,2,2048]{2,1,0:T(2,128)(2,1)S(1)}, bf16[2,2,2048]{2,1,0:T(2,128)(2,1)}, u32[]{:S(2)}) copy-start(bf16[2,2,2048]{2,1,0:T(2,128)(2,1)} %k.3) | copy-start | bytes 49156
  65.6 0.8 %copy-start.3 = (bf16[2,2,2048]{2,1,0:T(2,128)(2,1)S(1)}, bf16[2,2,2048]{2,1,0:T(2,128)(2,1)}, u32[]{:S(2)}) copy-start(bf16[2,2,2048]{2,1,0:T(2,128)(2,1)} %v.3) | copy-start | bytes 49156
  66.3 2.0 %collective-permute-start.14 = (f32[2,8,768]{2,1,0:T(8,128)S(1)}, f32[2,8,768]{2,1,0:T(8,128)S(1)}, u32[]{:S(2)}, u32[]{:S(2)}) collective-permute-start(f32[2,8,768]{2,1,0:T(8,128)S(1)} %get-tuple-element.39), channel_id=1, source_target_pairs={{0,1},{1,0},{2,3},{3,2},{4,5},{5,4},{6,7},{7,6},{8,9},{9,8},{10,11... | collective-permute-start | bytes 147464 | tf_op jit(solution)/shard_map/ppermute | solution.py:230

commit v3 on v2

--- a/solution.py
+++ b/solution.py
@@ -33,8 +33,8 @@
     return [ref for _, ref in sorted(zip(order, refs), key=lambda pair: pair[0])]
 
 
-def pack_kernel(n, order, st_hbm, q, k, v, g, parents_hbm, *rest):
-    outs, (parents, st, vectors, rows, sem, sem_small) = by_partner(order, rest[:n]), rest[n:]
+def pack_kernel(n, order, st_hbm, q, k, v, g, *rest):
+    outs, (st, vectors, rows, chunk, sem, sem_small, sem_out) = dict(zip(order, rest)), rest[-7:]
     slots, dim, columns = st.shape
     heads = columns // dim // n
     me = lax.axis_index("beam")
@@ -43,7 +43,6 @@
         return pl.ds(pl.multiple_of(head * dim, dim), count * dim)
 
     small = [pltpu.make_async_copy(ref, vectors.at[a], sem_small.at[a]) for a, ref in enumerate((q, k, v, g))]
-    small.append(pltpu.make_async_copy(parents_hbm, parents, sem_small.at[ARRAYS]))
     large = {}
     for x in order:
         at = lanes((me ^ x) * heads, heads)
@@ -63,20 +62,35 @@
             extra = []
             for i in range(heads):
                 at = lanes(first + i, 1)
-                outs[x][j, i * dim : (i + 1) * dim, :] = st[j, :, at].astype(BF16)
+                chunk[x, j, i * dim : (i + 1) * dim, :] = st[j, :, at].astype(BF16)
                 extra.append(rows[j, :, at])
-            outs[x][j, heads * dim :, :] = jnp.concatenate(extra, 0).astype(BF16)
-    small[ARRAYS].wait()
-
-
-def middle_kernel(n, order, parents, decay, *rest):
-    ins, outs, (buf, vectors, kept) = by_partner(order, rest[:n]), by_partner(order, rest[n : 2 * n]), rest[2 * n :]
-    slots, rows, dim = ins[0].shape
+            chunk[x, j, heads * dim :, :] = jnp.concatenate(extra, 0).astype(BF16)
+        large[x] = pltpu.make_async_copy(chunk.at[x], outs[x], sem_out.at[x])
+        large[x].start()
+    for x in order:
+        large[x].wait()
+
+
+def hold_kernel(chunk, out):
+    out[...] = chunk[...]
+
+
+def middle_kernel(n, first, second, parents_hbm, decay, *rest):
+    ins, outs = by_partner(first, rest[:n]), by_partner(second, rest[n : 2 * n])
+    buf, vectors, kept, parents, own, sem = rest[2 * n :]
+    copies = [pltpu.make_async_copy(parents_hbm, parents, sem.at[0]), pltpu.make_async_copy(ins[0], own, sem.at[1])]
+    for c in copies:
+        c.start()
+    ins[0] = own
+    slots, rows, dim = own.shape
     depth = rows - EXTRA
     heads = depth // dim
     total = n * slots
     me = lax.axis_index("beam")
-    for x in range(n):
+    for x in [*range(1, n), 0]:
+        if x == 0:
+            for c in copies:
+                c.wait()
         for j in range(slots):
             slot = (me ^ x) * slots + j
             buf[slot] = ins[x][j, :depth, :]
@@ -89,7 +103,7 @@
             for i in range(heads):
                 for place, array in enumerate((K, V)):
                     to = j * KEPT + i * 2 + place
-                    kept[to : to + 1, :] = vectors[pl.ds(middle * EXTRA + row_of(i, array, 0), 1), :]
+                    kept[to : to + 1, :] = vectors[pl.ds(parents[STEPS + 1, (me ^ x) * slots + j] + row_of(i, array, 0), 1), :]
         outs[x][slots * depth : slots * (depth + KEPT), :] = kept[...].astype(BF16)
     line = lax.broadcasted_iota(jnp.int32, (STEPS * total, dim), 0)
     mid_line = lax.broadcasted_iota(jnp.int32, (total, total), 0)
@@ -127,7 +141,7 @@
 
 
 def project_kernel(n, order, head_count, slots, weight, *rest):
-    ins, (keep, send, terms) = by_partner(order, rest[:n]), rest[n:]
+    ins, (keep, send, terms) = by_partner(order, rest[:n]), rest[n + 1 :]
     me, head = lax.axis_index("beam"), lax.axis_index("head")
     lines, dim = terms.shape[0], ins[0].shape[1]
     heads = weight.shape[0] // dim // n
@@ -147,16 +161,19 @@
         send[t] = terms[pl.ds(other, part), :]
 
 
-def final_kernel(n, order, decay, k, v, *rest):
-    ins, (out, ks, vs) = by_partner(order, rest[:n]), rest[n:]
-    slots, dim, columns = out.shape
+def final_kernel(n, order, first, decay, k, v, *rest):
+    ins, (result, *token, out, ks, vs, sem) = dict(zip(order, rest)), rest[-5 - first :]
+    if first:
+        token[0][...] = jnp.zeros_like(token[0])
+    slots, dim, columns = result.shape
     heads = columns // dim // n
     depth = heads * dim
     me = lax.axis_index("beam")
     ks[...] = k[1].astype(F32)
     vs[...] = v[1].astype(F32)
     line = lax.broadcasted_iota(jnp.int32, (16, dim), 0)
-    for x in range(n):
+    copies = []
+    for x in order:
         extra = ins[x][slots * depth : slots * (depth + KEPT), :].astype(F32)
         for j in range(slots):
             for i in range(heads):
@@ -175,69 +192,101 @@
                 )
                 first = j * depth + i * dim
                 out[j, :, at] = (d * d) * ins[x][first : first + dim, :].astype(F32) + outer
+        at = pl.ds(pl.multiple_of((me ^ x) * depth, depth), depth)
+        copies.append(pltpu.make_async_copy(out.at[:, :, at], result.at[:, :, at], sem.at[x]))
+        copies[-1].start()
+    for c in copies:
+        c.wait()
 
 
 def fast(n, head_count, states, decay_rates, queries, key_vectors, values, gate_logits, parents, out_weight):
     slots, dim, columns = states.shape
     heads = columns // dim // n
     total, depth = n * slots, heads * dim
-    order = [1, 4, 5, 6, 7, 2, 3, 0]
+    first, second = [4, 1, 2, 5, 3, 6, 7, 0], [4, 1, 2, 5, 3, 6, 7, 0]
     decay = jnp.broadcast_to(jnp.exp(-decay_rates)[:, None], (columns // dim, dim))
 
-    def exchange(chunks):
+    def exchange(order, chunks):
         return [
             lax.ppermute(chunk, "beam", [(j, j ^ x) for j in range(n)]) if x else chunk
             for x, chunk in zip(order, chunks)
         ]
 
-    *packed, table = pl.pallas_call(
-        functools.partial(pack_kernel, n, order),
-        out_shape=[jax.ShapeDtypeStruct((slots, depth + EXTRA, dim), BF16)] * n
-        + [jax.ShapeDtypeStruct(parents.shape, jnp.int32)],
-        in_specs=[ANY] * 6,
-        out_specs=[VMEM] * n + [SMEM],
-        scratch_shapes=[
-            pltpu.VMEM((slots, dim, columns), F32),
-            pltpu.VMEM((ARRAYS, *queries.shape), BF16),
-            pltpu.VMEM((slots, ARRAYS * STEPS, columns), F32),
-            pltpu.SemaphoreType.DMA((n,)),
-            pltpu.SemaphoreType.DMA((ARRAYS + 1,)),
-        ],
-    )(states, queries, key_vectors, values, gate_logits, parents)
+    table = jnp.concatenate([parents, parents * EXTRA], 0)
+    packed = []
+    for part in (first[:1], first[1:]):
+        packed += pl.pallas_call(
+            functools.partial(pack_kernel, n, part),
+            out_shape=[jax.ShapeDtypeStruct((slots, depth + EXTRA, dim), BF16)] * len(part),
+            in_specs=[ANY] * 5,
+            out_specs=[ANY] * len(part),
+            scratch_shapes=[
+                pltpu.VMEM((slots, dim, columns), F32),
+                pltpu.VMEM((ARRAYS, *queries.shape), BF16),
+                pltpu.VMEM((slots, ARRAYS * STEPS, columns), F32),
+                pltpu.VMEM((n, slots, depth + EXTRA, dim), BF16),
+                pltpu.SemaphoreType.DMA((n,)),
+                pltpu.SemaphoreType.DMA((ARRAYS,)),
+                pltpu.SemaphoreType.DMA((n,)),
+            ],
+        )(states, queries, key_vectors, values, gate_logits)
+    packed[-1] = pl.pallas_call(
+        hold_kernel,
+        out_shape=jax.ShapeDtypeStruct(packed[-1].shape, BF16),
+        in_specs=[VMEM],
+        out_specs=VMEM,
+        compiler_params=params(),
+    )(packed[-1])
     lines = slots * (depth + KEPT) + heads * STEPS * total
     picked = pl.pallas_call(
-        functools.partial(middle_kernel, n, order),
+        functools.partial(middle_kernel, n, first, second),
         out_shape=[jax.ShapeDtypeStruct((lines, dim), BF16)] * n,
-        in_specs=[SMEM] + [VMEM] * (n + 1),
+        in_specs=[ANY] + [VMEM] * n + [ANY],
         out_specs=[VMEM] * n,
         scratch_shapes=[
             pltpu.VMEM((total, depth, dim), BF16),
             pltpu.VMEM((total * EXTRA, dim), F32),
             pltpu.VMEM((slots * KEPT, dim), F32),
+            pltpu.SMEM(table.shape, jnp.int32),
+            pltpu.VMEM((slots, depth + EXTRA, dim), BF16),
+            pltpu.SemaphoreType.DMA((2,)),
         ],
         compiler_params=params(),
-    )(table, decay, *exchange(packed))
-    forked = exchange(picked)
+    )(table, decay, *exchange(first, packed))
+    forked = exchange(second, picked)
+    held = dict(zip(second, forked))
+
+    whole = jax.ShapeDtypeStruct(states.shape, F32)
+
+    def finish(part, *before):
+        return pl.pallas_call(
+            functools.partial(final_kernel, n, part, not before),
+            out_shape=[whole] if before else [whole, jax.ShapeDtypeStruct((8, dim), F32)],
+            in_specs=[VMEM] * (len(part) + 3) + [ANY] * len(before),
+            out_specs=[ANY] if before else [ANY, VMEM],
+            input_output_aliases={len(part) + 3: 0} if before else {},
+            scratch_shapes=[
+                pltpu.VMEM(states.shape, F32),
+                pltpu.VMEM((slots, columns), F32),
+                pltpu.VMEM((slots, columns), F32),
+                pltpu.SemaphoreType.DMA((n,)),
+            ],
+            compiler_params=params(),
+        )(decay, key_vectors, values, *[held[x] for x in part], *before)
+
+    begun, token = finish(second[:6] + second[-1:])
     piece = jax.ShapeDtypeStruct((STEPS, total // head_count, out_weight.shape[1]), F32)
     keep, send = pl.pallas_call(
-        functools.partial(project_kernel, n, order, head_count, slots),
+        functools.partial(project_kernel, n, second, head_count, slots),
         out_shape=[piece, piece],
-        in_specs=[VMEM] * (n + 1),
+        in_specs=[VMEM] * (n + 1) + [VMEM],
         out_specs=[VMEM] * 2,
         scratch_shapes=[pltpu.VMEM((STEPS * total, out_weight.shape[1]), F32)],
         compiler_params=params(),
-    )(out_weight, *forked)
+    )(out_weight, *forked, token)
     other = lax.ppermute(send, "head", [(0, 1), (1, 0)])
     projected = (keep + other).astype(BF16)
-    final = pl.pallas_call(
-        functools.partial(final_kernel, n, order),
-        out_shape=jax.ShapeDtypeStruct(states.shape, F32),
-        in_specs=[VMEM] + [VMEM] * (n + 2),
-        out_specs=VMEM,
-        scratch_shapes=[pltpu.VMEM((slots, columns), F32)] * 2,
-        compiler_params=params(),
-        cost_estimate=cost(1 << 31, 1 << 20),
-    )(decay, key_vectors, values, *forked)
+    (final,) = finish(second[6:-1], begun)
     return projected, final
 
 

time: 69.1 us -> 64 us (0.926); the launches traced: 68.8 us -> 62.8 us
  waiting for transfers between devices: 36.2 us -> 25.3 us
  starting transfers between devices: 22.5 us -> 26.4 us
  Pallas kernels: 6.51 us -> 8.68 us
    ppermute x14, waiting for transfers between devices: 36.2 us -> 25.1 us  [exchange(): lax.ppermute(chunk, 'beam', [(j, j ^ x) for j in range(n)])]
    ppermute x14, starting transfers between devices: 22.4 us -> 26.4 us  [exchange(): lax.ppermute(chunk, 'beam', [(j, j ^ x) for j in range(n)])]
    pallas_call x4 -> x7, Pallas kernels: 6.51 us -> 8.68 us  [the longest x2 4.34 us: fast(): pl.pallas_call(functools.partial(pack_kernel, n, part), out_shape=[jax.Sh...]
    unnamed x10 -> x12, local copies, waits for them, and re-layouts: 1.6 us -> 0.94 us
  transfers between devices with their start and end apart: 15 -> 15, of which waited for: 8 -> 6; matrix products, arithmetic and copies ran while one was open for 1% -> 0% of each run, Pallas kernels for 3% -> 8%
where the time goes in v3:
time: 64 us; the launch traced here: 62.8 us
  starting transfers between devices  26.4 us (41%)
  waiting for transfers between devices  25.3 us (40%)
  Pallas kernels  8.68 us (14%)
  local copies, waits for them, and re-layouts  1.01 us (2%)
  between operations  0.78 us (1%)
    ppermute x14, starting transfers between devices, exchange(): lax.ppermute(chunk, 'beam', [(j, j ^ x) for j in range(n)])  26.4 us
    ppermute x14, waiting for transfers between devices, exchange(): lax.ppermute(chunk, 'beam', [(j, j ^ x) for j in range(n)])  25.1 us
    pallas_call x2, Pallas kernels, fast(): pl.pallas_call(functools.partial(pack_kernel, n, part), out_shape=[jax.Sh...  4.34 us
    pallas_call x2, Pallas kernels, finish(): pl.pallas_call(functools.partial(final_kernel, n, part, not before), out_...  2.57 us
  transfers between devices with their start and end apart: 15, of which 6 were waited for; matrix products, arithmetic and copies ran while one was open for 0% of the time, Pallas kernels for 8%

profile of v3, /device:TPU:0, one launch (start us, length us, event | category | flops | bytes accessed | tf_op | source)
XLA Modules:
  0.0 62.8 jit_solution(7696238512148229622)
XLA Ops:
  0.6 0.0 copy-start.4
  0.6 0.0 copy-start.5
  0.6 1.9 %shard_map.95 = bf16[2,272,128]{2,1,0:T(8,128)(2,1)} custom-call(f32[2,128,2048]{2,1,0:T(8,128)} %st_hbm.3, bf16[2,2,2048]{2,1,0:T(2,128)(2,1)} %q.3, bf16[2,2,2048]{2,1,0:T(2,128)(2,1)} %k.7, bf16[2,2,2048]{2,1,0:T(2,128)(2,1)} %v.7, bf16[2,2,2048]{2,1,0:T(2,128)(2,1)} %g.3), custom_call_target="tpu_custom_call" | custom-call | tf_op jit(solution)/shard_map/pallas_call | solution.py:218
  2.6 0.0 copy-start.1
  2.6 0.0 copy-start.2
  2.6 0.0 copy-start
  2.6 4.1 %collective-permute-start = (bf16[2,272,128]{2,1,0:T(8,128)(2,1)}, bf16[2,272,128]{2,1,0:T(8,128)(2,1)S(1)}, u32[]{:S(2)}, u32[]{:S(2)}) collective-permute-start(bf16[2,272,128]{2,1,0:T(8,128)(2,1)} %shard_map.95), channel_id=1, source_target_pairs={{0,8},{2,10},{4,12},{6,14},{8,0},{10,2},{12,4},{14,6},{1,9},{3,11}... | collective-permute-start | bytes 417800 | tf_op jit(solution)/shard_map/ppermute | solution.py:211
  6.7 2.4 %shard_map.96 = (bf16[2,272,128]{2,1,0:T(8,128)(2,1)}, bf16[2,272,128]{2,1,0:T(8,128)(2,1)}, bf16[2,272,128]{2,1,0:T(8,128)(2,1)}, bf16[2,272,128]{2,1,0:T(8,128...) custom-call(f32[2,128,2048]{2,1,0:T(8,128)} %st_hbm.3, ...), custom_call_target="tpu_custom_call" | custom-call | tf_op jit(solution)/shard_map/pallas_call | solution.py:218
  9.1 1.6 %collective-permute-start.1 = (bf16[2,272,128]{2,1,0:T(8,128)(2,1)}, bf16[2,272,128]{2,1,0:T(8,128)(2,1)S(1)}, u32[]{:S(2)}, u32[]{:S(2)}) collective-permute-start(bf16[2,272,128]{2,1,0:T(8,128)(2,1)} %get-tuple-element.21), channel_id=1, source_target_pairs={{0,2},{2,0},{4,6},{6,4},{8,10},{10,8},{12,14},{14,12},{1,3},{3,1},... | collective-permute-start | bytes 417800 | tf_op jit(solution)/shard_map/ppermute | solution.py:211
  10.7 1.6 %collective-permute-start.2 = (bf16[2,272,128]{2,1,0:T(8,128)(2,1)}, bf16[2,272,128]{2,1,0:T(8,128)(2,1)S(1)}, u32[]{:S(2)}, u32[]{:S(2)}) collective-permute-start(bf16[2,272,128]{2,1,0:T(8,128)(2,1)} %get-tuple-element.22), channel_id=1, source_target_pairs={{0,4},{2,6},{4,0},{6,2},{8,12},{10,14},{12,8},{14,10},{1,5},{3,7},... | collective-permute-start | bytes 417800 | tf_op jit(solution)/shard_map/ppermute | solution.py:211
  12.3 0.5 collective-permute-start.3
  12.8 1.4 %collective-permute-start.4 = (bf16[2,272,128]{2,1,0:T(8,128)(2,1)}, bf16[2,272,128]{2,1,0:T(8,128)(2,1)S(1)}, u32[]{:S(2)}, u32[]{:S(2)}) collective-permute-start(bf16[2,272,128]{2,1,0:T(8,128)(2,1)} %get-tuple-element.24), channel_id=1, source_target_pairs={{0,6},{2,4},{4,2},{6,0},{8,14},{10,12},{12,10},{14,8},{1,7},{3,5},... | collective-permute-start | bytes 417800 | tf_op jit(solution)/shard_map/ppermute | solution.py:211
  14.2 0.0 copy-done.4
  14.2 0.0 collective-permute-done.rest_0_
  14.2 3.5 %collective-permute-start.5 = (bf16[2,272,128]{2,1,0:T(8,128)(2,1)}, bf16[2,272,128]{2,1,0:T(8,128)(2,1)S(1)}, u32[]{:S(2)}, u32[]{:S(2)}) collective-permute-start(bf16[2,272,128]{2,1,0:T(8,128)(2,1)} %get-tuple-element.25), channel_id=1, source_target_pairs={{0,12},{2,14},{4,8},{6,10},{8,4},{10,6},{12,0},{14,2},{1,13},{3,15... | collective-permute-start | bytes 417800 | tf_op jit(solution)/shard_map/ppermute | solution.py:211
  17.6 0.0 collective-permute-done.1.rest_1_
  17.6 1.3 %collective-permute-start.6 = (bf16[2,272,128]{2,1,0:T(8,128)(2,1)}, bf16[2,272,128]{2,1,0:T(8,128)(2,1)S(1)}, u32[]{:S(2)}, u32[]{:S(2)}) collective-permute-start(bf16[2,272,128]{2,1,0:T(8,128)(2,1)} %get-tuple-element.26), channel_id=1, source_target_pairs={{0,14},{2,12},{4,10},{6,8},{8,6},{10,4},{12,2},{14,0},{1,15},{3,13... | collective-permute-start | bytes 417800 | tf_op jit(solution)/shard_map/ppermute | solution.py:211
  19.0 0.0 copy-done.5
  19.0 0.0 copy-start.3
  19.0 0.9 %copy-done.3 = bf16[2,272,128]{2,1,0:T(8,128)(2,1)S(1)} copy-done((bf16[2,272,128]{2,1,0:T(8,128)(2,1)S(1)}, bf16[2,272,128]{2,1,0:T(8,128)(2,1)}, u32[]{:S(2)}) %copy-start.3) | copy-done | bytes 139288
  19.9 0.0 collective-permute-done.2.rest_2_
  19.9 8.4 %collective-permute-done.3.rest_3_ = bf16[2,272,128]{2,1,0:T(8,128)(2,1)S(1)} collective-permute-done((bf16[2,272,128]{2,1,0:T(8,128)(2,1)}, bf16[2,272,128]{2,1,0:T(8,128)(2,1)S(1)}, u32[]{:S(2)}, u32[]{:S(2)}) %collective-permute-start.3) | collective-permute-done | bytes 139296 | tf_op jit(solution)/shard_map/ppermute | solution.py:211
  28.3 1.1 %collective-permute-done.4.rest_4_ = bf16[2,272,128]{2,1,0:T(8,128)(2,1)S(1)} collective-permute-done((bf16[2,272,128]{2,1,0:T(8,128)(2,1)}, bf16[2,272,128]{2,1,0:T(8,128)(2,1)S(1)}, u32[]{:S(2)}, u32[]{:S(2)}) %collective-permute-start.4) | collective-permute-done | bytes 139296 | tf_op jit(solution)/shard_map/ppermute | solution.py:211
  29.5 0.0 collective-permute-done.5.rest_5_
  29.5 0.0 collective-permute-done.6.rest_6_
  29.5 0.1 broadcast_in_dim.2.decay
  29.5 1.1 %shard_map.98 = (bf16[592,128]{1,0:T(8,128)(2,1)S(1)}, bf16[592,128]{1,0:T(8,128)(2,1)S(1)}, bf16[592,128]{1,0:T(8,128)(2,1)S(1)}, bf16[592,128]{1,0:T(8,128)(2,...) custom-call(s32[4,16]{1,0:T(4,128)S(1)} %pad_add_fusion.parents_hbm,, ...), custom_call_target="tpu_custom_call" | custom-call | tf_op jit(solution)/shard_map/pallas_call | solution.py:241
  30.6 5.7 %collective-permute-start.7 = (bf16[592,128]{1,0:T(8,128)(2,1)S(1)}, bf16[592,128]{1,0:T(8,128)(2,1)S(1)}, u32[]{:S(2)}, u32[]{:S(2)}) collective-permute-start(bf16[592,128]{1,0:T(8,128)(2,1)S(1)} %get-tuple-element.28), channel_id=1, source_target_pairs={{0,8},{2,10},{4,12},{6,14},{8,0},{10,2},{12,4},{14,6},{1,9},{3,11}... | collective-permute-start | bytes 454664 | tf_op jit(solution)/shard_map/ppermute | solution.py:211
  36.3 0.5 collective-permute-start.8
  36.8 0.0 collective-permute-start.9
  36.9 3.0 %collective-permute-start.10 = (bf16[592,128]{1,0:T(8,128)(2,1)S(1)}, bf16[592,128]{1,0:T(8,128)(2,1)S(1)}, u32[]{:S(2)}, u32[]{:S(2)}) collective-permute-start(bf16[592,128]{1,0:T(8,128)(2,1)S(1)} %get-tuple-element.31), channel_id=1, source_target_pairs={{0,10},{2,8},{4,14},{6,12},{8,2},{10,0},{12,6},{14,4},{1,11},{3,9}... | collective-permute-start | bytes 454664 | tf_op jit(solution)/shard_map/ppermute | solution.py:211
  39.9 0.0 collective-permute-start.11
  39.9 5.8 %collective-permute-done.7.rest_0_ = bf16[592,128]{1,0:T(8,128)(2,1)S(1)} collective-permute-done((bf16[592,128]{1,0:T(8,128)(2,1)S(1)}, bf16[592,128]{1,0:T(8,128)(2,1)S(1)}, u32[]{:S(2)}, u32[]{:S(2)}) %collective-permute-start.7) | collective-permute-done | bytes 151584 | tf_op jit(solution)/shard_map/ppermute | solution.py:211
  45.7 0.0 collective-permute-start.12
  45.7 0.0 collective-permute-done.8.rest_1_
  45.7 3.2 %collective-permute-start.13 = (bf16[592,128]{1,0:T(8,128)(2,1)S(1)}, bf16[592,128]{1,0:T(8,128)(2,1)S(1)}, u32[]{:S(2)}, u32[]{:S(2)}) collective-permute-start(bf16[592,128]{1,0:T(8,128)(2,1)S(1)} %get-tuple-element.34), channel_id=1, source_target_pairs={{0,14},{2,12},{4,10},{6,8},{8,6},{10,4},{12,2},{14,0},{1,15},{3,13... | collective-permute-start | bytes 454664 | tf_op jit(solution)/shard_map/ppermute | solution.py:211
  48.9 0.0 collective-permute-done.9.rest_2_
  48.9 2.5 %collective-permute-done.10.rest_3_ = bf16[592,128]{1,0:T(8,128)(2,1)S(1)} collective-permute-done((bf16[592,128]{1,0:T(8,128)(2,1)S(1)}, bf16[592,128]{1,0:T(8,128)(2,1)S(1)}, u32[]{:S(2)}, u32[]{:S(2)}) %collective-permute-start.10) | collective-permute-done | bytes 151584 | tf_op jit(solution)/shard_map/ppermute | solution.py:211
  51.4 7.2 %collective-permute-done.11.rest_4_ = bf16[592,128]{1,0:T(8,128)(2,1)S(1)} collective-permute-done((bf16[592,128]{1,0:T(8,128)(2,1)S(1)}, bf16[592,128]{1,0:T(8,128)(2,1)S(1)}, u32[]{:S(2)}, u32[]{:S(2)}) %collective-permute-start.11) | collective-permute-done | bytes 151584 | tf_op jit(solution)/shard_map/ppermute | solution.py:211
  58.6 0.0 collective-permute-done.12.rest_5_
  58.6 0.0 copy-done.1
  58.6 0.0 copy-done.2
  58.6 1.5 %shard_map.99 = (f32[2,128,2048]{2,1,0:T(8,128)}, f32[8,128]{1,0:T(8,128)S(1)}) custom-call(f32[16,128]{1,0:T(8,128)S(1)} %broadcast_in_dim.2.decay, bf16[2,2,2048]{2,1,0:T(2,128)(2,1)S(1)} %copy-done.1, bf16[2,2,2048]{2,1,0:T(2,128)(2,1)S(1)} %copy-done.2, bf16[592,128]{1,0:T(8,128)(2,1)S(1)} %collective-permute-done.7.rest_0_, ...), custom_call_target="tpu_custom_call" | custom-call | tf_op jit(solution)/shard_map/pallas_call | solution.py:262
  60.2 0.0 collective-permute-done.13.rest_6_.rest_0_
  60.2 0.0 copy-done
  60.2 0.7 %shard_map.100 = (f32[2,8,768]{2,1,0:T(8,128)S(1)}, f32[2,8,768]{2,1,0:T(8,128)S(1)}) custom-call(bf16[2048,768]{1,0:T(8,128)(2,1)S(1)} %copy-done, bf16[592,128]{1,0:T(8,128)(2,1)S(1)} %collective-permute-done.7.rest_0_, bf16[592,128]{1,0:T(8,128)(2,1)S(1)} %collective-permute-done.8.rest_1_, bf16[592,128]{1,0:T(8,128)(2,1)S(1)} %collective-permute-done.9.rest_2_, ...), custom_call_target="tpu_custom_call" | custom-call | tf_op jit(solution)/shard_map/pallas_call | solution.py:279
  60.9 0.1 collective-permute-start.14
  61.0 1.0 %shard_map.101 = f32[2,128,2048]{2,1,0:T(8,128)} custom-call(f32[16,128]{1,0:T(8,128)S(1)} %broadcast_in_dim.2.decay, bf16[2,2,2048]{2,1,0:T(2,128)(2,1)S(1)} %copy-done.1, bf16[2,2,2048]{2,1,0:T(2,128)(2,1)S(1)} %copy-done.2, bf16[592,128]{1,0:T(8,128)(2,1)S(1)} %collective-permute-done.13.rest_6_.rest_0_, ...), custom_call_target="tpu_custom_call", output_to_operand_aliasing={{}: (4, {})} | custom-call | tf_op jit(solution)/shard_map/pallas_call | solution.py:262
  62.0 0.2 collective-permute-done.14
  62.2 0.6 add_convert_fusion
  (4 shorter events, 0.0 us)
Async XLA Ops:
  0.6 13.5 %copy-start.4 = (s32[2,16]{1,0:T(2,128)S(1)}, s32[2,16]{1,0:T(2,128)}, u32[]{:S(2)}) copy-start(s32[2,16]{1,0:T(2,128)} %param.14) | copy-start | bytes 388
  0.6 18.4 %copy-start.5 = (f32[16]{0:T(128)S(1)}, f32[16]{0:T(128)}, u32[]{:S(2)}) copy-start(f32[16]{0:T(128)} %param.9) | copy-start | bytes 196
  2.6 56.1 %copy-start.1 = (bf16[2,2,2048]{2,1,0:T(2,128)(2,1)S(1)}, bf16[2,2,2048]{2,1,0:T(2,128)(2,1)}, u32[]{:S(2)}) copy-start(bf16[2,2,2048]{2,1,0:T(2,128)(2,1)} %k.7) | copy-start | bytes 49156
  2.6 56.1 %copy-start.2 = (bf16[2,2,2048]{2,1,0:T(2,128)(2,1)S(1)}, bf16[2,2,2048]{2,1,0:T(2,128)(2,1)}, u32[]{:S(2)}) copy-start(bf16[2,2,2048]{2,1,0:T(2,128)(2,1)} %v.7) | copy-start | bytes 49156
  2.6 57.6 %copy-start = (bf16[2048,768]{1,0:T(8,128)(2,1)S(1)}, bf16[2048,768]{1,0:T(8,128)(2,1)}, u32[]{:S(2)}) copy-start(bf16[2048,768]{1,0:T(8,128)(2,1)} %weight.1) | copy-start | bytes 9437188
  2.6 11.6 %collective-permute-start = (bf16[2,272,128]{2,1,0:T(8,128)(2,1)}, bf16[2,272,128]{2,1,0:T(8,128)(2,1)S(1)}, u32[]{:S(2)}, u32[]{:S(2)}) collective-permute-start(bf16[2,272,128]{2,1,0:T(8,128)(2,1)} %shard_map.95), channel_id=1, source_target_pairs={{0,8},{2,10},{4,12},{6,14},{8,0},{10,2},{12,4},{14,6},{1,9},{3,11}... | collective-permute-start | bytes 417800 | tf_op jit(solution)/shard_map/ppermute | solution.py:211
  9.1 8.5 %collective-permute-start.1 = (bf16[2,272,128]{2,1,0:T(8,128)(2,1)}, bf16[2,272,128]{2,1,0:T(8,128)(2,1)S(1)}, u32[]{:S(2)}, u32[]{:S(2)}) collective-permute-start(bf16[2,272,128]{2,1,0:T(8,128)(2,1)} %get-tuple-element.21), channel_id=1, source_target_pairs={{0,2},{2,0},{4,6},{6,4},{8,10},{10,8},{12,14},{14,12},{1,3},{3,1},... | collective-permute-start | bytes 417800 | tf_op jit(solution)/shard_map/ppermute | solution.py:211
  10.7 9.2 %collective-permute-start.2 = (bf16[2,272,128]{2,1,0:T(8,128)(2,1)}, bf16[2,272,128]{2,1,0:T(8,128)(2,1)S(1)}, u32[]{:S(2)}, u32[]{:S(2)}) collective-permute-start(bf16[2,272,128]{2,1,0:T(8,128)(2,1)} %get-tuple-element.22), channel_id=1, source_target_pairs={{0,4},{2,6},{4,0},{6,2},{8,12},{10,14},{12,8},{14,10},{1,5},{3,7},... | collective-permute-start | bytes 417800 | tf_op jit(solution)/shard_map/ppermute | solution.py:211
  12.3 16.1 %collective-permute-start.3 = (bf16[2,272,128]{2,1,0:T(8,128)(2,1)}, bf16[2,272,128]{2,1,0:T(8,128)(2,1)S(1)}, u32[]{:S(2)}, u32[]{:S(2)}) collective-permute-start(bf16[2,272,128]{2,1,0:T(8,128)(2,1)} %get-tuple-element.23), channel_id=1, source_target_pairs={{0,10},{2,8},{4,14},{6,12},{8,2},{10,0},{12,6},{14,4},{1,11},{3,9}... | collective-permute-start | bytes 417800 | tf_op jit(solution)/shard_map/ppermute | solution.py:211
  12.8 16.7 %collective-permute-start.4 = (bf16[2,272,128]{2,1,0:T(8,128)(2,1)}, bf16[2,272,128]{2,1,0:T(8,128)(2,1)S(1)}, u32[]{:S(2)}, u32[]{:S(2)}) collective-permute-start(bf16[2,272,128]{2,1,0:T(8,128)(2,1)} %get-tuple-element.24), channel_id=1, source_target_pairs={{0,6},{2,4},{4,2},{6,0},{8,14},{10,12},{12,10},{14,8},{1,7},{3,5},... | collective-permute-start | bytes 417800 | tf_op jit(solution)/shard_map/ppermute | solution.py:211
  14.2 15.3 %collective-permute-start.5 = (bf16[2,272,128]{2,1,0:T(8,128)(2,1)}, bf16[2,272,128]{2,1,0:T(8,128)(2,1)S(1)}, u32[]{:S(2)}, u32[]{:S(2)}) collective-permute-start(bf16[2,272,128]{2,1,0:T(8,128)(2,1)} %get-tuple-element.25), channel_id=1, source_target_pairs={{0,12},{2,14},{4,8},{6,10},{8,4},{10,6},{12,0},{14,2},{1,13},{3,15... | collective-permute-start | bytes 417800 | tf_op jit(solution)/shard_map/ppermute | solution.py:211
  17.6 11.8 %collective-permute-start.6 = (bf16[2,272,128]{2,1,0:T(8,128)(2,1)}, bf16[2,272,128]{2,1,0:T(8,128)(2,1)S(1)}, u32[]{:S(2)}, u32[]{:S(2)}) collective-permute-start(bf16[2,272,128]{2,1,0:T(8,128)(2,1)} %get-tuple-element.26), channel_id=1, source_target_pairs={{0,14},{2,12},{4,10},{6,8},{8,6},{10,4},{12,2},{14,0},{1,15},{3,13... | collective-permute-start | bytes 417800 | tf_op jit(solution)/shard_map/ppermute | solution.py:211
  19.0 0.9 %copy-start.3 = (bf16[2,272,128]{2,1,0:T(8,128)(2,1)S(1)}, bf16[2,272,128]{2,1,0:T(8,128)(2,1)}, u32[]{:S(2)}) copy-start(bf16[2,272,128]{2,1,0:T(8,128)(2,1)} %get-tuple-element.27.chunk) | copy-start | bytes 417796
  30.6 15.1 %collective-permute-start.7 = (bf16[592,128]{1,0:T(8,128)(2,1)S(1)}, bf16[592,128]{1,0:T(8,128)(2,1)S(1)}, u32[]{:S(2)}, u32[]{:S(2)}) collective-permute-start(bf16[592,128]{1,0:T(8,128)(2,1)S(1)} %get-tuple-element.28), channel_id=1, source_target_pairs={{0,8},{2,10},{4,12},{6,14},{8,0},{10,2},{12,4},{14,6},{1,9},{3,11}... | collective-permute-start | bytes 454664 | tf_op jit(solution)/shard_map/ppermute | solution.py:211
  36.3 9.4 %collective-permute-start.8 = (bf16[592,128]{1,0:T(8,128)(2,1)S(1)}, bf16[592,128]{1,0:T(8,128)(2,1)S(1)}, u32[]{:S(2)}, u32[]{:S(2)}) collective-permute-start(bf16[592,128]{1,0:T(8,128)(2,1)S(1)} %get-tuple-element.29), channel_id=1, source_target_pairs={{0,2},{2,0},{4,6},{6,4},{8,10},{10,8},{12,14},{14,12},{1,3},{3,1},... | collective-permute-start | bytes 454664 | tf_op jit(solution)/shard_map/ppermute | solution.py:211
  36.8 12.1 %collective-permute-start.9 = (bf16[592,128]{1,0:T(8,128)(2,1)S(1)}, bf16[592,128]{1,0:T(8,128)(2,1)S(1)}, u32[]{:S(2)}, u32[]{:S(2)}) collective-permute-start(bf16[592,128]{1,0:T(8,128)(2,1)S(1)} %get-tuple-element.30), channel_id=1, source_target_pairs={{0,4},{2,6},{4,0},{6,2},{8,12},{10,14},{12,8},{14,10},{1,5},{3,7},... | collective-permute-start | bytes 454664 | tf_op jit(solution)/shard_map/ppermute | solution.py:211
  36.9 14.6 %collective-permute-start.10 = (bf16[592,128]{1,0:T(8,128)(2,1)S(1)}, bf16[592,128]{1,0:T(8,128)(2,1)S(1)}, u32[]{:S(2)}, u32[]{:S(2)}) collective-permute-start(bf16[592,128]{1,0:T(8,128)(2,1)S(1)} %get-tuple-element.31), channel_id=1, source_target_pairs={{0,10},{2,8},{4,14},{6,12},{8,2},{10,0},{12,6},{14,4},{1,11},{3,9}... | collective-permute-start | bytes 454664 | tf_op jit(solution)/shard_map/ppermute | solution.py:211
  39.9 18.8 %collective-permute-start.11 = (bf16[592,128]{1,0:T(8,128)(2,1)S(1)}, bf16[592,128]{1,0:T(8,128)(2,1)S(1)}, u32[]{:S(2)}, u32[]{:S(2)}) collective-permute-start(bf16[592,128]{1,0:T(8,128)(2,1)S(1)} %get-tuple-element.32), channel_id=1, source_target_pairs={{0,6},{2,4},{4,2},{6,0},{8,14},{10,12},{12,10},{14,8},{1,7},{3,5},... | collective-permute-start | bytes 454664 | tf_op jit(solution)/shard_map/ppermute | solution.py:211
  45.7 12.9 %collective-permute-start.12 = (bf16[592,128]{1,0:T(8,128)(2,1)S(1)}, bf16[592,128]{1,0:T(8,128)(2,1)S(1)}, u32[]{:S(2)}, u32[]{:S(2)}) collective-permute-start(bf16[592,128]{1,0:T(8,128)(2,1)S(1)} %get-tuple-element.33), channel_id=1, source_target_pairs={{0,12},{2,14},{4,8},{6,10},{8,4},{10,6},{12,0},{14,2},{1,13},{3,15... | collective-permute-start | bytes 454664 | tf_op jit(solution)/shard_map/ppermute | solution.py:211
  45.7 14.5 %collective-permute-start.13 = (bf16[592,128]{1,0:T(8,128)(2,1)S(1)}, bf16[592,128]{1,0:T(8,128)(2,1)S(1)}, u32[]{:S(2)}, u32[]{:S(2)}) collective-permute-start(bf16[592,128]{1,0:T(8,128)(2,1)S(1)} %get-tuple-element.34), channel_id=1, source_target_pairs={{0,14},{2,12},{4,10},{6,8},{8,6},{10,4},{12,2},{14,0},{1,15},{3,13... | collective-permute-start | bytes 454664 | tf_op jit(solution)/shard_map/ppermute | solution.py:211
  60.9 1.3 %collective-permute-start.14 = (f32[2,8,768]{2,1,0:T(8,128)S(1)}, f32[2,8,768]{2,1,0:T(8,128)S(1)}, u32[]{:S(2)}, u32[]{:S(2)}) collective-permute-start(f32[2,8,768]{2,1,0:T(8,128)S(1)} %get-tuple-element.38), channel_id=1, source_target_pairs={{0,1},{1,0},{2,3},{3,2},{4,5},{5,4},{6,7},{7,6},{8,9},{9,8},{10,11... | collective-permute-start | bytes 147464 | tf_op jit(solution)/shard_map/ppermute | solution.py:287

commit v4 on v3

--- a/solution.py
+++ b/solution.py
@@ -42,19 +42,23 @@
     def lanes(head, count):
         return pl.ds(pl.multiple_of(head * dim, dim), count * dim)
 
-    small = [pltpu.make_async_copy(ref, vectors.at[a], sem_small.at[a]) for a, ref in enumerate((q, k, v, g))]
+    at = lanes((me ^ order[0]) * heads, heads) if len(order) == 1 else slice(None)
+    small = [
+        pltpu.make_async_copy(ref.at[:, :, at], vectors.at[a, :, :, at], sem_small.at[a])
+        for a, ref in enumerate((q, k, v, g))
+    ]
     large = {}
     for x in order:
-        at = lanes((me ^ x) * heads, heads)
-        large[x] = pltpu.make_async_copy(st_hbm.at[:, :, at], st.at[:, :, at], sem.at[x])
-    for c in small + list(large.values()):
+        here = lanes((me ^ x) * heads, heads)
+        large[x] = pltpu.make_async_copy(st_hbm.at[:, :, here], st.at[:, :, here], sem.at[x])
+    for c in [large[order[0]], *small, *list(large.values())[1:]]:
         c.start()
     for a in range(ARRAYS):
         small[a].wait()
-        whole = vectors[a].astype(F32)
+        whole = vectors[a, :, :, at].astype(F32)
         for t in range(STEPS):
             for j in range(slots):
-                rows[j, a * STEPS + t : a * STEPS + t + 1, :] = whole[t, j : j + 1]
+                rows[j, a * STEPS + t : a * STEPS + t + 1, at] = whole[t, j : j + 1]
     for x in order:
         large[x].wait()
         first = (me ^ x) * heads
@@ -93,13 +97,17 @@
                 c.wait()
         for j in range(slots):
             slot = (me ^ x) * slots + j
-            buf[slot] = ins[x][j, :depth, :]
+            for i in range(heads):
+                to = pl.ds(pl.multiple_of(slot * dim, dim), dim)
+                buf[i, to, :] = ins[x][j, i * dim : (i + 1) * dim, :]
             at = pl.multiple_of(slot * EXTRA, EXTRA)
             vectors[pl.ds(at, EXTRA), :] = ins[x][j, depth:, :].astype(F32)
     for x in range(n):
         for j in range(slots):
             middle = parents[1, (me ^ x) * slots + j]
-            outs[x][j * depth : (j + 1) * depth, :] = buf[parents[0, middle]]
+            root = pl.ds(pl.multiple_of(parents[0, middle] * dim, dim), dim)
+            for i in range(heads):
+                outs[x][j * depth + i * dim : j * depth + (i + 1) * dim, :] = buf[i, root, :]
             for i in range(heads):
                 for place, array in enumerate((K, V)):
                     to = j * KEPT + i * 2 + place
@@ -124,10 +132,8 @@
         q1, q2, k1, k2 = get(Q, 0), get(Q, 1), get(K, 0), get(K, 1)
         v1, v2 = get(V, 0), get(V, 1)
         queries = jnp.concatenate([q1, q2], 0)
-        acc = jnp.zeros((STEPS * total, dim), F32)
-        for slot in range(total):
-            mine = jnp.where(source == slot, queries, 0.0).astype(BF16)
-            acc += jnp.dot(mine, buf[slot, i * dim : (i + 1) * dim, :], preferred_element_type=F32)
+        mine = [jnp.where(source == slot, queries, 0.0).astype(BF16) for slot in range(total)]
+        acc = jnp.dot(jnp.concatenate(mine, 1), buf[i], preferred_element_type=F32)
         k1m = jnp.dot(pick, k1.astype(BF16), preferred_element_type=F32)
         v1m = jnp.dot(pick, v1.astype(BF16), preferred_element_type=F32)
         r1 = d * acc[:total] + jnp.sum(q1 * k1, -1, keepdims=True) * v1
@@ -140,19 +146,24 @@
             outs[x][at : at + STEPS * total, :] = attn
 
 
-def project_kernel(n, order, head_count, slots, weight, *rest):
-    ins, (keep, send, terms) = by_partner(order, rest[:n]), rest[n + 1 :]
-    me, head = lax.axis_index("beam"), lax.axis_index("head")
-    lines, dim = terms.shape[0], ins[0].shape[1]
+def project(n, slots, lines, weight, ins):
+    me = lax.axis_index("beam")
+    dim = next(iter(ins.values())).shape[1]
     heads = weight.shape[0] // dim // n
     first = slots * (heads * dim + KEPT)
     acc = None
-    for x in range(n):
+    for x, ref in ins.items():
         rows = pl.ds(pl.multiple_of((me ^ x) * heads * dim, dim), heads * dim)
-        lhs = [ins[x][first + i * lines : first + (i + 1) * lines, :] for i in range(heads)]
+        lhs = [ref[first + i * lines : first + (i + 1) * lines, :] for i in range(heads)]
         term = jnp.dot(jnp.concatenate(lhs, 1), weight[rows, :], preferred_element_type=F32)
         acc = term if acc is None else acc + term
-    terms[...] = acc
+    return acc
+
+
+def project_kernel(n, order, head_count, slots, weight, begun, *rest):
+    ins, (keep, send, terms) = dict(zip(order, rest)), rest[len(order) :]
+    head, lines = lax.axis_index("head"), terms.shape[0]
+    terms[...] = begun[...] + project(n, slots, lines, weight, ins)
     part = lines // STEPS // head_count
     for t in range(STEPS):
         own = pl.multiple_of(t * part * head_count + head * part, part)
@@ -162,10 +173,12 @@
 
 
 def final_kernel(n, order, first, decay, k, v, *rest):
-    ins, (result, *token, out, ks, vs, sem) = dict(zip(order, rest)), rest[-5 - first :]
     if first:
-        token[0][...] = jnp.zeros_like(token[0])
+        weight, *rest = rest
+    ins, (result, *terms, out, ks, vs, sem) = dict(zip(order, rest)), rest[-5 - first :]
     slots, dim, columns = result.shape
+    if first:
+        terms[0][...] = project(n, slots, terms[0].shape[0], weight, ins)
     heads = columns // dim // n
     depth = heads * dim
     me = lax.axis_index("beam")
@@ -244,7 +257,7 @@
         in_specs=[ANY] + [VMEM] * n + [ANY],
         out_specs=[VMEM] * n,
         scratch_shapes=[
-            pltpu.VMEM((total, depth, dim), BF16),
+            pltpu.VMEM((heads, total * dim, dim), BF16),
             pltpu.VMEM((total * EXTRA, dim), F32),
             pltpu.VMEM((slots * KEPT, dim), F32),
             pltpu.SMEM(table.shape, jnp.int32),
@@ -259,10 +272,11 @@
     whole = jax.ShapeDtypeStruct(states.shape, F32)
 
     def finish(part, *before):
+        more = [] if before else [out_weight]
         return pl.pallas_call(
             functools.partial(final_kernel, n, part, not before),
-            out_shape=[whole] if before else [whole, jax.ShapeDtypeStruct((8, dim), F32)],
-            in_specs=[VMEM] * (len(part) + 3) + [ANY] * len(before),
+            out_shape=[whole] if before else [whole, jax.ShapeDtypeStruct((STEPS * total, out_weight.shape[1]), F32)],
+            in_specs=[VMEM] * (len(more) + len(part) + 3) + [ANY] * len(before),
             out_specs=[ANY] if before else [ANY, VMEM],
             input_output_aliases={len(part) + 3: 0} if before else {},
             scratch_shapes=[
@@ -272,18 +286,18 @@
                 pltpu.SemaphoreType.DMA((n,)),
             ],
             compiler_params=params(),
-        )(decay, key_vectors, values, *[held[x] for x in part], *before)
-
-    begun, token = finish(second[:6] + second[-1:])
+        )(decay, key_vectors, values, *more, *[held[x] for x in part], *before)
+
+    begun, partial = finish(second[:6] + second[-1:])
     piece = jax.ShapeDtypeStruct((STEPS, total // head_count, out_weight.shape[1]), F32)
     keep, send = pl.pallas_call(
-        functools.partial(project_kernel, n, second, head_count, slots),
+        functools.partial(project_kernel, n, second[6:-1], head_count, slots),
         out_shape=[piece, piece],
-        in_specs=[VMEM] * (n + 1) + [VMEM],
+        in_specs=[VMEM] * (n + 1 - 6),
         out_specs=[VMEM] * 2,
         scratch_shapes=[pltpu.VMEM((STEPS * total, out_weight.shape[1]), F32)],
         compiler_params=params(),
-    )(out_weight, *forked, token)
+    )(out_weight, partial, *forked[6:-1])
     other = lax.ppermute(send, "head", [(0, 1), (1, 0)])
     projected = (keep + other).astype(BF16)
     (final,) = finish(second[6:-1], begun)

time: 64 us -> 63.4 us (level)
  no operation moved by 1% of the time
where the time goes in v4:
time: 63.4 us; the launch traced here: 62.5 us
  starting transfers between devices  26.4 us (42%)
  waiting for transfers between devices  25.3 us (40%)
  Pallas kernels  8.37 us (13%)
  local copies, waits for them, and re-layouts  1.01 us (2%)
  between operations  0.78 us (1%)
    ppermute x14, starting transfers between devices, exchange(): lax.ppermute(chunk, 'beam', [(j, j ^ x) for j in range(n)])  26.4 us
    ppermute x14, waiting for transfers between devices, exchange(): lax.ppermute(chunk, 'beam', [(j, j ^ x) for j in range(n)])  25.1 us
    pallas_call x2, Pallas kernels, fast(): pl.pallas_call(functools.partial(pack_kernel, n, part), out_shape=[jax.Sh...  4.33 us
    pallas_call x2, Pallas kernels, finish(): pl.pallas_call(functools.partial(final_kernel, n, part, not before), out_...  2.84 us
  transfers between devices with their start and end apart: 15, of which 6 were waited for; matrix products, arithmetic and copies ran while one was open for 0% of the time, Pallas kernels for 8%

profile of v4, /device:TPU:0, one launch (start us, length us, event | category | flops | bytes accessed | tf_op | source)
XLA Modules:
  0.0 62.5 jit_solution(1652177604830936916)
XLA Ops:
  0.6 0.0 copy-start.4
  0.6 0.0 copy-start.5
  0.6 1.9 %shard_map.95 = bf16[2,272,128]{2,1,0:T(8,128)(2,1)} custom-call(f32[2,128,2048]{2,1,0:T(8,128)} %st_hbm.3, bf16[2,2,2048]{2,1,0:T(2,128)(2,1)} %q.3, bf16[2,2,2048]{2,1,0:T(2,128)(2,1)} %k.7, bf16[2,2,2048]{2,1,0:T(2,128)(2,1)} %v.7, bf16[2,2,2048]{2,1,0:T(2,128)(2,1)} %g.3), custom_call_target="tpu_custom_call" | custom-call | tf_op jit(solution)/shard_map/pallas_call | solution.py:231
  2.5 0.0 copy-start
  2.6 0.0 copy-start.1
  2.6 0.0 copy-start.2
  2.6 4.1 %collective-permute-start = (bf16[2,272,128]{2,1,0:T(8,128)(2,1)}, bf16[2,272,128]{2,1,0:T(8,128)(2,1)S(1)}, u32[]{:S(2)}, u32[]{:S(2)}) collective-permute-start(bf16[2,272,128]{2,1,0:T(8,128)(2,1)} %shard_map.95), channel_id=1, source_target_pairs={{0,8},{2,10},{4,12},{6,14},{8,0},{10,2},{12,4},{14,6},{1,9},{3,11}... | collective-permute-start | bytes 417800 | tf_op jit(solution)/shard_map/ppermute | solution.py:224
  6.7 2.4 %shard_map.96 = (bf16[2,272,128]{2,1,0:T(8,128)(2,1)}, bf16[2,272,128]{2,1,0:T(8,128)(2,1)}, bf16[2,272,128]{2,1,0:T(8,128)(2,1)}, bf16[2,272,128]{2,1,0:T(8,128...) custom-call(f32[2,128,2048]{2,1,0:T(8,128)} %st_hbm.3, ...), custom_call_target="tpu_custom_call" | custom-call | tf_op jit(solution)/shard_map/pallas_call | solution.py:231
  9.1 1.6 %collective-permute-start.1 = (bf16[2,272,128]{2,1,0:T(8,128)(2,1)}, bf16[2,272,128]{2,1,0:T(8,128)(2,1)S(1)}, u32[]{:S(2)}, u32[]{:S(2)}) collective-permute-start(bf16[2,272,128]{2,1,0:T(8,128)(2,1)} %get-tuple-element.21), channel_id=1, source_target_pairs={{0,2},{2,0},{4,6},{6,4},{8,10},{10,8},{12,14},{14,12},{1,3},{3,1},... | collective-permute-start | bytes 417800 | tf_op jit(solution)/shard_map/ppermute | solution.py:224
  10.7 1.6 %collective-permute-start.2 = (bf16[2,272,128]{2,1,0:T(8,128)(2,1)}, bf16[2,272,128]{2,1,0:T(8,128)(2,1)S(1)}, u32[]{:S(2)}, u32[]{:S(2)}) collective-permute-start(bf16[2,272,128]{2,1,0:T(8,128)(2,1)} %get-tuple-element.22), channel_id=1, source_target_pairs={{0,4},{2,6},{4,0},{6,2},{8,12},{10,14},{12,8},{14,10},{1,5},{3,7},... | collective-permute-start | bytes 417800 | tf_op jit(solution)/shard_map/ppermute | solution.py:224
  12.3 0.5 collective-permute-start.3
  12.8 1.4 %collective-permute-start.4 = (bf16[2,272,128]{2,1,0:T(8,128)(2,1)}, bf16[2,272,128]{2,1,0:T(8,128)(2,1)S(1)}, u32[]{:S(2)}, u32[]{:S(2)}) collective-permute-start(bf16[2,272,128]{2,1,0:T(8,128)(2,1)} %get-tuple-element.24), channel_id=1, source_target_pairs={{0,6},{2,4},{4,2},{6,0},{8,14},{10,12},{12,10},{14,8},{1,7},{3,5},... | collective-permute-start | bytes 417800 | tf_op jit(solution)/shard_map/ppermute | solution.py:224
  14.2 0.0 copy-done.4
  14.2 0.0 collective-permute-done.rest_0_
  14.2 3.5 %collective-permute-start.5 = (bf16[2,272,128]{2,1,0:T(8,128)(2,1)}, bf16[2,272,128]{2,1,0:T(8,128)(2,1)S(1)}, u32[]{:S(2)}, u32[]{:S(2)}) collective-permute-start(bf16[2,272,128]{2,1,0:T(8,128)(2,1)} %get-tuple-element.25), channel_id=1, source_target_pairs={{0,12},{2,14},{4,8},{6,10},{8,4},{10,6},{12,0},{14,2},{1,13},{3,15... | collective-permute-start | bytes 417800 | tf_op jit(solution)/shard_map/ppermute | solution.py:224
  17.6 0.0 collective-permute-done.1.rest_1_
  17.6 1.3 %collective-permute-start.6 = (bf16[2,272,128]{2,1,0:T(8,128)(2,1)}, bf16[2,272,128]{2,1,0:T(8,128)(2,1)S(1)}, u32[]{:S(2)}, u32[]{:S(2)}) collective-permute-start(bf16[2,272,128]{2,1,0:T(8,128)(2,1)} %get-tuple-element.26), channel_id=1, source_target_pairs={{0,14},{2,12},{4,10},{6,8},{8,6},{10,4},{12,2},{14,0},{1,15},{3,13... | collective-permute-start | bytes 417800 | tf_op jit(solution)/shard_map/ppermute | solution.py:224
  19.0 0.0 copy-done.5
  19.0 0.0 copy-start.3
  19.0 0.9 %copy-done.3 = bf16[2,272,128]{2,1,0:T(8,128)(2,1)S(1)} copy-done((bf16[2,272,128]{2,1,0:T(8,128)(2,1)S(1)}, bf16[2,272,128]{2,1,0:T(8,128)(2,1)}, u32[]{:S(2)}) %copy-start.3) | copy-done | bytes 139288
  19.9 0.0 collective-permute-done.2.rest_2_
  19.9 8.4 %collective-permute-done.3.rest_3_ = bf16[2,272,128]{2,1,0:T(8,128)(2,1)S(1)} collective-permute-done((bf16[2,272,128]{2,1,0:T(8,128)(2,1)}, bf16[2,272,128]{2,1,0:T(8,128)(2,1)S(1)}, u32[]{:S(2)}, u32[]{:S(2)}) %collective-permute-start.3) | collective-permute-done | bytes 139296 | tf_op jit(solution)/shard_map/ppermute | solution.py:224
  28.3 1.1 %collective-permute-done.4.rest_4_ = bf16[2,272,128]{2,1,0:T(8,128)(2,1)S(1)} collective-permute-done((bf16[2,272,128]{2,1,0:T(8,128)(2,1)}, bf16[2,272,128]{2,1,0:T(8,128)(2,1)S(1)}, u32[]{:S(2)}, u32[]{:S(2)}) %collective-permute-start.4) | collective-permute-done | bytes 139296 | tf_op jit(solution)/shard_map/ppermute | solution.py:224
  29.4 0.0 collective-permute-done.5.rest_5_
  29.5 0.0 collective-permute-done.6.rest_6_
  29.5 0.1 broadcast_in_dim.2.decay
  29.5 1.0 %shard_map.98 = (bf16[592,128]{1,0:T(8,128)(2,1)S(1)}, bf16[592,128]{1,0:T(8,128)(2,1)S(1)}, bf16[592,128]{1,0:T(8,128)(2,1)S(1)}, bf16[592,128]{1,0:T(8,128)(2,...) custom-call(s32[4,16]{1,0:T(4,128)S(1)} %pad_add_fusion.parents_hbm,, ...), custom_call_target="tpu_custom_call" | custom-call | tf_op jit(solution)/shard_map/pallas_call | solution.py:254
  30.5 5.7 %collective-permute-start.7 = (bf16[592,128]{1,0:T(8,128)(2,1)S(1)}, bf16[592,128]{1,0:T(8,128)(2,1)S(1)}, u32[]{:S(2)}, u32[]{:S(2)}) collective-permute-start(bf16[592,128]{1,0:T(8,128)(2,1)S(1)} %get-tuple-element.28), channel_id=1, source_target_pairs={{0,8},{2,10},{4,12},{6,14},{8,0},{10,2},{12,4},{14,6},{1,9},{3,11}... | collective-permute-start | bytes 454664 | tf_op jit(solution)/shard_map/ppermute | solution.py:224
  36.2 0.5 collective-permute-start.8
  36.7 0.0 collective-permute-start.9
  36.7 3.0 %collective-permute-start.10 = (bf16[592,128]{1,0:T(8,128)(2,1)S(1)}, bf16[592,128]{1,0:T(8,128)(2,1)S(1)}, u32[]{:S(2)}, u32[]{:S(2)}) collective-permute-start(bf16[592,128]{1,0:T(8,128)(2,1)S(1)} %get-tuple-element.31), channel_id=1, source_target_pairs={{0,10},{2,8},{4,14},{6,12},{8,2},{10,0},{12,6},{14,4},{1,11},{3,9}... | collective-permute-start | bytes 454664 | tf_op jit(solution)/shard_map/ppermute | solution.py:224
  39.7 0.0 collective-permute-start.11
  39.7 5.8 %collective-permute-done.7.rest_1_ = bf16[592,128]{1,0:T(8,128)(2,1)S(1)} collective-permute-done((bf16[592,128]{1,0:T(8,128)(2,1)S(1)}, bf16[592,128]{1,0:T(8,128)(2,1)S(1)}, u32[]{:S(2)}, u32[]{:S(2)}) %collective-permute-start.7) | collective-permute-done | bytes 151584 | tf_op jit(solution)/shard_map/ppermute | solution.py:224
  45.6 0.0 collective-permute-start.12
  45.6 0.0 collective-permute-done.8.rest_2_
  45.6 3.2 %collective-permute-start.13 = (bf16[592,128]{1,0:T(8,128)(2,1)S(1)}, bf16[592,128]{1,0:T(8,128)(2,1)S(1)}, u32[]{:S(2)}, u32[]{:S(2)}) collective-permute-start(bf16[592,128]{1,0:T(8,128)(2,1)S(1)} %get-tuple-element.36), channel_id=1, source_target_pairs={{0,14},{2,12},{4,10},{6,8},{8,6},{10,4},{12,2},{14,0},{1,15},{3,13... | collective-permute-start | bytes 454664 | tf_op jit(solution)/shard_map/ppermute | solution.py:224
  48.8 0.0 collective-permute-done.9.rest_3_
  48.8 2.5 %collective-permute-done.10.rest_4_ = bf16[592,128]{1,0:T(8,128)(2,1)S(1)} collective-permute-done((bf16[592,128]{1,0:T(8,128)(2,1)S(1)}, bf16[592,128]{1,0:T(8,128)(2,1)S(1)}, u32[]{:S(2)}, u32[]{:S(2)}) %collective-permute-start.10) | collective-permute-done | bytes 151584 | tf_op jit(solution)/shard_map/ppermute | solution.py:224
  51.3 7.2 %collective-permute-done.11.rest_5_ = bf16[592,128]{1,0:T(8,128)(2,1)S(1)} collective-permute-done((bf16[592,128]{1,0:T(8,128)(2,1)S(1)}, bf16[592,128]{1,0:T(8,128)(2,1)S(1)}, u32[]{:S(2)}, u32[]{:S(2)}) %collective-permute-start.11) | collective-permute-done | bytes 151584 | tf_op jit(solution)/shard_map/ppermute | solution.py:224
  58.5 0.0 collective-permute-done.12.rest_6_
  58.5 0.0 copy-done
  58.5 0.0 copy-done.1
  58.5 0.0 copy-done.2
  58.5 1.8 %shard_map.99 = (f32[2,128,2048]{2,1,0:T(8,128)}, f32[32,768]{1,0:T(8,128)S(1)}) custom-call(f32[16,128]{1,0:T(8,128)S(1)} %broadcast_in_dim.2.decay, bf16[2,2,2048]{2,1,0:T(2,128)(2,1)S(1)} %copy-done.1, bf16[2,2,2048]{2,1,0:T(2,128)(2,1)S(1)} %copy-done.2, bf16[2048,768]{1,0:T(8,128)(2,1)S(1)} %copy-done, ...), custom_call_target="tpu_custom_call" | custom-call | tf_op jit(solution)/shard_map/pallas_call | solution.py:276
  60.4 0.0 collective-permute-done.13.rest_0_
  60.4 0.2 shard_map.100
  60.6 0.0 collective-permute-start.14
  60.6 1.0 %shard_map.101 = f32[2,128,2048]{2,1,0:T(8,128)} custom-call(f32[16,128]{1,0:T(8,128)S(1)} %broadcast_in_dim.2.decay, bf16[2,2,2048]{2,1,0:T(2,128)(2,1)S(1)} %copy-done.1, bf16[2,2,2048]{2,1,0:T(2,128)(2,1)S(1)} %copy-done.2, bf16[592,128]{1,0:T(8,128)(2,1)S(1)} %collective-permute-done.13.rest_0_, ...), custom_call_target="tpu_custom_call", output_to_operand_aliasing={{}: (4, {})} | custom-call | tf_op jit(solution)/shard_map/pallas_call | solution.py:276
  61.7 0.2 collective-permute-done.14
  61.9 0.6 add_convert_fusion
  (4 shorter events, 0.0 us)
Async XLA Ops:
  0.6 13.5 %copy-start.4 = (s32[2,16]{1,0:T(2,128)S(1)}, s32[2,16]{1,0:T(2,128)}, u32[]{:S(2)}) copy-start(s32[2,16]{1,0:T(2,128)} %param.14) | copy-start | bytes 388
  0.6 18.3 %copy-start.5 = (f32[16]{0:T(128)S(1)}, f32[16]{0:T(128)}, u32[]{:S(2)}) copy-start(f32[16]{0:T(128)} %param.9) | copy-start | bytes 196
  2.5 56.0 %copy-start = (bf16[2048,768]{1,0:T(8,128)(2,1)S(1)}, bf16[2048,768]{1,0:T(8,128)(2,1)}, u32[]{:S(2)}) copy-start(bf16[2048,768]{1,0:T(8,128)(2,1)} %weight.1) | copy-start | bytes 9437188
  2.6 56.0 %copy-start.1 = (bf16[2,2,2048]{2,1,0:T(2,128)(2,1)S(1)}, bf16[2,2,2048]{2,1,0:T(2,128)(2,1)}, u32[]{:S(2)}) copy-start(bf16[2,2,2048]{2,1,0:T(2,128)(2,1)} %k.7) | copy-start | bytes 49156
  2.6 56.0 %copy-start.2 = (bf16[2,2,2048]{2,1,0:T(2,128)(2,1)S(1)}, bf16[2,2,2048]{2,1,0:T(2,128)(2,1)}, u32[]{:S(2)}) copy-start(bf16[2,2,2048]{2,1,0:T(2,128)(2,1)} %v.7) | copy-start | bytes 49156
  2.6 11.6 %collective-permute-start = (bf16[2,272,128]{2,1,0:T(8,128)(2,1)}, bf16[2,272,128]{2,1,0:T(8,128)(2,1)S(1)}, u32[]{:S(2)}, u32[]{:S(2)}) collective-permute-start(bf16[2,272,128]{2,1,0:T(8,128)(2,1)} %shard_map.95), channel_id=1, source_target_pairs={{0,8},{2,10},{4,12},{6,14},{8,0},{10,2},{12,4},{14,6},{1,9},{3,11}... | collective-permute-start | bytes 417800 | tf_op jit(solution)/shard_map/ppermute | solution.py:224
  9.1 8.5 %collective-permute-start.1 = (bf16[2,272,128]{2,1,0:T(8,128)(2,1)}, bf16[2,272,128]{2,1,0:T(8,128)(2,1)S(1)}, u32[]{:S(2)}, u32[]{:S(2)}) collective-permute-start(bf16[2,272,128]{2,1,0:T(8,128)(2,1)} %get-tuple-element.21), channel_id=1, source_target_pairs={{0,2},{2,0},{4,6},{6,4},{8,10},{10,8},{12,14},{14,12},{1,3},{3,1},... | collective-permute-start | bytes 417800 | tf_op jit(solution)/shard_map/ppermute | solution.py:224
  10.7 9.2 %collective-permute-start.2 = (bf16[2,272,128]{2,1,0:T(8,128)(2,1)}, bf16[2,272,128]{2,1,0:T(8,128)(2,1)S(1)}, u32[]{:S(2)}, u32[]{:S(2)}) collective-permute-start(bf16[2,272,128]{2,1,0:T(8,128)(2,1)} %get-tuple-element.22), channel_id=1, source_target_pairs={{0,4},{2,6},{4,0},{6,2},{8,12},{10,14},{12,8},{14,10},{1,5},{3,7},... | collective-permute-start | bytes 417800 | tf_op jit(solution)/shard_map/ppermute | solution.py:224
  12.3 16.1 %collective-permute-start.3 = (bf16[2,272,128]{2,1,0:T(8,128)(2,1)}, bf16[2,272,128]{2,1,0:T(8,128)(2,1)S(1)}, u32[]{:S(2)}, u32[]{:S(2)}) collective-permute-start(bf16[2,272,128]{2,1,0:T(8,128)(2,1)} %get-tuple-element.23), channel_id=1, source_target_pairs={{0,10},{2,8},{4,14},{6,12},{8,2},{10,0},{12,6},{14,4},{1,11},{3,9}... | collective-permute-start | bytes 417800 | tf_op jit(solution)/shard_map/ppermute | solution.py:224
  12.8 16.7 %collective-permute-start.4 = (bf16[2,272,128]{2,1,0:T(8,128)(2,1)}, bf16[2,272,128]{2,1,0:T(8,128)(2,1)S(1)}, u32[]{:S(2)}, u32[]{:S(2)}) collective-permute-start(bf16[2,272,128]{2,1,0:T(8,128)(2,1)} %get-tuple-element.24), channel_id=1, source_target_pairs={{0,6},{2,4},{4,2},{6,0},{8,14},{10,12},{12,10},{14,8},{1,7},{3,5},... | collective-permute-start | bytes 417800 | tf_op jit(solution)/shard_map/ppermute | solution.py:224
  14.2 15.3 %collective-permute-start.5 = (bf16[2,272,128]{2,1,0:T(8,128)(2,1)}, bf16[2,272,128]{2,1,0:T(8,128)(2,1)S(1)}, u32[]{:S(2)}, u32[]{:S(2)}) collective-permute-start(bf16[2,272,128]{2,1,0:T(8,128)(2,1)} %get-tuple-element.25), channel_id=1, source_target_pairs={{0,12},{2,14},{4,8},{6,10},{8,4},{10,6},{12,0},{14,2},{1,13},{3,15... | collective-permute-start | bytes 417800 | tf_op jit(solution)/shard_map/ppermute | solution.py:224
  17.6 11.8 %collective-permute-start.6 = (bf16[2,272,128]{2,1,0:T(8,128)(2,1)}, bf16[2,272,128]{2,1,0:T(8,128)(2,1)S(1)}, u32[]{:S(2)}, u32[]{:S(2)}) collective-permute-start(bf16[2,272,128]{2,1,0:T(8,128)(2,1)} %get-tuple-element.26), channel_id=1, source_target_pairs={{0,14},{2,12},{4,10},{6,8},{8,6},{10,4},{12,2},{14,0},{1,15},{3,13... | collective-permute-start | bytes 417800 | tf_op jit(solution)/shard_map/ppermute | solution.py:224
  19.0 0.9 %copy-start.3 = (bf16[2,272,128]{2,1,0:T(8,128)(2,1)S(1)}, bf16[2,272,128]{2,1,0:T(8,128)(2,1)}, u32[]{:S(2)}) copy-start(bf16[2,272,128]{2,1,0:T(8,128)(2,1)} %get-tuple-element.27.chunk) | copy-start | bytes 417796
  30.5 15.1 %collective-permute-start.7 = (bf16[592,128]{1,0:T(8,128)(2,1)S(1)}, bf16[592,128]{1,0:T(8,128)(2,1)S(1)}, u32[]{:S(2)}, u32[]{:S(2)}) collective-permute-start(bf16[592,128]{1,0:T(8,128)(2,1)S(1)} %get-tuple-element.28), channel_id=1, source_target_pairs={{0,8},{2,10},{4,12},{6,14},{8,0},{10,2},{12,4},{14,6},{1,9},{3,11}... | collective-permute-start | bytes 454664 | tf_op jit(solution)/shard_map/ppermute | solution.py:224
  36.2 9.4 %collective-permute-start.8 = (bf16[592,128]{1,0:T(8,128)(2,1)S(1)}, bf16[592,128]{1,0:T(8,128)(2,1)S(1)}, u32[]{:S(2)}, u32[]{:S(2)}) collective-permute-start(bf16[592,128]{1,0:T(8,128)(2,1)S(1)} %get-tuple-element.29), channel_id=1, source_target_pairs={{0,2},{2,0},{4,6},{6,4},{8,10},{10,8},{12,14},{14,12},{1,3},{3,1},... | collective-permute-start | bytes 454664 | tf_op jit(solution)/shard_map/ppermute | solution.py:224
  36.7 12.1 %collective-permute-start.9 = (bf16[592,128]{1,0:T(8,128)(2,1)S(1)}, bf16[592,128]{1,0:T(8,128)(2,1)S(1)}, u32[]{:S(2)}, u32[]{:S(2)}) collective-permute-start(bf16[592,128]{1,0:T(8,128)(2,1)S(1)} %get-tuple-element.30), channel_id=1, source_target_pairs={{0,4},{2,6},{4,0},{6,2},{8,12},{10,14},{12,8},{14,10},{1,5},{3,7},... | collective-permute-start | bytes 454664 | tf_op jit(solution)/shard_map/ppermute | solution.py:224
  36.7 14.6 %collective-permute-start.10 = (bf16[592,128]{1,0:T(8,128)(2,1)S(1)}, bf16[592,128]{1,0:T(8,128)(2,1)S(1)}, u32[]{:S(2)}, u32[]{:S(2)}) collective-permute-start(bf16[592,128]{1,0:T(8,128)(2,1)S(1)} %get-tuple-element.31), channel_id=1, source_target_pairs={{0,10},{2,8},{4,14},{6,12},{8,2},{10,0},{12,6},{14,4},{1,11},{3,9}... | collective-permute-start | bytes 454664 | tf_op jit(solution)/shard_map/ppermute | solution.py:224
  39.7 18.8 %collective-permute-start.11 = (bf16[592,128]{1,0:T(8,128)(2,1)S(1)}, bf16[592,128]{1,0:T(8,128)(2,1)S(1)}, u32[]{:S(2)}, u32[]{:S(2)}) collective-permute-start(bf16[592,128]{1,0:T(8,128)(2,1)S(1)} %get-tuple-element.32), channel_id=1, source_target_pairs={{0,6},{2,4},{4,2},{6,0},{8,14},{10,12},{12,10},{14,8},{1,7},{3,5},... | collective-permute-start | bytes 454664 | tf_op jit(solution)/shard_map/ppermute | solution.py:224
  45.6 12.9 %collective-permute-start.12 = (bf16[592,128]{1,0:T(8,128)(2,1)S(1)}, bf16[592,128]{1,0:T(8,128)(2,1)S(1)}, u32[]{:S(2)}, u32[]{:S(2)}) collective-permute-start(bf16[592,128]{1,0:T(8,128)(2,1)S(1)} %get-tuple-element.33), channel_id=1, source_target_pairs={{0,12},{2,14},{4,8},{6,10},{8,4},{10,6},{12,0},{14,2},{1,13},{3,15... | collective-permute-start | bytes 454664 | tf_op jit(solution)/shard_map/ppermute | solution.py:224
  45.6 14.8 %collective-permute-start.13 = (bf16[592,128]{1,0:T(8,128)(2,1)S(1)}, bf16[592,128]{1,0:T(8,128)(2,1)S(1)}, u32[]{:S(2)}, u32[]{:S(2)}) collective-permute-start(bf16[592,128]{1,0:T(8,128)(2,1)S(1)} %get-tuple-element.36), channel_id=1, source_target_pairs={{0,14},{2,12},{4,10},{6,8},{8,6},{10,4},{12,2},{14,0},{1,15},{3,13... | collective-permute-start | bytes 454664 | tf_op jit(solution)/shard_map/ppermute | solution.py:224
  60.6 1.3 %collective-permute-start.14 = (f32[2,8,768]{2,1,0:T(8,128)S(1)}, f32[2,8,768]{2,1,0:T(8,128)S(1)}, u32[]{:S(2)}, u32[]{:S(2)}) collective-permute-start(f32[2,8,768]{2,1,0:T(8,128)S(1)} %get-tuple-element.38), channel_id=1, source_target_pairs={{0,1},{1,0},{2,3},{3,2},{4,5},{5,4},{6,7},{7,6},{8,9},{9,8},{10,11... | collective-permute-start | bytes 147464 | tf_op jit(solution)/shard_map/ppermute | solution.py:301

commit v5 on v4

--- a/solution.py
+++ b/solution.py
@@ -81,7 +81,7 @@
 
 def middle_kernel(n, first, second, parents_hbm, decay, *rest):
     ins, outs = by_partner(first, rest[:n]), by_partner(second, rest[n : 2 * n])
-    buf, vectors, kept, parents, own, sem = rest[2 * n :]
+    attn_out, buf, vectors, kept, parents, own, sem = rest[2 * n :]
     copies = [pltpu.make_async_copy(parents_hbm, parents, sem.at[0]), pltpu.make_async_copy(ins[0], own, sem.at[1])]
     for c in copies:
         c.start()
@@ -141,18 +141,17 @@
         r2 = r2 + jnp.sum(q2 * k2, -1, keepdims=True) * v2
         attn = [jax.nn.sigmoid(get(G, 0)) * r1, jax.nn.sigmoid(get(G, 1)) * r2]
         attn = jnp.concatenate(attn, 0).astype(BF16)
-        at = slots * (depth + KEPT) + i * STEPS * total
-        for x in range(n):
-            outs[x][at : at + STEPS * total, :] = attn
-
-
-def project(n, slots, lines, weight, ins):
+        lines = slice(i * STEPS * total, (i + 1) * STEPS * total)
+        attn_out[lines, :] = attn
+        outs[n // 2][slots * (depth + KEPT) + lines.start : slots * (depth + KEPT) + lines.stop, :] = attn
+
+
+def project(n, lines, weight, pieces):
     me = lax.axis_index("beam")
-    dim = next(iter(ins.values())).shape[1]
+    dim = next(iter(pieces.values()))[0].shape[1]
     heads = weight.shape[0] // dim // n
-    first = slots * (heads * dim + KEPT)
     acc = None
-    for x, ref in ins.items():
+    for x, (ref, first) in pieces.items():
         rows = pl.ds(pl.multiple_of((me ^ x) * heads * dim, dim), heads * dim)
         lhs = [ref[first + i * lines : first + (i + 1) * lines, :] for i in range(heads)]
         term = jnp.dot(jnp.concatenate(lhs, 1), weight[rows, :], preferred_element_type=F32)
@@ -160,10 +159,19 @@
     return acc
 
 
-def project_kernel(n, order, head_count, slots, weight, begun, *rest):
-    ins, (keep, send, terms) = dict(zip(order, rest)), rest[len(order) :]
+def relay_kernel(have, got, out):
+    more = out.shape[0] - have.shape[0]
+    out[: have.shape[0], :] = have[...]
+    out[have.shape[0] :, :] = got[got.shape[0] - more :, :]
+
+
+def project_kernel(n, order, head_count, weight, begun, *rest):
+    keep, send, terms = rest[-3:]
+    pieces = {}
+    for places, ref in zip(order, rest):
+        pieces |= {x: (ref, at * (ref.shape[0] // len(places))) for at, x in enumerate(places)}
     head, lines = lax.axis_index("head"), terms.shape[0]
-    terms[...] = begun[...] + project(n, slots, lines, weight, ins)
+    terms[...] = begun[...] + project(n, lines, weight, pieces)
     part = lines // STEPS // head_count
     for t in range(STEPS):
         own = pl.multiple_of(t * part * head_count + head * part, part)
@@ -174,11 +182,13 @@
 
 def final_kernel(n, order, first, decay, k, v, *rest):
     if first:
-        weight, *rest = rest
+        weight, attn, *rest = rest
     ins, (result, *terms, out, ks, vs, sem) = dict(zip(order, rest)), rest[-5 - first :]
     slots, dim, columns = result.shape
     if first:
-        terms[0][...] = project(n, slots, terms[0].shape[0], weight, ins)
+        across = ins[n // 2]
+        pieces = {0: (attn, 0), n // 2: (across, across.shape[0] - attn.shape[0])}
+        terms[0][...] = project(n, terms[0].shape[0], weight, pieces)
     heads = columns // dim // n
     depth = heads * dim
     me = lax.axis_index("beam")
@@ -250,12 +260,16 @@
         out_specs=VMEM,
         compiler_params=params(),
     )(packed[-1])
-    lines = slots * (depth + KEPT) + heads * STEPS * total
-    picked = pl.pallas_call(
+    attn_shape = jax.ShapeDtypeStruct((heads * STEPS * total, dim), BF16)
+    lines = slots * (depth + KEPT)
+    *picked, attn = pl.pallas_call(
         functools.partial(middle_kernel, n, first, second),
-        out_shape=[jax.ShapeDtypeStruct((lines, dim), BF16)] * n,
+        out_shape=[
+            jax.ShapeDtypeStruct((lines + (attn_shape.shape[0] if x == n // 2 else 0), dim), BF16) for x in second
+        ]
+        + [attn_shape],
         in_specs=[ANY] + [VMEM] * n + [ANY],
-        out_specs=[VMEM] * n,
+        out_specs=[VMEM] * (n + 1),
         scratch_shapes=[
             pltpu.VMEM((heads, total * dim, dim), BF16),
             pltpu.VMEM((total * EXTRA, dim), F32),
@@ -268,11 +282,25 @@
     )(table, decay, *exchange(first, packed))
     forked = exchange(second, picked)
     held = dict(zip(second, forked))
+    have, got, places, hop = attn, held[n // 2], [0, n // 2], 1
+    relayed = {}
+    while hop < n // 2:
+        have = pl.pallas_call(
+            relay_kernel,
+            out_shape=jax.ShapeDtypeStruct((len(places) * attn.shape[0], dim), BF16),
+            in_specs=[VMEM] * 2,
+            out_specs=VMEM,
+            compiler_params=params(),
+        )(have, got)
+        (got,) = exchange([hop], [have])
+        relayed[tuple(x ^ hop for x in places)] = got
+        places += [x ^ hop for x in places]
+        hop *= 2
 
     whole = jax.ShapeDtypeStruct(states.shape, F32)
 
     def finish(part, *before):
-        more = [] if before else [out_weight]
+        more = [] if before else [out_weight, attn]
         return pl.pallas_call(
             functools.partial(final_kernel, n, part, not before),
             out_shape=[whole] if before else [whole, jax.ShapeDtypeStruct((STEPS * total, out_weight.shape[1]), F32)],
@@ -288,19 +316,19 @@
             compiler_params=params(),
         )(decay, key_vectors, values, *more, *[held[x] for x in part], *before)
 
-    begun, partial = finish(second[:6] + second[-1:])
+    begun, partial = finish(second[:5] + second[-1:])
     piece = jax.ShapeDtypeStruct((STEPS, total // head_count, out_weight.shape[1]), F32)
     keep, send = pl.pallas_call(
-        functools.partial(project_kernel, n, second[6:-1], head_count, slots),
+        functools.partial(project_kernel, n, list(relayed), head_count),
         out_shape=[piece, piece],
-        in_specs=[VMEM] * (n + 1 - 6),
+        in_specs=[VMEM] * (2 + len(relayed)),
         out_specs=[VMEM] * 2,
         scratch_shapes=[pltpu.VMEM((STEPS * total, out_weight.shape[1]), F32)],
         compiler_params=params(),
-    )(out_weight, partial, *forked[6:-1])
+    )(out_weight, partial, *relayed.values())
     other = lax.ppermute(send, "head", [(0, 1), (1, 0)])
     projected = (keep + other).astype(BF16)
-    (final,) = finish(second[6:-1], begun)
+    (final,) = finish(second[5:-1], begun)
     return projected, final
 
 

time: 63.4 us -> 60.6 us (0.956); the launches traced: 62.5 us -> 60.4 us
  waiting for transfers between devices: 25.3 us -> 23.1 us
    ppermute x14 -> x16, waiting for transfers between devices: 25.1 us -> 23.1 us  [exchange(): lax.ppermute(chunk, 'beam', [(j, j ^ x) for j in range(n)])]
    ppermute x14 -> x16, starting transfers between devices: 26.4 us -> 26.4 us  [exchange(): lax.ppermute(chunk, 'beam', [(j, j ^ x) for j in range(n)])]
  transfers between devices with their start and end apart: 15 -> 17, of which waited for: 6 -> 6; matrix products, arithmetic and copies ran while one was open for 0% -> 0% of each run, Pallas kernels for 8% -> 9%
where the time goes in v5:
time: 60.6 us; the launch traced here: 60.4 us
  starting transfers between devices  26.4 us (44%)
  waiting for transfers between devices  23.1 us (38%)
  Pallas kernels  8.48 us (14%)
  local copies, waits for them, and re-layouts  1.01 us (2%)
  between operations  0.8 us (1%)
  other arithmetic  0.63 us (1%)
    ppermute x16, starting transfers between devices, exchange(): lax.ppermute(chunk, 'beam', [(j, j ^ x) for j in range(n)])  26.4 us
    ppermute x16, waiting for transfers between devices, exchange(): lax.ppermute(chunk, 'beam', [(j, j ^ x) for j in range(n)])  23.1 us
    pallas_call x2, Pallas kernels, fast(): pl.pallas_call(functools.partial(pack_kernel, n, part), out_shape=[jax.Sh...  4.33 us
    pallas_call x2, Pallas kernels, finish(): pl.pallas_call(functools.partial(final_kernel, n, part, not before), out_...  2.61 us
  transfers between devices with their start and end apart: 17, of which 6 were waited for; matrix products, arithmetic and copies ran while one was open for 0% of the time, Pallas kernels for 9%

profile of v5, /device:TPU:0, one launch (start us, length us, event | category | flops | bytes accessed | tf_op | source)
XLA Modules:
  0.0 60.4 jit_solution(17168701354555504360)
XLA Ops:
  0.6 0.0 copy-start.4
  0.6 0.0 copy-start.5
  0.6 1.9 %shard_map.95 = bf16[2,272,128]{2,1,0:T(8,128)(2,1)} custom-call(f32[2,128,2048]{2,1,0:T(8,128)} %st_hbm.3, bf16[2,2,2048]{2,1,0:T(2,128)(2,1)} %q.3, bf16[2,2,2048]{2,1,0:T(2,128)(2,1)} %k.7, bf16[2,2,2048]{2,1,0:T(2,128)(2,1)} %v.7, bf16[2,2,2048]{2,1,0:T(2,128)(2,1)} %g.3), custom_call_target="tpu_custom_call" | custom-call | tf_op jit(solution)/shard_map/pallas_call | solution.py:241
  2.5 0.0 copy-start
  2.6 0.0 copy-start.1
  2.6 0.0 copy-start.2
  2.6 4.1 %collective-permute-start = (bf16[2,272,128]{2,1,0:T(8,128)(2,1)}, bf16[2,272,128]{2,1,0:T(8,128)(2,1)S(1)}, u32[]{:S(2)}, u32[]{:S(2)}) collective-permute-start(bf16[2,272,128]{2,1,0:T(8,128)(2,1)} %shard_map.95), channel_id=1, source_target_pairs={{0,8},{2,10},{4,12},{6,14},{8,0},{10,2},{12,4},{14,6},{1,9},{3,11}... | collective-permute-start | bytes 417800 | tf_op jit(solution)/shard_map/ppermute | solution.py:234
  6.7 2.4 %shard_map.96 = (bf16[2,272,128]{2,1,0:T(8,128)(2,1)}, bf16[2,272,128]{2,1,0:T(8,128)(2,1)}, bf16[2,272,128]{2,1,0:T(8,128)(2,1)}, bf16[2,272,128]{2,1,0:T(8,128...) custom-call(f32[2,128,2048]{2,1,0:T(8,128)} %st_hbm.3, ...), custom_call_target="tpu_custom_call" | custom-call | tf_op jit(solution)/shard_map/pallas_call | solution.py:241
  9.1 1.6 %collective-permute-start.1 = (bf16[2,272,128]{2,1,0:T(8,128)(2,1)}, bf16[2,272,128]{2,1,0:T(8,128)(2,1)S(1)}, u32[]{:S(2)}, u32[]{:S(2)}) collective-permute-start(bf16[2,272,128]{2,1,0:T(8,128)(2,1)} %get-tuple-element.22), channel_id=1, source_target_pairs={{0,2},{2,0},{4,6},{6,4},{8,10},{10,8},{12,14},{14,12},{1,3},{3,1},... | collective-permute-start | bytes 417800 | tf_op jit(solution)/shard_map/ppermute | solution.py:234
  10.7 1.6 %collective-permute-start.2 = (bf16[2,272,128]{2,1,0:T(8,128)(2,1)}, bf16[2,272,128]{2,1,0:T(8,128)(2,1)S(1)}, u32[]{:S(2)}, u32[]{:S(2)}) collective-permute-start(bf16[2,272,128]{2,1,0:T(8,128)(2,1)} %get-tuple-element.23), channel_id=1, source_target_pairs={{0,4},{2,6},{4,0},{6,2},{8,12},{10,14},{12,8},{14,10},{1,5},{3,7},... | collective-permute-start | bytes 417800 | tf_op jit(solution)/shard_map/ppermute | solution.py:234
  12.3 0.5 collective-permute-start.3
  12.8 1.4 %collective-permute-start.4 = (bf16[2,272,128]{2,1,0:T(8,128)(2,1)}, bf16[2,272,128]{2,1,0:T(8,128)(2,1)S(1)}, u32[]{:S(2)}, u32[]{:S(2)}) collective-permute-start(bf16[2,272,128]{2,1,0:T(8,128)(2,1)} %get-tuple-element.25), channel_id=1, source_target_pairs={{0,6},{2,4},{4,2},{6,0},{8,14},{10,12},{12,10},{14,8},{1,7},{3,5},... | collective-permute-start | bytes 417800 | tf_op jit(solution)/shard_map/ppermute | solution.py:234
  14.2 0.0 copy-done.4
  14.2 0.0 collective-permute-done.rest_0_
  14.2 3.5 %collective-permute-start.5 = (bf16[2,272,128]{2,1,0:T(8,128)(2,1)}, bf16[2,272,128]{2,1,0:T(8,128)(2,1)S(1)}, u32[]{:S(2)}, u32[]{:S(2)}) collective-permute-start(bf16[2,272,128]{2,1,0:T(8,128)(2,1)} %get-tuple-element.26), channel_id=1, source_target_pairs={{0,12},{2,14},{4,8},{6,10},{8,4},{10,6},{12,0},{14,2},{1,13},{3,15... | collective-permute-start | bytes 417800 | tf_op jit(solution)/shard_map/ppermute | solution.py:234
  17.6 0.0 collective-permute-done.1.rest_1_
  17.6 1.3 %collective-permute-start.6 = (bf16[2,272,128]{2,1,0:T(8,128)(2,1)}, bf16[2,272,128]{2,1,0:T(8,128)(2,1)S(1)}, u32[]{:S(2)}, u32[]{:S(2)}) collective-permute-start(bf16[2,272,128]{2,1,0:T(8,128)(2,1)} %get-tuple-element.27), channel_id=1, source_target_pairs={{0,14},{2,12},{4,10},{6,8},{8,6},{10,4},{12,2},{14,0},{1,15},{3,13... | collective-permute-start | bytes 417800 | tf_op jit(solution)/shard_map/ppermute | solution.py:234
  19.0 0.0 copy-done.5
  19.0 0.0 copy-start.3
  19.0 0.9 %copy-done.3 = bf16[2,272,128]{2,1,0:T(8,128)(2,1)S(1)} copy-done((bf16[2,272,128]{2,1,0:T(8,128)(2,1)S(1)}, bf16[2,272,128]{2,1,0:T(8,128)(2,1)}, u32[]{:S(2)}) %copy-start.3) | copy-done | bytes 139288
  19.9 0.0 collective-permute-done.2.rest_2_
  19.9 8.4 %collective-permute-done.3.rest_3_ = bf16[2,272,128]{2,1,0:T(8,128)(2,1)S(1)} collective-permute-done((bf16[2,272,128]{2,1,0:T(8,128)(2,1)}, bf16[2,272,128]{2,1,0:T(8,128)(2,1)S(1)}, u32[]{:S(2)}, u32[]{:S(2)}) %collective-permute-start.3) | collective-permute-done | bytes 139296 | tf_op jit(solution)/shard_map/ppermute | solution.py:234
  28.3 1.1 %collective-permute-done.4.rest_4_ = bf16[2,272,128]{2,1,0:T(8,128)(2,1)S(1)} collective-permute-done((bf16[2,272,128]{2,1,0:T(8,128)(2,1)}, bf16[2,272,128]{2,1,0:T(8,128)(2,1)S(1)}, u32[]{:S(2)}, u32[]{:S(2)}) %collective-permute-start.4) | collective-permute-done | bytes 139296 | tf_op jit(solution)/shard_map/ppermute | solution.py:234
  29.4 0.0 collective-permute-done.5.rest_5_
  29.5 0.0 collective-permute-done.6.rest_6_
  29.5 0.1 broadcast_in_dim.2.decay
  29.5 1.0 %shard_map.98 = (bf16[592,128]{1,0:T(8,128)(2,1)S(1)}, bf16[528,128]{1,0:T(8,128)(2,1)S(1)}, bf16[528,128]{1,0:T(8,128)(2,1)S(1)}, bf16[528,128]{1,0:T(8,128)(2,...) custom-call(s32[4,16]{1,0:T(4,128)S(1)} %pad_add_fusion.parents_hbm,, ...), custom_call_target="tpu_custom_call" | custom-call | tf_op jit(solution)/shard_map/pallas_call | solution.py:265
  30.5 5.7 %collective-permute-start.7 = (bf16[592,128]{1,0:T(8,128)(2,1)S(1)}, bf16[592,128]{1,0:T(8,128)(2,1)S(1)}, u32[]{:S(2)}, u32[]{:S(2)}) collective-permute-start(bf16[592,128]{1,0:T(8,128)(2,1)S(1)} %get-tuple-element.30), channel_id=1, source_target_pairs={{0,8},{2,10},{4,12},{6,14},{8,0},{10,2},{12,4},{14,6},{1,9},{3,11}... | collective-permute-start | bytes 454664 | tf_op jit(solution)/shard_map/ppermute | solution.py:234
  36.2 0.5 collective-permute-start.8
  36.7 0.0 collective-permute-start.9
  36.7 3.0 %collective-permute-start.10 = (bf16[528,128]{1,0:T(8,128)(2,1)S(1)}, bf16[528,128]{1,0:T(8,128)(2,1)S(1)}, u32[]{:S(2)}, u32[]{:S(2)}) collective-permute-start(bf16[528,128]{1,0:T(8,128)(2,1)S(1)} %get-tuple-element.33), channel_id=1, source_target_pairs={{0,10},{2,8},{4,14},{6,12},{8,2},{10,0},{12,6},{14,4},{1,11},{3,9}... | collective-permute-start | bytes 405512 | tf_op jit(solution)/shard_map/ppermute | solution.py:234
  39.7 0.0 collective-permute-start.11
  39.7 6.1 %collective-permute-done.7.rest_2_.got = bf16[592,128]{1,0:T(8,128)(2,1)S(1)} collective-permute-done((bf16[592,128]{1,0:T(8,128)(2,1)S(1)}, bf16[592,128]{1,0:T(8,128)(2,1)S(1)}, u32[]{:S(2)}, u32[]{:S(2)}) %collective-permute-start.7) | collective-permute-done | bytes 151584 | tf_op jit(solution)/shard_map/ppermute | solution.py:234
  45.8 0.3 collective-permute-start.12
  46.1 0.0 collective-permute-done.8.rest_3_
  46.1 0.0 collective-permute-start.15
  46.1 4.1 %collective-permute-done.12.got.rest_0_ = bf16[128,128]{1,0:T(8,128)(2,1)S(1)} collective-permute-done((bf16[128,128]{1,0:T(8,128)(2,1)S(1)}, bf16[128,128]{1,0:T(8,128)(2,1)S(1)}, u32[]{:S(2)}, u32[]{:S(2)}) %collective-permute-start.12) | collective-permute-done | bytes 32800 | tf_op jit(solution)/shard_map/ppermute | solution.py:234
  50.2 0.9 %collective-permute-start.16 = (bf16[528,128]{1,0:T(8,128)(2,1)S(1)}, bf16[528,128]{1,0:T(8,128)(2,1)S(1)}, u32[]{:S(2)}, u32[]{:S(2)}) collective-permute-start(bf16[528,128]{1,0:T(8,128)(2,1)S(1)} %get-tuple-element.40), channel_id=1, source_target_pairs={{0,14},{2,12},{4,10},{6,8},{8,6},{10,4},{12,2},{14,0},{1,15},{3,13... | collective-permute-start | bytes 405512 | tf_op jit(solution)/shard_map/ppermute | solution.py:234
  51.1 0.0 collective-permute-done.9.rest_4_
  51.1 2.0 %collective-permute-start.13 = (bf16[256,128]{1,0:T(8,128)(2,1)S(1)}, bf16[256,128]{1,0:T(8,128)(2,1)S(1)}, u32[]{:S(2)}, u32[]{:S(2)}) collective-permute-start(bf16[256,128]{1,0:T(8,128)(2,1)S(1)} %shard_map.101), channel_id=1, source_target_pairs={{0,4},{2,6},{4,0},{6,2},{8,12},{10,14},{12,8},{14,10},{1,5},{3,7},... | collective-permute-start | bytes 196616 | tf_op jit(solution)/shard_map/ppermute | solution.py:234
  53.2 0.0 collective-permute-done.10.rest_5_
  53.2 0.0 collective-permute-done.11.rest_6_
  53.2 0.0 copy-done
  53.2 0.0 copy-done.1
  53.2 0.0 copy-done.2
  53.2 1.5 %shard_map.99 = (f32[2,128,2048]{2,1,0:T(8,128)}, f32[32,768]{1,0:T(8,128)S(1)}) custom-call(f32[16,128]{1,0:T(8,128)S(1)} %broadcast_in_dim.2.decay, bf16[2,2,2048]{2,1,0:T(2,128)(2,1)S(1)} %copy-done.1, bf16[2,2,2048]{2,1,0:T(2,128)(2,1)S(1)} %copy-done.2, bf16[2048,768]{1,0:T(8,128)(2,1)S(1)} %copy-done, ...), custom_call_target="tpu_custom_call" | custom-call | tf_op jit(solution)/shard_map/pallas_call | solution.py:304
  54.7 2.7 %collective-permute-done.13.rest_1_ = bf16[256,128]{1,0:T(8,128)(2,1)S(1)} collective-permute-done((bf16[256,128]{1,0:T(8,128)(2,1)S(1)}, bf16[256,128]{1,0:T(8,128)(2,1)S(1)}, u32[]{:S(2)}, u32[]{:S(2)}) %collective-permute-start.13) | collective-permute-done | bytes 65568 | tf_op jit(solution)/shard_map/ppermute | solution.py:234
  57.4 0.5 shard_map.102
  57.9 0.1 collective-permute-start.14
  58.0 0.0 collective-permute-done.15.rest_0_
  58.0 0.7 %collective-permute-done.16.rest_1_ = bf16[528,128]{1,0:T(8,128)(2,1)S(1)} collective-permute-done((bf16[528,128]{1,0:T(8,128)(2,1)S(1)}, bf16[528,128]{1,0:T(8,128)(2,1)S(1)}, u32[]{:S(2)}, u32[]{:S(2)}) %collective-permute-start.16) | collective-permute-done | bytes 135200 | tf_op jit(solution)/shard_map/ppermute | solution.py:234
  58.7 1.1 %shard_map.103 = f32[2,128,2048]{2,1,0:T(8,128)} custom-call(f32[16,128]{1,0:T(8,128)S(1)} %broadcast_in_dim.2.decay, bf16[2,2,2048]{2,1,0:T(2,128)(2,1)S(1)} %copy-done.1, bf16[2,2,2048]{2,1,0:T(2,128)(2,1)S(1)} %copy-done.2, bf16[528,128]{1,0:T(8,128)(2,1)S(1)} %collective-permute-done.15.rest_0_, ...), custom_call_target="tpu_custom_call", output_to_operand_aliasing={{}: (5, {})} | custom-call | tf_op jit(solution)/shard_map/pallas_call | solution.py:304
  59.8 0.0 collective-permute-done.14
  59.8 0.6 %add_convert_fusion = bf16[2,8,768]{2,1,0:T(8,128)(2,1)} fusion(f32[2,8,768]{2,1,0:T(8,128)S(1)} %get-tuple-element.37, f32[2,8,768]{2,1,0:T(8,128)S(1)} %collective-permute-done.14), kind=kLoop, calls=%fused_computation | loop fusion | flops 24576 | bytes 122880 | tf_op jit(solution)/shard_map/convert_element_type | solution.py:330
  (6 shorter events, 0.0 us)
Async XLA Ops:
  0.6 13.5 %copy-start.4 = (s32[2,16]{1,0:T(2,128)S(1)}, s32[2,16]{1,0:T(2,128)}, u32[]{:S(2)}) copy-start(s32[2,16]{1,0:T(2,128)} %param.14) | copy-start | bytes 388
  0.6 18.3 %copy-start.5 = (f32[16]{0:T(128)S(1)}, f32[16]{0:T(128)}, u32[]{:S(2)}) copy-start(f32[16]{0:T(128)} %param.9) | copy-start | bytes 196
  2.5 50.6 %copy-start = (bf16[2048,768]{1,0:T(8,128)(2,1)S(1)}, bf16[2048,768]{1,0:T(8,128)(2,1)}, u32[]{:S(2)}) copy-start(bf16[2048,768]{1,0:T(8,128)(2,1)} %weight.1) | copy-start | bytes 9437188
  2.6 50.6 %copy-start.1 = (bf16[2,2,2048]{2,1,0:T(2,128)(2,1)S(1)}, bf16[2,2,2048]{2,1,0:T(2,128)(2,1)}, u32[]{:S(2)}) copy-start(bf16[2,2,2048]{2,1,0:T(2,128)(2,1)} %k.7) | copy-start | bytes 49156
  2.6 50.6 %copy-start.2 = (bf16[2,2,2048]{2,1,0:T(2,128)(2,1)S(1)}, bf16[2,2,2048]{2,1,0:T(2,128)(2,1)}, u32[]{:S(2)}) copy-start(bf16[2,2,2048]{2,1,0:T(2,128)(2,1)} %v.7) | copy-start | bytes 49156
  2.6 11.6 %collective-permute-start = (bf16[2,272,128]{2,1,0:T(8,128)(2,1)}, bf16[2,272,128]{2,1,0:T(8,128)(2,1)S(1)}, u32[]{:S(2)}, u32[]{:S(2)}) collective-permute-start(bf16[2,272,128]{2,1,0:T(8,128)(2,1)} %shard_map.95), channel_id=1, source_target_pairs={{0,8},{2,10},{4,12},{6,14},{8,0},{10,2},{12,4},{14,6},{1,9},{3,11}... | collective-permute-start | bytes 417800 | tf_op jit(solution)/shard_map/ppermute | solution.py:234
  9.1 8.5 %collective-permute-start.1 = (bf16[2,272,128]{2,1,0:T(8,128)(2,1)}, bf16[2,272,128]{2,1,0:T(8,128)(2,1)S(1)}, u32[]{:S(2)}, u32[]{:S(2)}) collective-permute-start(bf16[2,272,128]{2,1,0:T(8,128)(2,1)} %get-tuple-element.22), channel_id=1, source_target_pairs={{0,2},{2,0},{4,6},{6,4},{8,10},{10,8},{12,14},{14,12},{1,3},{3,1},... | collective-permute-start | bytes 417800 | tf_op jit(solution)/shard_map/ppermute | solution.py:234
  10.7 9.2 %collective-permute-start.2 = (bf16[2,272,128]{2,1,0:T(8,128)(2,1)}, bf16[2,272,128]{2,1,0:T(8,128)(2,1)S(1)}, u32[]{:S(2)}, u32[]{:S(2)}) collective-permute-start(bf16[2,272,128]{2,1,0:T(8,128)(2,1)} %get-tuple-element.23), channel_id=1, source_target_pairs={{0,4},{2,6},{4,0},{6,2},{8,12},{10,14},{12,8},{14,10},{1,5},{3,7},... | collective-permute-start | bytes 417800 | tf_op jit(solution)/shard_map/ppermute | solution.py:234
  12.3 16.1 %collective-permute-start.3 = (bf16[2,272,128]{2,1,0:T(8,128)(2,1)}, bf16[2,272,128]{2,1,0:T(8,128)(2,1)S(1)}, u32[]{:S(2)}, u32[]{:S(2)}) collective-permute-start(bf16[2,272,128]{2,1,0:T(8,128)(2,1)} %get-tuple-element.24), channel_id=1, source_target_pairs={{0,10},{2,8},{4,14},{6,12},{8,2},{10,0},{12,6},{14,4},{1,11},{3,9}... | collective-permute-start | bytes 417800 | tf_op jit(solution)/shard_map/ppermute | solution.py:234
  12.8 16.7 %collective-permute-start.4 = (bf16[2,272,128]{2,1,0:T(8,128)(2,1)}, bf16[2,272,128]{2,1,0:T(8,128)(2,1)S(1)}, u32[]{:S(2)}, u32[]{:S(2)}) collective-permute-start(bf16[2,272,128]{2,1,0:T(8,128)(2,1)} %get-tuple-element.25), channel_id=1, source_target_pairs={{0,6},{2,4},{4,2},{6,0},{8,14},{10,12},{12,10},{14,8},{1,7},{3,5},... | collective-permute-start | bytes 417800 | tf_op jit(solution)/shard_map/ppermute | solution.py:234
  14.2 15.3 %collective-permute-start.5 = (bf16[2,272,128]{2,1,0:T(8,128)(2,1)}, bf16[2,272,128]{2,1,0:T(8,128)(2,1)S(1)}, u32[]{:S(2)}, u32[]{:S(2)}) collective-permute-start(bf16[2,272,128]{2,1,0:T(8,128)(2,1)} %get-tuple-element.26), channel_id=1, source_target_pairs={{0,12},{2,14},{4,8},{6,10},{8,4},{10,6},{12,0},{14,2},{1,13},{3,15... | collective-permute-start | bytes 417800 | tf_op jit(solution)/shard_map/ppermute | solution.py:234
  17.6 11.8 %collective-permute-start.6 = (bf16[2,272,128]{2,1,0:T(8,128)(2,1)}, bf16[2,272,128]{2,1,0:T(8,128)(2,1)S(1)}, u32[]{:S(2)}, u32[]{:S(2)}) collective-permute-start(bf16[2,272,128]{2,1,0:T(8,128)(2,1)} %get-tuple-element.27), channel_id=1, source_target_pairs={{0,14},{2,12},{4,10},{6,8},{8,6},{10,4},{12,2},{14,0},{1,15},{3,13... | collective-permute-start | bytes 417800 | tf_op jit(solution)/shard_map/ppermute | solution.py:234
  19.0 0.9 %copy-start.3 = (bf16[2,272,128]{2,1,0:T(8,128)(2,1)S(1)}, bf16[2,272,128]{2,1,0:T(8,128)(2,1)}, u32[]{:S(2)}) copy-start(bf16[2,272,128]{2,1,0:T(8,128)(2,1)} %get-tuple-element.28.chunk) | copy-start | bytes 417796
  30.5 15.3 %collective-permute-start.7 = (bf16[592,128]{1,0:T(8,128)(2,1)S(1)}, bf16[592,128]{1,0:T(8,128)(2,1)S(1)}, u32[]{:S(2)}, u32[]{:S(2)}) collective-permute-start(bf16[592,128]{1,0:T(8,128)(2,1)S(1)} %get-tuple-element.30), channel_id=1, source_target_pairs={{0,8},{2,10},{4,12},{6,14},{8,0},{10,2},{12,4},{14,6},{1,9},{3,11}... | collective-permute-start | bytes 454664 | tf_op jit(solution)/shard_map/ppermute | solution.py:234
  36.2 9.9 %collective-permute-start.8 = (bf16[528,128]{1,0:T(8,128)(2,1)S(1)}, bf16[528,128]{1,0:T(8,128)(2,1)S(1)}, u32[]{:S(2)}, u32[]{:S(2)}) collective-permute-start(bf16[528,128]{1,0:T(8,128)(2,1)S(1)} %get-tuple-element.31), channel_id=1, source_target_pairs={{0,2},{2,0},{4,6},{6,4},{8,10},{10,8},{12,14},{14,12},{1,3},{3,1},... | collective-permute-start | bytes 405512 | tf_op jit(solution)/shard_map/ppermute | solution.py:234
  36.7 14.4 %collective-permute-start.9 = (bf16[528,128]{1,0:T(8,128)(2,1)S(1)}, bf16[528,128]{1,0:T(8,128)(2,1)S(1)}, u32[]{:S(2)}, u32[]{:S(2)}) collective-permute-start(bf16[528,128]{1,0:T(8,128)(2,1)S(1)} %get-tuple-element.32), channel_id=1, source_target_pairs={{0,4},{2,6},{4,0},{6,2},{8,12},{10,14},{12,8},{14,10},{1,5},{3,7},... | collective-permute-start | bytes 405512 | tf_op jit(solution)/shard_map/ppermute | solution.py:234
  36.7 16.4 %collective-permute-start.10 = (bf16[528,128]{1,0:T(8,128)(2,1)S(1)}, bf16[528,128]{1,0:T(8,128)(2,1)S(1)}, u32[]{:S(2)}, u32[]{:S(2)}) collective-permute-start(bf16[528,128]{1,0:T(8,128)(2,1)S(1)} %get-tuple-element.33), channel_id=1, source_target_pairs={{0,10},{2,8},{4,14},{6,12},{8,2},{10,0},{12,6},{14,4},{1,11},{3,9}... | collective-permute-start | bytes 405512 | tf_op jit(solution)/shard_map/ppermute | solution.py:234
  39.7 13.4 %collective-permute-start.11 = (bf16[528,128]{1,0:T(8,128)(2,1)S(1)}, bf16[528,128]{1,0:T(8,128)(2,1)S(1)}, u32[]{:S(2)}, u32[]{:S(2)}) collective-permute-start(bf16[528,128]{1,0:T(8,128)(2,1)S(1)} %get-tuple-element.34), channel_id=1, source_target_pairs={{0,6},{2,4},{4,2},{6,0},{8,14},{10,12},{12,10},{14,8},{1,7},{3,5},... | collective-permute-start | bytes 405512 | tf_op jit(solution)/shard_map/ppermute | solution.py:234
  45.8 4.4 %collective-permute-start.12 = (bf16[128,128]{1,0:T(8,128)(2,1)S(1)}, bf16[128,128]{1,0:T(8,128)(2,1)S(1)}, u32[]{:S(2)}, u32[]{:S(2)}) collective-permute-start(bf16[128,128]{1,0:T(8,128)(2,1)S(1)} %shard_map.100.have), channel_id=1, source_target_pairs={{0,2},{2,0},{4,6},{6,4},{8,10},{10,8},{12,14},{14,12},{1,3},{3,1},... | collective-permute-start | bytes 98312 | tf_op jit(solution)/shard_map/ppermute | solution.py:234
  46.1 11.9 %collective-permute-start.15 = (bf16[528,128]{1,0:T(8,128)(2,1)S(1)}, bf16[528,128]{1,0:T(8,128)(2,1)S(1)}, u32[]{:S(2)}, u32[]{:S(2)}) collective-permute-start(bf16[528,128]{1,0:T(8,128)(2,1)S(1)} %get-tuple-element.39), channel_id=1, source_target_pairs={{0,12},{2,14},{4,8},{6,10},{8,4},{10,6},{12,0},{14,2},{1,13},{3,15... | collective-permute-start | bytes 405512 | tf_op jit(solution)/shard_map/ppermute | solution.py:234
  50.2 8.4 %collective-permute-start.16 = (bf16[528,128]{1,0:T(8,128)(2,1)S(1)}, bf16[528,128]{1,0:T(8,128)(2,1)S(1)}, u32[]{:S(2)}, u32[]{:S(2)}) collective-permute-start(bf16[528,128]{1,0:T(8,128)(2,1)S(1)} %get-tuple-element.40), channel_id=1, source_target_pairs={{0,14},{2,12},{4,10},{6,8},{8,6},{10,4},{12,2},{14,0},{1,15},{3,13... | collective-permute-start | bytes 405512 | tf_op jit(solution)/shard_map/ppermute | solution.py:234
  51.1 6.3 %collective-permute-start.13 = (bf16[256,128]{1,0:T(8,128)(2,1)S(1)}, bf16[256,128]{1,0:T(8,128)(2,1)S(1)}, u32[]{:S(2)}, u32[]{:S(2)}) collective-permute-start(bf16[256,128]{1,0:T(8,128)(2,1)S(1)} %shard_map.101), channel_id=1, source_target_pairs={{0,4},{2,6},{4,0},{6,2},{8,12},{10,14},{12,8},{14,10},{1,5},{3,7},... | collective-permute-start | bytes 196616 | tf_op jit(solution)/shard_map/ppermute | solution.py:234
  57.9 1.9 %collective-permute-start.14 = (f32[2,8,768]{2,1,0:T(8,128)S(1)}, f32[2,8,768]{2,1,0:T(8,128)S(1)}, u32[]{:S(2)}, u32[]{:S(2)}) collective-permute-start(f32[2,8,768]{2,1,0:T(8,128)S(1)} %get-tuple-element.38), channel_id=1, source_target_pairs={{0,1},{1,0},{2,3},{3,2},{4,5},{5,4},{6,7},{7,6},{8,9},{9,8},{10,11... | collective-permute-start | bytes 147464 | tf_op jit(solution)/shard_map/ppermute | solution.py:329

commit v6 on v5

--- a/solution.py
+++ b/solution.py
@@ -183,7 +183,14 @@
 def final_kernel(n, order, first, decay, k, v, *rest):
     if first:
         weight, attn, *rest = rest
-    ins, (result, *terms, out, ks, vs, sem) = dict(zip(order, rest)), rest[-5 - first :]
+    ins, (result, *more, out, ks, vs, total, sem) = dict(zip(order, rest)), rest[-7:]
+    if first:
+        terms = more
+    else:
+        keep, other = rest[len(order) + 1 : len(order) + 3]
+        total[...] = (keep[...] + other[...]).astype(BF16)
+        projected = pltpu.make_async_copy(total, more[0], sem.at[n])
+        projected.start()
     slots, dim, columns = result.shape
     if first:
         across = ins[n // 2]
@@ -213,20 +220,22 @@
                 outer = lax.dot_general(
                     lhs.astype(BF16), rhs.astype(BF16), (((0,), (0,)), ((), ())), preferred_element_type=F32
                 )
-                first = j * depth + i * dim
-                out[j, :, at] = (d * d) * ins[x][first : first + dim, :].astype(F32) + outer
+                begin = j * depth + i * dim
+                out[j, :, at] = (d * d) * ins[x][begin : begin + dim, :].astype(F32) + outer
         at = pl.ds(pl.multiple_of((me ^ x) * depth, depth), depth)
         copies.append(pltpu.make_async_copy(out.at[:, :, at], result.at[:, :, at], sem.at[x]))
         copies[-1].start()
     for c in copies:
         c.wait()
+    if not first:
+        projected.wait()
 
 
 def fast(n, head_count, states, decay_rates, queries, key_vectors, values, gate_logits, parents, out_weight):
     slots, dim, columns = states.shape
     heads = columns // dim // n
     total, depth = n * slots, heads * dim
-    first, second = [4, 1, 2, 5, 3, 6, 7, 0], [4, 1, 2, 5, 3, 6, 7, 0]
+    first, second = [4, 1, 2, 3, 5, 6, 7, 0], [4, 1, 2, 5, 3, 6, 7, 0]
     decay = jnp.broadcast_to(jnp.exp(-decay_rates)[:, None], (columns // dim, dim))
 
     def exchange(order, chunks):
@@ -298,20 +307,22 @@
         hop *= 2
 
     whole = jax.ShapeDtypeStruct(states.shape, F32)
+    summed = jax.ShapeDtypeStruct((STEPS, total // head_count, out_weight.shape[1]), BF16)
 
     def finish(part, *before):
         more = [] if before else [out_weight, attn]
         return pl.pallas_call(
             functools.partial(final_kernel, n, part, not before),
-            out_shape=[whole] if before else [whole, jax.ShapeDtypeStruct((STEPS * total, out_weight.shape[1]), F32)],
-            in_specs=[VMEM] * (len(more) + len(part) + 3) + [ANY] * len(before),
-            out_specs=[ANY] if before else [ANY, VMEM],
+            out_shape=[whole, summed if before else jax.ShapeDtypeStruct((STEPS * total, out_weight.shape[1]), F32)],
+            in_specs=[VMEM] * (len(more) + len(part) + 3) + ([ANY, VMEM, VMEM] if before else []),
+            out_specs=[ANY, ANY if before else VMEM],
             input_output_aliases={len(part) + 3: 0} if before else {},
             scratch_shapes=[
                 pltpu.VMEM(states.shape, F32),
                 pltpu.VMEM((slots, columns), F32),
                 pltpu.VMEM((slots, columns), F32),
-                pltpu.SemaphoreType.DMA((n,)),
+                pltpu.VMEM(summed.shape, BF16),
+                pltpu.SemaphoreType.DMA((n + 1,)),
             ],
             compiler_params=params(),
         )(decay, key_vectors, values, *more, *[held[x] for x in part], *before)
@@ -327,8 +338,7 @@
         compiler_params=params(),
     )(out_weight, partial, *relayed.values())
     other = lax.ppermute(send, "head", [(0, 1), (1, 0)])
-    projected = (keep + other).astype(BF16)
-    (final,) = finish(second[5:-1], begun)
+    final, projected = finish(second[5:-1], begun, keep, other)
     return projected, final
 
 

time: 60.6 us -> 60 us (0.990)
  starting transfers between devices: 26.4 us -> 29.2 us
  waiting for transfers between devices: 23.1 us -> 20.3 us
  other arithmetic: 0.63 us -> 0.02 us
    ppermute x16, waiting for transfers between devices: 23.1 us -> 19.1 us  [exchange(): lax.ppermute(chunk, 'beam', [(j, j ^ x) for j in range(n)])]
    ppermute x16, starting transfers between devices: 26.4 us -> 29.1 us  [exchange(): lax.ppermute(chunk, 'beam', [(j, j ^ x) for j in range(n)])]
    ppermute x1, waiting for transfers between devices: 0.01 us -> 1.2 us  [fast(): other = lax.ppermute(send, 'head', [(0, 1), (1, 0)])]
    convert_element_type x1 -> x0, other arithmetic: 0.62 us -> none  [fast(): projected = (keep + other).astype(BF16)]
  transfers between devices with their start and end apart: 17 -> 17, of which waited for: 6 -> 7; matrix products, arithmetic and copies ran while one was open for 0% -> 0% of each run, Pallas kernels for 9% -> 8%
where the time goes in v6:
time: 60 us; the launch traced here: 59.8 us
  starting transfers between devices  29.2 us (49%)
  waiting for transfers between devices  20.3 us (34%)
  Pallas kernels  8.54 us (14%)
  local copies, waits for them, and re-layouts  1.01 us (2%)
  between operations  0.79 us (1%)
    ppermute x16, starting transfers between devices, exchange(): lax.ppermute(chunk, 'beam', [(j, j ^ x) for j in range(n)])  29.1 us
    ppermute x16, waiting for transfers between devices, exchange(): lax.ppermute(chunk, 'beam', [(j, j ^ x) for j in range(n)])  19.1 us
    pallas_call x2, Pallas kernels, fast(): pl.pallas_call(functools.partial(pack_kernel, n, part), out_shape=[jax.Sh...  4.37 us
    pallas_call x2, Pallas kernels, finish(): pl.pallas_call(functools.partial(final_kernel, n, part, not before), out_...  2.63 us
  transfers between devices with their start and end apart: 17, of which 7 were waited for; matrix products, arithmetic and copies ran while one was open for 0% of the time, Pallas kernels for 8%

profile of v6, /device:TPU:0, one launch (start us, length us, event | category | flops | bytes accessed | tf_op | source)
XLA Modules:
  0.0 59.8 jit_solution(13543342462871622540)
XLA Ops:
  0.6 0.0 copy-start.4
  0.6 0.0 copy-start.5
  0.6 1.9 %shard_map.95 = bf16[2,272,128]{2,1,0:T(8,128)(2,1)} custom-call(f32[2,128,2048]{2,1,0:T(8,128)} %st_hbm.3, bf16[2,2,2048]{2,1,0:T(2,128)(2,1)} %q.3, bf16[2,2,2048]{2,1,0:T(2,128)(2,1)} %k.7, bf16[2,2,2048]{2,1,0:T(2,128)(2,1)} %v.7, bf16[2,2,2048]{2,1,0:T(2,128)(2,1)} %g.3), custom_call_target="tpu_custom_call" | custom-call | tf_op jit(solution)/shard_map/pallas_call | solution.py:250
  2.5 0.0 copy-start
  2.6 0.0 copy-start.1
  2.6 0.0 copy-start.2
  2.6 4.1 %collective-permute-start = (bf16[2,272,128]{2,1,0:T(8,128)(2,1)}, bf16[2,272,128]{2,1,0:T(8,128)(2,1)S(1)}, u32[]{:S(2)}, u32[]{:S(2)}) collective-permute-start(bf16[2,272,128]{2,1,0:T(8,128)(2,1)} %shard_map.95), channel_id=1, source_target_pairs={{0,8},{2,10},{4,12},{6,14},{8,0},{10,2},{12,4},{14,6},{1,9},{3,11}... | collective-permute-start | bytes 417800 | tf_op jit(solution)/shard_map/ppermute | solution.py:243
  6.7 2.5 %shard_map.96 = (bf16[2,272,128]{2,1,0:T(8,128)(2,1)}, bf16[2,272,128]{2,1,0:T(8,128)(2,1)}, bf16[2,272,128]{2,1,0:T(8,128)(2,1)}, bf16[2,272,128]{2,1,0:T(8,128...) custom-call(f32[2,128,2048]{2,1,0:T(8,128)} %st_hbm.3, ...), custom_call_target="tpu_custom_call" | custom-call | tf_op jit(solution)/shard_map/pallas_call | solution.py:250
  9.2 1.6 %collective-permute-start.1 = (bf16[2,272,128]{2,1,0:T(8,128)(2,1)}, bf16[2,272,128]{2,1,0:T(8,128)(2,1)S(1)}, u32[]{:S(2)}, u32[]{:S(2)}) collective-permute-start(bf16[2,272,128]{2,1,0:T(8,128)(2,1)} %get-tuple-element.24), channel_id=1, source_target_pairs={{0,2},{2,0},{4,6},{6,4},{8,10},{10,8},{12,14},{14,12},{1,3},{3,1},... | collective-permute-start | bytes 417800 | tf_op jit(solution)/shard_map/ppermute | solution.py:243
  10.7 1.6 %collective-permute-start.2 = (bf16[2,272,128]{2,1,0:T(8,128)(2,1)}, bf16[2,272,128]{2,1,0:T(8,128)(2,1)S(1)}, u32[]{:S(2)}, u32[]{:S(2)}) collective-permute-start(bf16[2,272,128]{2,1,0:T(8,128)(2,1)} %get-tuple-element.25), channel_id=1, source_target_pairs={{0,4},{2,6},{4,0},{6,2},{8,12},{10,14},{12,8},{14,10},{1,5},{3,7},... | collective-permute-start | bytes 417800 | tf_op jit(solution)/shard_map/ppermute | solution.py:243
  12.3 0.4 collective-permute-start.3
  12.7 1.5 %collective-permute-start.4 = (bf16[2,272,128]{2,1,0:T(8,128)(2,1)}, bf16[2,272,128]{2,1,0:T(8,128)(2,1)S(1)}, u32[]{:S(2)}, u32[]{:S(2)}) collective-permute-start(bf16[2,272,128]{2,1,0:T(8,128)(2,1)} %get-tuple-element.27), channel_id=1, source_target_pairs={{0,10},{2,8},{4,14},{6,12},{8,2},{10,0},{12,6},{14,4},{1,11},{3,9}... | collective-permute-start | bytes 417800 | tf_op jit(solution)/shard_map/ppermute | solution.py:243
  14.2 0.0 copy-done.4
  14.2 0.0 collective-permute-done.rest_0_
  14.2 3.5 %collective-permute-start.5 = (bf16[2,272,128]{2,1,0:T(8,128)(2,1)}, bf16[2,272,128]{2,1,0:T(8,128)(2,1)S(1)}, u32[]{:S(2)}, u32[]{:S(2)}) collective-permute-start(bf16[2,272,128]{2,1,0:T(8,128)(2,1)} %get-tuple-element.28), channel_id=1, source_target_pairs={{0,12},{2,14},{4,8},{6,10},{8,4},{10,6},{12,0},{14,2},{1,13},{3,15... | collective-permute-start | bytes 417800 | tf_op jit(solution)/shard_map/ppermute | solution.py:243
  17.7 0.0 collective-permute-done.1.rest_1_
  17.7 0.8 %collective-permute-start.6 = (bf16[2,272,128]{2,1,0:T(8,128)(2,1)}, bf16[2,272,128]{2,1,0:T(8,128)(2,1)S(1)}, u32[]{:S(2)}, u32[]{:S(2)}) collective-permute-start(bf16[2,272,128]{2,1,0:T(8,128)(2,1)} %get-tuple-element.29), channel_id=1, source_target_pairs={{0,14},{2,12},{4,10},{6,8},{8,6},{10,4},{12,2},{14,0},{1,15},{3,13... | collective-permute-start | bytes 417800 | tf_op jit(solution)/shard_map/ppermute | solution.py:243
  18.5 0.0 copy-done.5
  18.5 0.0 copy-start.3
  18.5 0.9 %copy-done.3 = bf16[2,272,128]{2,1,0:T(8,128)(2,1)S(1)} copy-done((bf16[2,272,128]{2,1,0:T(8,128)(2,1)S(1)}, bf16[2,272,128]{2,1,0:T(8,128)(2,1)}, u32[]{:S(2)}) %copy-start.3) | copy-done | bytes 139288
  19.4 0.0 collective-permute-done.2.rest_2_
  19.4 9.6 %collective-permute-done.3.rest_3_ = bf16[2,272,128]{2,1,0:T(8,128)(2,1)S(1)} collective-permute-done((bf16[2,272,128]{2,1,0:T(8,128)(2,1)}, bf16[2,272,128]{2,1,0:T(8,128)(2,1)S(1)}, u32[]{:S(2)}, u32[]{:S(2)}) %collective-permute-start.3) | collective-permute-done | bytes 139296 | tf_op jit(solution)/shard_map/ppermute | solution.py:243
  29.1 0.8 %collective-permute-done.4.rest_4_ = bf16[2,272,128]{2,1,0:T(8,128)(2,1)S(1)} collective-permute-done((bf16[2,272,128]{2,1,0:T(8,128)(2,1)}, bf16[2,272,128]{2,1,0:T(8,128)(2,1)S(1)}, u32[]{:S(2)}, u32[]{:S(2)}) %collective-permute-start.4) | collective-permute-done | bytes 139296 | tf_op jit(solution)/shard_map/ppermute | solution.py:243
  29.8 0.0 collective-permute-done.5.rest_5_
  29.8 0.0 collective-permute-done.6.rest_6_
  29.8 0.1 broadcast_in_dim.2.decay
  29.9 1.0 %shard_map.98 = (bf16[592,128]{1,0:T(8,128)(2,1)S(1)}, bf16[528,128]{1,0:T(8,128)(2,1)S(1)}, bf16[528,128]{1,0:T(8,128)(2,1)S(1)}, bf16[528,128]{1,0:T(8,128)(2,...) custom-call(s32[4,16]{1,0:T(4,128)S(1)} %pad_add_fusion.parents_hbm,, ...), custom_call_target="tpu_custom_call" | custom-call | tf_op jit(solution)/shard_map/pallas_call | solution.py:274
  30.9 5.3 %collective-permute-start.9 = (bf16[592,128]{1,0:T(8,128)(2,1)S(1)}, bf16[592,128]{1,0:T(8,128)(2,1)S(1)}, u32[]{:S(2)}, u32[]{:S(2)}) collective-permute-start(bf16[592,128]{1,0:T(8,128)(2,1)S(1)} %get-tuple-element.34), channel_id=1, source_target_pairs={{0,8},{2,10},{4,12},{6,14},{8,0},{10,2},{12,4},{14,6},{1,9},{3,11}... | collective-permute-start | bytes 454664 | tf_op jit(solution)/shard_map/ppermute | solution.py:243
  36.2 1.0 %collective-permute-start.10 = (bf16[528,128]{1,0:T(8,128)(2,1)S(1)}, bf16[528,128]{1,0:T(8,128)(2,1)S(1)}, u32[]{:S(2)}, u32[]{:S(2)}) collective-permute-start(bf16[528,128]{1,0:T(8,128)(2,1)S(1)} %get-tuple-element.35), channel_id=1, source_target_pairs={{0,2},{2,0},{4,6},{6,4},{8,10},{10,8},{12,14},{14,12},{1,3},{3,1},... | collective-permute-start | bytes 405512 | tf_op jit(solution)/shard_map/ppermute | solution.py:243
  37.2 0.1 collective-permute-start.11
  37.3 2.9 %collective-permute-start.12 = (bf16[528,128]{1,0:T(8,128)(2,1)S(1)}, bf16[528,128]{1,0:T(8,128)(2,1)S(1)}, u32[]{:S(2)}, u32[]{:S(2)}) collective-permute-start(bf16[528,128]{1,0:T(8,128)(2,1)S(1)} %get-tuple-element.37), channel_id=1, source_target_pairs={{0,10},{2,8},{4,14},{6,12},{8,2},{10,0},{12,6},{14,4},{1,11},{3,9}... | collective-permute-start | bytes 405512 | tf_op jit(solution)/shard_map/ppermute | solution.py:243
  40.1 0.9 %collective-permute-start.13 = (bf16[528,128]{1,0:T(8,128)(2,1)S(1)}, bf16[528,128]{1,0:T(8,128)(2,1)S(1)}, u32[]{:S(2)}, u32[]{:S(2)}) collective-permute-start(bf16[528,128]{1,0:T(8,128)(2,1)S(1)} %get-tuple-element.38), channel_id=1, source_target_pairs={{0,6},{2,4},{4,2},{6,0},{8,14},{10,12},{12,10},{14,8},{1,7},{3,5},... | collective-permute-start | bytes 405512 | tf_op jit(solution)/shard_map/ppermute | solution.py:243
  41.0 3.6 %collective-permute-done.9.rest_2_.got = bf16[592,128]{1,0:T(8,128)(2,1)S(1)} collective-permute-done((bf16[592,128]{1,0:T(8,128)(2,1)S(1)}, bf16[592,128]{1,0:T(8,128)(2,1)S(1)}, u32[]{:S(2)}, u32[]{:S(2)}) %collective-permute-start.9) | collective-permute-done | bytes 151584 | tf_op jit(solution)/shard_map/ppermute | solution.py:243
  44.6 1.5 %collective-permute-start.14 = (bf16[128,128]{1,0:T(8,128)(2,1)S(1)}, bf16[128,128]{1,0:T(8,128)(2,1)S(1)}, u32[]{:S(2)}, u32[]{:S(2)}) collective-permute-start(bf16[128,128]{1,0:T(8,128)(2,1)S(1)} %shard_map.100.have), channel_id=1, source_target_pairs={{0,2},{2,0},{4,6},{6,4},{8,10},{10,8},{12,14},{14,12},{1,3},{3,1},... | collective-permute-start | bytes 98312 | tf_op jit(solution)/shard_map/ppermute | solution.py:243
  46.1 0.0 collective-permute-done.10.rest_3_
  46.1 1.5 %collective-permute-start.7 = (bf16[528,128]{1,0:T(8,128)(2,1)S(1)}, bf16[528,128]{1,0:T(8,128)(2,1)S(1)}, u32[]{:S(2)}, u32[]{:S(2)}) collective-permute-start(bf16[528,128]{1,0:T(8,128)(2,1)S(1)} %get-tuple-element.31), channel_id=1, source_target_pairs={{0,12},{2,14},{4,8},{6,10},{8,4},{10,6},{12,0},{14,2},{1,13},{3,15... | collective-permute-start | bytes 405512 | tf_op jit(solution)/shard_map/ppermute | solution.py:243
  47.6 1.0 %collective-permute-done.14.got.rest_0_ = bf16[128,128]{1,0:T(8,128)(2,1)S(1)} collective-permute-done((bf16[128,128]{1,0:T(8,128)(2,1)S(1)}, bf16[128,128]{1,0:T(8,128)(2,1)S(1)}, u32[]{:S(2)}, u32[]{:S(2)}) %collective-permute-start.14) | collective-permute-done | bytes 32800 | tf_op jit(solution)/shard_map/ppermute | solution.py:243
  48.6 2.5 %collective-permute-start.8 = (bf16[528,128]{1,0:T(8,128)(2,1)S(1)}, bf16[528,128]{1,0:T(8,128)(2,1)S(1)}, u32[]{:S(2)}, u32[]{:S(2)}) collective-permute-start(bf16[528,128]{1,0:T(8,128)(2,1)S(1)} %get-tuple-element.32), channel_id=1, source_target_pairs={{0,14},{2,12},{4,10},{6,8},{8,6},{10,4},{12,2},{14,0},{1,15},{3,13... | collective-permute-start | bytes 405512 | tf_op jit(solution)/shard_map/ppermute | solution.py:243
  51.1 0.0 collective-permute-done.11.rest_4_
  51.1 0.1 collective-permute-start.15
  51.2 1.7 %collective-permute-done.12.rest_5_ = bf16[528,128]{1,0:T(8,128)(2,1)S(1)} collective-permute-done((bf16[528,128]{1,0:T(8,128)(2,1)S(1)}, bf16[528,128]{1,0:T(8,128)(2,1)S(1)}, u32[]{:S(2)}, u32[]{:S(2)}) %collective-permute-start.12) | collective-permute-done | bytes 135200 | tf_op jit(solution)/shard_map/ppermute | solution.py:243
  52.9 0.0 collective-permute-done.13.rest_6_
  52.9 0.0 copy-done
  52.9 0.0 copy-done.1
  52.9 0.0 copy-done.2
  52.9 1.5 %shard_map.99 = (f32[2,128,2048]{2,1,0:T(8,128)}, f32[32,768]{1,0:T(8,128)S(1)}) custom-call(f32[16,128]{1,0:T(8,128)S(1)} %broadcast_in_dim.2.decay, bf16[2,2,2048]{2,1,0:T(2,128)(2,1)S(1)} %copy-done.1, bf16[2,2,2048]{2,1,0:T(2,128)(2,1)S(1)} %copy-done.2, bf16[2048,768]{1,0:T(8,128)(2,1)S(1)} %copy-done, ...), custom_call_target="tpu_custom_call" | custom-call | tf_op jit(solution)/shard_map/pallas_call | solution.py:314
  54.5 2.4 %collective-permute-done.15.rest_1_ = bf16[256,128]{1,0:T(8,128)(2,1)S(1)} collective-permute-done((bf16[256,128]{1,0:T(8,128)(2,1)S(1)}, bf16[256,128]{1,0:T(8,128)(2,1)S(1)}, u32[]{:S(2)}, u32[]{:S(2)}) %collective-permute-start.15) | collective-permute-done | bytes 65568 | tf_op jit(solution)/shard_map/ppermute | solution.py:243
  56.9 0.5 shard_map.102
  57.4 0.1 collective-permute-start.16
  57.5 0.0 collective-permute-done.7.rest_0_
  57.5 0.0 collective-permute-done.8.rest_1_
  57.5 1.2 %collective-permute-done.16.rest_4_ = f32[2,8,768]{2,1,0:T(8,128)S(1)} collective-permute-done((f32[2,8,768]{2,1,0:T(8,128)S(1)}, f32[2,8,768]{2,1,0:T(8,128)S(1)}, u32[]{:S(2)}, u32[]{:S(2)}) %collective-permute-start.16) | collective-permute-done | bytes 49184 | tf_op jit(solution)/shard_map/ppermute | solution.py:340
  58.7 1.1 %shard_map.103 = (f32[2,128,2048]{2,1,0:T(8,128)}, bf16[2,8,768]{2,1,0:T(8,128)(2,1)}) custom-call(f32[16,128]{1,0:T(8,128)S(1)} %broadcast_in_dim.2.decay, bf16[2,2,2048]{2,1,0:T(2,128)(2,1)S(1)} %copy-done.1, bf16[2,2,2048]{2,1,0:T(2,128)(2,1)S(1)} %copy-done.2, ...), custom_call_target="tpu_custom_call", output_to_operand_aliasing={{0}: (5, {})} | custom-call | tf_op jit(solution)/shard_map/pallas_call | solution.py:314
  (6 shorter events, 0.0 us)
Async XLA Ops:
  0.6 13.6 %copy-start.4 = (s32[2,16]{1,0:T(2,128)S(1)}, s32[2,16]{1,0:T(2,128)}, u32[]{:S(2)}) copy-start(s32[2,16]{1,0:T(2,128)} %param.14) | copy-start | bytes 388
  0.6 17.8 %copy-start.5 = (f32[16]{0:T(128)S(1)}, f32[16]{0:T(128)}, u32[]{:S(2)}) copy-start(f32[16]{0:T(128)} %param.9) | copy-start | bytes 196
  2.5 50.4 %copy-start = (bf16[2048,768]{1,0:T(8,128)(2,1)S(1)}, bf16[2048,768]{1,0:T(8,128)(2,1)}, u32[]{:S(2)}) copy-start(bf16[2048,768]{1,0:T(8,128)(2,1)} %weight.1) | copy-start | bytes 9437188
  2.6 50.4 %copy-start.1 = (bf16[2,2,2048]{2,1,0:T(2,128)(2,1)S(1)}, bf16[2,2,2048]{2,1,0:T(2,128)(2,1)}, u32[]{:S(2)}) copy-start(bf16[2,2,2048]{2,1,0:T(2,128)(2,1)} %k.7) | copy-start | bytes 49156
  2.6 50.4 %copy-start.2 = (bf16[2,2,2048]{2,1,0:T(2,128)(2,1)S(1)}, bf16[2,2,2048]{2,1,0:T(2,128)(2,1)}, u32[]{:S(2)}) copy-start(bf16[2,2,2048]{2,1,0:T(2,128)(2,1)} %v.7) | copy-start | bytes 49156
  2.6 11.6 %collective-permute-start = (bf16[2,272,128]{2,1,0:T(8,128)(2,1)}, bf16[2,272,128]{2,1,0:T(8,128)(2,1)S(1)}, u32[]{:S(2)}, u32[]{:S(2)}) collective-permute-start(bf16[2,272,128]{2,1,0:T(8,128)(2,1)} %shard_map.95), channel_id=1, source_target_pairs={{0,8},{2,10},{4,12},{6,14},{8,0},{10,2},{12,4},{14,6},{1,9},{3,11}... | collective-permute-start | bytes 417800 | tf_op jit(solution)/shard_map/ppermute | solution.py:243
  9.2 8.5 %collective-permute-start.1 = (bf16[2,272,128]{2,1,0:T(8,128)(2,1)}, bf16[2,272,128]{2,1,0:T(8,128)(2,1)S(1)}, u32[]{:S(2)}, u32[]{:S(2)}) collective-permute-start(bf16[2,272,128]{2,1,0:T(8,128)(2,1)} %get-tuple-element.24), channel_id=1, source_target_pairs={{0,2},{2,0},{4,6},{6,4},{8,10},{10,8},{12,14},{14,12},{1,3},{3,1},... | collective-permute-start | bytes 417800 | tf_op jit(solution)/shard_map/ppermute | solution.py:243
  10.7 8.7 %collective-permute-start.2 = (bf16[2,272,128]{2,1,0:T(8,128)(2,1)}, bf16[2,272,128]{2,1,0:T(8,128)(2,1)S(1)}, u32[]{:S(2)}, u32[]{:S(2)}) collective-permute-start(bf16[2,272,128]{2,1,0:T(8,128)(2,1)} %get-tuple-element.25), channel_id=1, source_target_pairs={{0,4},{2,6},{4,0},{6,2},{8,12},{10,14},{12,8},{14,10},{1,5},{3,7},... | collective-permute-start | bytes 417800 | tf_op jit(solution)/shard_map/ppermute | solution.py:243
  12.3 16.8 %collective-permute-start.3 = (bf16[2,272,128]{2,1,0:T(8,128)(2,1)}, bf16[2,272,128]{2,1,0:T(8,128)(2,1)S(1)}, u32[]{:S(2)}, u32[]{:S(2)}) collective-permute-start(bf16[2,272,128]{2,1,0:T(8,128)(2,1)} %get-tuple-element.26), channel_id=1, source_target_pairs={{0,6},{2,4},{4,2},{6,0},{8,14},{10,12},{12,10},{14,8},{1,7},{3,5},... | collective-permute-start | bytes 417800 | tf_op jit(solution)/shard_map/ppermute | solution.py:243
  12.7 17.1 %collective-permute-start.4 = (bf16[2,272,128]{2,1,0:T(8,128)(2,1)}, bf16[2,272,128]{2,1,0:T(8,128)(2,1)S(1)}, u32[]{:S(2)}, u32[]{:S(2)}) collective-permute-start(bf16[2,272,128]{2,1,0:T(8,128)(2,1)} %get-tuple-element.27), channel_id=1, source_target_pairs={{0,10},{2,8},{4,14},{6,12},{8,2},{10,0},{12,6},{14,4},{1,11},{3,9}... | collective-permute-start | bytes 417800 | tf_op jit(solution)/shard_map/ppermute | solution.py:243
  14.2 15.6 %collective-permute-start.5 = (bf16[2,272,128]{2,1,0:T(8,128)(2,1)}, bf16[2,272,128]{2,1,0:T(8,128)(2,1)S(1)}, u32[]{:S(2)}, u32[]{:S(2)}) collective-permute-start(bf16[2,272,128]{2,1,0:T(8,128)(2,1)} %get-tuple-element.28), channel_id=1, source_target_pairs={{0,12},{2,14},{4,8},{6,10},{8,4},{10,6},{12,0},{14,2},{1,13},{3,15... | collective-permute-start | bytes 417800 | tf_op jit(solution)/shard_map/ppermute | solution.py:243
  17.7 12.2 %collective-permute-start.6 = (bf16[2,272,128]{2,1,0:T(8,128)(2,1)}, bf16[2,272,128]{2,1,0:T(8,128)(2,1)S(1)}, u32[]{:S(2)}, u32[]{:S(2)}) collective-permute-start(bf16[2,272,128]{2,1,0:T(8,128)(2,1)} %get-tuple-element.29), channel_id=1, source_target_pairs={{0,14},{2,12},{4,10},{6,8},{8,6},{10,4},{12,2},{14,0},{1,15},{3,13... | collective-permute-start | bytes 417800 | tf_op jit(solution)/shard_map/ppermute | solution.py:243
  18.5 0.9 %copy-start.3 = (bf16[2,272,128]{2,1,0:T(8,128)(2,1)S(1)}, bf16[2,272,128]{2,1,0:T(8,128)(2,1)}, u32[]{:S(2)}) copy-start(bf16[2,272,128]{2,1,0:T(8,128)(2,1)} %get-tuple-element.30.chunk) | copy-start | bytes 417796
  30.9 13.7 %collective-permute-start.9 = (bf16[592,128]{1,0:T(8,128)(2,1)S(1)}, bf16[592,128]{1,0:T(8,128)(2,1)S(1)}, u32[]{:S(2)}, u32[]{:S(2)}) collective-permute-start(bf16[592,128]{1,0:T(8,128)(2,1)S(1)} %get-tuple-element.34), channel_id=1, source_target_pairs={{0,8},{2,10},{4,12},{6,14},{8,0},{10,2},{12,4},{14,6},{1,9},{3,11}... | collective-permute-start | bytes 454664 | tf_op jit(solution)/shard_map/ppermute | solution.py:243
  36.2 9.9 %collective-permute-start.10 = (bf16[528,128]{1,0:T(8,128)(2,1)S(1)}, bf16[528,128]{1,0:T(8,128)(2,1)S(1)}, u32[]{:S(2)}, u32[]{:S(2)}) collective-permute-start(bf16[528,128]{1,0:T(8,128)(2,1)S(1)} %get-tuple-element.35), channel_id=1, source_target_pairs={{0,2},{2,0},{4,6},{6,4},{8,10},{10,8},{12,14},{14,12},{1,3},{3,1},... | collective-permute-start | bytes 405512 | tf_op jit(solution)/shard_map/ppermute | solution.py:243
  37.2 13.9 %collective-permute-start.11 = (bf16[528,128]{1,0:T(8,128)(2,1)S(1)}, bf16[528,128]{1,0:T(8,128)(2,1)S(1)}, u32[]{:S(2)}, u32[]{:S(2)}) collective-permute-start(bf16[528,128]{1,0:T(8,128)(2,1)S(1)} %get-tuple-element.36), channel_id=1, source_target_pairs={{0,4},{2,6},{4,0},{6,2},{8,12},{10,14},{12,8},{14,10},{1,5},{3,7},... | collective-permute-start | bytes 405512 | tf_op jit(solution)/shard_map/ppermute | solution.py:243
  37.3 15.7 %collective-permute-start.12 = (bf16[528,128]{1,0:T(8,128)(2,1)S(1)}, bf16[528,128]{1,0:T(8,128)(2,1)S(1)}, u32[]{:S(2)}, u32[]{:S(2)}) collective-permute-start(bf16[528,128]{1,0:T(8,128)(2,1)S(1)} %get-tuple-element.37), channel_id=1, source_target_pairs={{0,10},{2,8},{4,14},{6,12},{8,2},{10,0},{12,6},{14,4},{1,11},{3,9}... | collective-permute-start | bytes 405512 | tf_op jit(solution)/shard_map/ppermute | solution.py:243
  40.1 12.8 %collective-permute-start.13 = (bf16[528,128]{1,0:T(8,128)(2,1)S(1)}, bf16[528,128]{1,0:T(8,128)(2,1)S(1)}, u32[]{:S(2)}, u32[]{:S(2)}) collective-permute-start(bf16[528,128]{1,0:T(8,128)(2,1)S(1)} %get-tuple-element.38), channel_id=1, source_target_pairs={{0,6},{2,4},{4,2},{6,0},{8,14},{10,12},{12,10},{14,8},{1,7},{3,5},... | collective-permute-start | bytes 405512 | tf_op jit(solution)/shard_map/ppermute | solution.py:243
  44.6 4.0 %collective-permute-start.14 = (bf16[128,128]{1,0:T(8,128)(2,1)S(1)}, bf16[128,128]{1,0:T(8,128)(2,1)S(1)}, u32[]{:S(2)}, u32[]{:S(2)}) collective-permute-start(bf16[128,128]{1,0:T(8,128)(2,1)S(1)} %shard_map.100.have), channel_id=1, source_target_pairs={{0,2},{2,0},{4,6},{6,4},{8,10},{10,8},{12,14},{14,12},{1,3},{3,1},... | collective-permute-start | bytes 98312 | tf_op jit(solution)/shard_map/ppermute | solution.py:243
  46.1 11.4 %collective-permute-start.7 = (bf16[528,128]{1,0:T(8,128)(2,1)S(1)}, bf16[528,128]{1,0:T(8,128)(2,1)S(1)}, u32[]{:S(2)}, u32[]{:S(2)}) collective-permute-start(bf16[528,128]{1,0:T(8,128)(2,1)S(1)} %get-tuple-element.31), channel_id=1, source_target_pairs={{0,12},{2,14},{4,8},{6,10},{8,4},{10,6},{12,0},{14,2},{1,13},{3,15... | collective-permute-start | bytes 405512 | tf_op jit(solution)/shard_map/ppermute | solution.py:243
  48.6 8.9 %collective-permute-start.8 = (bf16[528,128]{1,0:T(8,128)(2,1)S(1)}, bf16[528,128]{1,0:T(8,128)(2,1)S(1)}, u32[]{:S(2)}, u32[]{:S(2)}) collective-permute-start(bf16[528,128]{1,0:T(8,128)(2,1)S(1)} %get-tuple-element.32), channel_id=1, source_target_pairs={{0,14},{2,12},{4,10},{6,8},{8,6},{10,4},{12,2},{14,0},{1,15},{3,13... | collective-permute-start | bytes 405512 | tf_op jit(solution)/shard_map/ppermute | solution.py:243
  51.1 5.8 %collective-permute-start.15 = (bf16[256,128]{1,0:T(8,128)(2,1)S(1)}, bf16[256,128]{1,0:T(8,128)(2,1)S(1)}, u32[]{:S(2)}, u32[]{:S(2)}) collective-permute-start(bf16[256,128]{1,0:T(8,128)(2,1)S(1)} %shard_map.101), channel_id=1, source_target_pairs={{0,4},{2,6},{4,0},{6,2},{8,12},{10,14},{12,8},{14,10},{1,5},{3,7},... | collective-permute-start | bytes 196616 | tf_op jit(solution)/shard_map/ppermute | solution.py:243
  57.4 1.3 %collective-permute-start.16 = (f32[2,8,768]{2,1,0:T(8,128)S(1)}, f32[2,8,768]{2,1,0:T(8,128)S(1)}, u32[]{:S(2)}, u32[]{:S(2)}) collective-permute-start(f32[2,8,768]{2,1,0:T(8,128)S(1)} %get-tuple-element.43), channel_id=1, source_target_pairs={{0,1},{1,0},{2,3},{3,2},{4,5},{5,4},{6,7},{7,6},{8,9},{9,8},{10,11... | collective-permute-start | bytes 147464 | tf_op jit(solution)/shard_map/ppermute | solution.py:340

commit v7 on v6

--- a/solution.py
+++ b/solution.py
@@ -235,7 +235,7 @@
     slots, dim, columns = states.shape
     heads = columns // dim // n
     total, depth = n * slots, heads * dim
-    first, second = [4, 1, 2, 3, 5, 6, 7, 0], [4, 1, 2, 5, 3, 6, 7, 0]
+    first, second = [4, 1, 2, 3, 5, 6, 7, 0], [4, 1, 2, 3, 5, 6, 7, 0]
     decay = jnp.broadcast_to(jnp.exp(-decay_rates)[:, None], (columns // dim, dim))
 
     def exchange(order, chunks):
@@ -281,7 +281,7 @@
         out_specs=[VMEM] * (n + 1),
         scratch_shapes=[
             pltpu.VMEM((heads, total * dim, dim), BF16),
-            pltpu.VMEM((total * EXTRA, dim), F32),
+            pltpu.VMEM(((total + 1) * EXTRA, dim), F32),
             pltpu.VMEM((slots * KEPT, dim), F32),
             pltpu.SMEM(table.shape, jnp.int32),
             pltpu.VMEM((slots, depth + EXTRA, dim), BF16),

time: 60 us -> 59.1 us (0.985)
  waiting for transfers between devices: 20.3 us -> 17.2 us
  starting transfers between devices: 29.2 us -> 31.3 us
    ppermute x16, waiting for transfers between devices: 19.1 us -> 16 us  [exchange(): lax.ppermute(chunk, 'beam', [(j, j ^ x) for j in range(n)])]
    ppermute x16, starting transfers between devices: 29.1 us -> 31.2 us  [exchange(): lax.ppermute(chunk, 'beam', [(j, j ^ x) for j in range(n)])]
  transfers between devices with their start and end apart: 17 -> 17, of which waited for: 7 -> 6; matrix products, arithmetic and copies ran while one was open for 0% -> 0% of each run, Pallas kernels for 8% -> 8%
where the time goes in v7:
time: 59.1 us; the launch traced here: 58.9 us
  starting transfers between devices  31.3 us (53%)
  waiting for transfers between devices  17.2 us (29%)
  Pallas kernels  8.54 us (14%)
  local copies, waits for them, and re-layouts  1.01 us (2%)
  between operations  0.79 us (1%)
    ppermute x16, starting transfers between devices, exchange(): lax.ppermute(chunk, 'beam', [(j, j ^ x) for j in range(n)])  31.2 us
    ppermute x16, waiting for transfers between devices, exchange(): lax.ppermute(chunk, 'beam', [(j, j ^ x) for j in range(n)])  16 us
    pallas_call x2, Pallas kernels, fast(): pl.pallas_call(functools.partial(pack_kernel, n, part), out_shape=[jax.Sh...  4.37 us
    pallas_call x2, Pallas kernels, finish(): pl.pallas_call(functools.partial(final_kernel, n, part, not before), out_...  2.63 us
    ppermute x1, waiting for transfers between devices, fast(): other = lax.ppermute(send, 'head', [(0, 1), (1, 0)])  1.2 us
  transfers between devices with their start and end apart: 17, of which 6 were waited for; matrix products, arithmetic and copies ran while one was open for 0% of the time, Pallas kernels for 8%

profile of v7, /device:TPU:0, one launch (start us, length us, event | category | flops | bytes accessed | tf_op | source)
XLA Modules:
  0.0 58.9 jit_solution(8515837570319218804)
XLA Ops:
  0.6 0.0 copy-start.4
  0.6 0.0 copy-start.5
  0.6 1.9 %shard_map.95 = bf16[2,272,128]{2,1,0:T(8,128)(2,1)} custom-call(f32[2,128,2048]{2,1,0:T(8,128)} %st_hbm.3, bf16[2,2,2048]{2,1,0:T(2,128)(2,1)} %q.3, bf16[2,2,2048]{2,1,0:T(2,128)(2,1)} %k.7, bf16[2,2,2048]{2,1,0:T(2,128)(2,1)} %v.7, bf16[2,2,2048]{2,1,0:T(2,128)(2,1)} %g.3), custom_call_target="tpu_custom_call" | custom-call | tf_op jit(solution)/shard_map/pallas_call | solution.py:250
  2.5 0.0 copy-start
  2.6 0.0 copy-start.1
  2.6 0.0 copy-start.2
  2.6 4.1 %collective-permute-start = (bf16[2,272,128]{2,1,0:T(8,128)(2,1)}, bf16[2,272,128]{2,1,0:T(8,128)(2,1)S(1)}, u32[]{:S(2)}, u32[]{:S(2)}) collective-permute-start(bf16[2,272,128]{2,1,0:T(8,128)(2,1)} %shard_map.95), channel_id=1, source_target_pairs={{0,8},{2,10},{4,12},{6,14},{8,0},{10,2},{12,4},{14,6},{1,9},{3,11}... | collective-permute-start | bytes 417800 | tf_op jit(solution)/shard_map/ppermute | solution.py:243
  6.7 2.5 %shard_map.96 = (bf16[2,272,128]{2,1,0:T(8,128)(2,1)}, bf16[2,272,128]{2,1,0:T(8,128)(2,1)}, bf16[2,272,128]{2,1,0:T(8,128)(2,1)}, bf16[2,272,128]{2,1,0:T(8,128...) custom-call(f32[2,128,2048]{2,1,0:T(8,128)} %st_hbm.3, ...), custom_call_target="tpu_custom_call" | custom-call | tf_op jit(solution)/shard_map/pallas_call | solution.py:250
  9.2 1.6 %collective-permute-start.1 = (bf16[2,272,128]{2,1,0:T(8,128)(2,1)}, bf16[2,272,128]{2,1,0:T(8,128)(2,1)S(1)}, u32[]{:S(2)}, u32[]{:S(2)}) collective-permute-start(bf16[2,272,128]{2,1,0:T(8,128)(2,1)} %get-tuple-element.24), channel_id=1, source_target_pairs={{0,2},{2,0},{4,6},{6,4},{8,10},{10,8},{12,14},{14,12},{1,3},{3,1},... | collective-permute-start | bytes 417800 | tf_op jit(solution)/shard_map/ppermute | solution.py:243
  10.7 1.6 %collective-permute-start.2 = (bf16[2,272,128]{2,1,0:T(8,128)(2,1)}, bf16[2,272,128]{2,1,0:T(8,128)(2,1)S(1)}, u32[]{:S(2)}, u32[]{:S(2)}) collective-permute-start(bf16[2,272,128]{2,1,0:T(8,128)(2,1)} %get-tuple-element.25), channel_id=1, source_target_pairs={{0,4},{2,6},{4,0},{6,2},{8,12},{10,14},{12,8},{14,10},{1,5},{3,7},... | collective-permute-start | bytes 417800 | tf_op jit(solution)/shard_map/ppermute | solution.py:243
  12.3 0.4 collective-permute-start.3
  12.7 1.5 %collective-permute-start.4 = (bf16[2,272,128]{2,1,0:T(8,128)(2,1)}, bf16[2,272,128]{2,1,0:T(8,128)(2,1)S(1)}, u32[]{:S(2)}, u32[]{:S(2)}) collective-permute-start(bf16[2,272,128]{2,1,0:T(8,128)(2,1)} %get-tuple-element.27), channel_id=1, source_target_pairs={{0,10},{2,8},{4,14},{6,12},{8,2},{10,0},{12,6},{14,4},{1,11},{3,9}... | collective-permute-start | bytes 417800 | tf_op jit(solution)/shard_map/ppermute | solution.py:243
  14.2 0.0 copy-done.4
  14.2 0.0 collective-permute-done.rest_0_
  14.2 3.5 %collective-permute-start.5 = (bf16[2,272,128]{2,1,0:T(8,128)(2,1)}, bf16[2,272,128]{2,1,0:T(8,128)(2,1)S(1)}, u32[]{:S(2)}, u32[]{:S(2)}) collective-permute-start(bf16[2,272,128]{2,1,0:T(8,128)(2,1)} %get-tuple-element.28), channel_id=1, source_target_pairs={{0,12},{2,14},{4,8},{6,10},{8,4},{10,6},{12,0},{14,2},{1,13},{3,15... | collective-permute-start | bytes 417800 | tf_op jit(solution)/shard_map/ppermute | solution.py:243
  17.7 0.0 collective-permute-done.1.rest_1_
  17.7 0.8 %collective-permute-start.6 = (bf16[2,272,128]{2,1,0:T(8,128)(2,1)}, bf16[2,272,128]{2,1,0:T(8,128)(2,1)S(1)}, u32[]{:S(2)}, u32[]{:S(2)}) collective-permute-start(bf16[2,272,128]{2,1,0:T(8,128)(2,1)} %get-tuple-element.29), channel_id=1, source_target_pairs={{0,14},{2,12},{4,10},{6,8},{8,6},{10,4},{12,2},{14,0},{1,15},{3,13... | collective-permute-start | bytes 417800 | tf_op jit(solution)/shard_map/ppermute | solution.py:243
  18.5 0.0 copy-done.5
  18.5 0.0 copy-start.3
  18.5 0.9 %copy-done.3 = bf16[2,272,128]{2,1,0:T(8,128)(2,1)S(1)} copy-done((bf16[2,272,128]{2,1,0:T(8,128)(2,1)S(1)}, bf16[2,272,128]{2,1,0:T(8,128)(2,1)}, u32[]{:S(2)}) %copy-start.3) | copy-done | bytes 139288
  19.4 0.0 collective-permute-done.2.rest_2_
  19.4 9.6 %collective-permute-done.3.rest_3_ = bf16[2,272,128]{2,1,0:T(8,128)(2,1)S(1)} collective-permute-done((bf16[2,272,128]{2,1,0:T(8,128)(2,1)}, bf16[2,272,128]{2,1,0:T(8,128)(2,1)S(1)}, u32[]{:S(2)}, u32[]{:S(2)}) %collective-permute-start.3) | collective-permute-done | bytes 139296 | tf_op jit(solution)/shard_map/ppermute | solution.py:243
  29.1 0.8 %collective-permute-done.4.rest_4_ = bf16[2,272,128]{2,1,0:T(8,128)(2,1)S(1)} collective-permute-done((bf16[2,272,128]{2,1,0:T(8,128)(2,1)}, bf16[2,272,128]{2,1,0:T(8,128)(2,1)S(1)}, u32[]{:S(2)}, u32[]{:S(2)}) %collective-permute-start.4) | collective-permute-done | bytes 139296 | tf_op jit(solution)/shard_map/ppermute | solution.py:243
  29.8 0.0 collective-permute-done.5.rest_5_
  29.8 0.0 collective-permute-done.6.rest_6_
  29.8 0.1 broadcast_in_dim.2.decay
  29.9 1.0 %shard_map.98 = (bf16[592,128]{1,0:T(8,128)(2,1)S(1)}, bf16[528,128]{1,0:T(8,128)(2,1)S(1)}, bf16[528,128]{1,0:T(8,128)(2,1)S(1)}, bf16[528,128]{1,0:T(8,128)(2,...) custom-call(s32[4,16]{1,0:T(4,128)S(1)} %pad_add_fusion.parents_hbm,, ...), custom_call_target="tpu_custom_call" | custom-call | tf_op jit(solution)/shard_map/pallas_call | solution.py:274
  30.9 5.3 %collective-permute-start.9 = (bf16[592,128]{1,0:T(8,128)(2,1)S(1)}, bf16[592,128]{1,0:T(8,128)(2,1)S(1)}, u32[]{:S(2)}, u32[]{:S(2)}) collective-permute-start(bf16[592,128]{1,0:T(8,128)(2,1)S(1)} %get-tuple-element.34), channel_id=1, source_target_pairs={{0,8},{2,10},{4,12},{6,14},{8,0},{10,2},{12,4},{14,6},{1,9},{3,11}... | collective-permute-start | bytes 454664 | tf_op jit(solution)/shard_map/ppermute | solution.py:243
  36.2 1.0 %collective-permute-start.10 = (bf16[528,128]{1,0:T(8,128)(2,1)S(1)}, bf16[528,128]{1,0:T(8,128)(2,1)S(1)}, u32[]{:S(2)}, u32[]{:S(2)}) collective-permute-start(bf16[528,128]{1,0:T(8,128)(2,1)S(1)} %get-tuple-element.35), channel_id=1, source_target_pairs={{0,2},{2,0},{4,6},{6,4},{8,10},{10,8},{12,14},{14,12},{1,3},{3,1},... | collective-permute-start | bytes 405512 | tf_op jit(solution)/shard_map/ppermute | solution.py:243
  37.2 0.1 collective-permute-start.11
  37.3 2.4 %collective-permute-start.12 = (bf16[528,128]{1,0:T(8,128)(2,1)S(1)}, bf16[528,128]{1,0:T(8,128)(2,1)S(1)}, u32[]{:S(2)}, u32[]{:S(2)}) collective-permute-start(bf16[528,128]{1,0:T(8,128)(2,1)S(1)} %get-tuple-element.37), channel_id=1, source_target_pairs={{0,6},{2,4},{4,2},{6,0},{8,14},{10,12},{12,10},{14,8},{1,7},{3,5},... | collective-permute-start | bytes 405512 | tf_op jit(solution)/shard_map/ppermute | solution.py:243
  39.7 1.3 %collective-permute-start.13 = (bf16[528,128]{1,0:T(8,128)(2,1)S(1)}, bf16[528,128]{1,0:T(8,128)(2,1)S(1)}, u32[]{:S(2)}, u32[]{:S(2)}) collective-permute-start(bf16[528,128]{1,0:T(8,128)(2,1)S(1)} %get-tuple-element.38), channel_id=1, source_target_pairs={{0,10},{2,8},{4,14},{6,12},{8,2},{10,0},{12,6},{14,4},{1,11},{3,9}... | collective-permute-start | bytes 405512 | tf_op jit(solution)/shard_map/ppermute | solution.py:243
  41.0 0.0 collective-permute-done.9.rest_2_.got
  41.0 1.2 %collective-permute-start.14 = (bf16[128,128]{1,0:T(8,128)(2,1)S(1)}, bf16[128,128]{1,0:T(8,128)(2,1)S(1)}, u32[]{:S(2)}, u32[]{:S(2)}) collective-permute-start(bf16[128,128]{1,0:T(8,128)(2,1)S(1)} %shard_map.100.have), channel_id=1, source_target_pairs={{0,2},{2,0},{4,6},{6,4},{8,10},{10,8},{12,14},{14,12},{1,3},{3,1},... | collective-permute-start | bytes 98312 | tf_op jit(solution)/shard_map/ppermute | solution.py:243
  42.2 1.2 %collective-permute-done.10.rest_3_ = bf16[528,128]{1,0:T(8,128)(2,1)S(1)} collective-permute-done((bf16[528,128]{1,0:T(8,128)(2,1)S(1)}, bf16[528,128]{1,0:T(8,128)(2,1)S(1)}, u32[]{:S(2)}, u32[]{:S(2)}) %collective-permute-start.10) | collective-permute-done | bytes 135200 | tf_op jit(solution)/shard_map/ppermute | solution.py:243
  43.5 2.8 %collective-permute-start.7 = (bf16[528,128]{1,0:T(8,128)(2,1)S(1)}, bf16[528,128]{1,0:T(8,128)(2,1)S(1)}, u32[]{:S(2)}, u32[]{:S(2)}) collective-permute-start(bf16[528,128]{1,0:T(8,128)(2,1)S(1)} %get-tuple-element.31), channel_id=1, source_target_pairs={{0,12},{2,14},{4,8},{6,10},{8,4},{10,6},{12,0},{14,2},{1,13},{3,15... | collective-permute-start | bytes 405512 | tf_op jit(solution)/shard_map/ppermute | solution.py:243
  46.2 0.0 collective-permute-done.14.got.rest_0_
  46.2 3.7 %collective-permute-start.8 = (bf16[528,128]{1,0:T(8,128)(2,1)S(1)}, bf16[528,128]{1,0:T(8,128)(2,1)S(1)}, u32[]{:S(2)}, u32[]{:S(2)}) collective-permute-start(bf16[528,128]{1,0:T(8,128)(2,1)S(1)} %get-tuple-element.32), channel_id=1, source_target_pairs={{0,14},{2,12},{4,10},{6,8},{8,6},{10,4},{12,2},{14,0},{1,15},{3,13... | collective-permute-start | bytes 405512 | tf_op jit(solution)/shard_map/ppermute | solution.py:243
  49.9 0.0 collective-permute-done.11.rest_4_
  49.9 0.1 collective-permute-start.15
  50.0 0.0 collective-permute-done.12.rest_5_
  50.0 3.8 %collective-permute-done.13.rest_6_ = bf16[528,128]{1,0:T(8,128)(2,1)S(1)} collective-permute-done((bf16[528,128]{1,0:T(8,128)(2,1)S(1)}, bf16[528,128]{1,0:T(8,128)(2,1)S(1)}, u32[]{:S(2)}, u32[]{:S(2)}) %collective-permute-start.13) | collective-permute-done | bytes 135200 | tf_op jit(solution)/shard_map/ppermute | solution.py:243
  53.8 0.0 copy-done
  53.9 0.0 copy-done.1
  53.9 0.0 copy-done.2
  53.9 1.5 %shard_map.99 = (f32[2,128,2048]{2,1,0:T(8,128)}, f32[32,768]{1,0:T(8,128)S(1)}) custom-call(f32[16,128]{1,0:T(8,128)S(1)} %broadcast_in_dim.2.decay, bf16[2,2,2048]{2,1,0:T(2,128)(2,1)S(1)} %copy-done.1, bf16[2,2,2048]{2,1,0:T(2,128)(2,1)S(1)} %copy-done.2, bf16[2048,768]{1,0:T(8,128)(2,1)S(1)} %copy-done, ...), custom_call_target="tpu_custom_call" | custom-call | tf_op jit(solution)/shard_map/pallas_call | solution.py:314
  55.4 0.6 collective-permute-done.15.rest_1_
  56.0 0.5 shard_map.102
  56.5 0.1 collective-permute-start.16
  56.6 0.0 collective-permute-done.7.rest_0_
  56.6 0.0 collective-permute-done.8.rest_1_
  56.6 1.2 %collective-permute-done.16.rest_4_ = f32[2,8,768]{2,1,0:T(8,128)S(1)} collective-permute-done((f32[2,8,768]{2,1,0:T(8,128)S(1)}, f32[2,8,768]{2,1,0:T(8,128)S(1)}, u32[]{:S(2)}, u32[]{:S(2)}) %collective-permute-start.16) | collective-permute-done | bytes 49184 | tf_op jit(solution)/shard_map/ppermute | solution.py:340
  57.8 1.1 %shard_map.103 = (f32[2,128,2048]{2,1,0:T(8,128)}, bf16[2,8,768]{2,1,0:T(8,128)(2,1)}) custom-call(f32[16,128]{1,0:T(8,128)S(1)} %broadcast_in_dim.2.decay, bf16[2,2,2048]{2,1,0:T(2,128)(2,1)S(1)} %copy-done.1, bf16[2,2,2048]{2,1,0:T(2,128)(2,1)S(1)} %copy-done.2, ...), custom_call_target="tpu_custom_call", output_to_operand_aliasing={{0}: (5, {})} | custom-call | tf_op jit(solution)/shard_map/pallas_call | solution.py:314
  (6 shorter events, 0.0 us)
Async XLA Ops:
  0.6 13.6 %copy-start.4 = (s32[2,16]{1,0:T(2,128)S(1)}, s32[2,16]{1,0:T(2,128)}, u32[]{:S(2)}) copy-start(s32[2,16]{1,0:T(2,128)} %param.14) | copy-start | bytes 388
  0.6 17.8 %copy-start.5 = (f32[16]{0:T(128)S(1)}, f32[16]{0:T(128)}, u32[]{:S(2)}) copy-start(f32[16]{0:T(128)} %param.9) | copy-start | bytes 196
  2.5 51.3 %copy-start = (bf16[2048,768]{1,0:T(8,128)(2,1)S(1)}, bf16[2048,768]{1,0:T(8,128)(2,1)}, u32[]{:S(2)}) copy-start(bf16[2048,768]{1,0:T(8,128)(2,1)} %weight.1) | copy-start | bytes 9437188
  2.6 51.3 %copy-start.1 = (bf16[2,2,2048]{2,1,0:T(2,128)(2,1)S(1)}, bf16[2,2,2048]{2,1,0:T(2,128)(2,1)}, u32[]{:S(2)}) copy-start(bf16[2,2,2048]{2,1,0:T(2,128)(2,1)} %k.7) | copy-start | bytes 49156
  2.6 51.3 %copy-start.2 = (bf16[2,2,2048]{2,1,0:T(2,128)(2,1)S(1)}, bf16[2,2,2048]{2,1,0:T(2,128)(2,1)}, u32[]{:S(2)}) copy-start(bf16[2,2,2048]{2,1,0:T(2,128)(2,1)} %v.7) | copy-start | bytes 49156
  2.6 11.6 %collective-permute-start = (bf16[2,272,128]{2,1,0:T(8,128)(2,1)}, bf16[2,272,128]{2,1,0:T(8,128)(2,1)S(1)}, u32[]{:S(2)}, u32[]{:S(2)}) collective-permute-start(bf16[2,272,128]{2,1,0:T(8,128)(2,1)} %shard_map.95), channel_id=1, source_target_pairs={{0,8},{2,10},{4,12},{6,14},{8,0},{10,2},{12,4},{14,6},{1,9},{3,11}... | collective-permute-start | bytes 417800 | tf_op jit(solution)/shard_map/ppermute | solution.py:243
  9.2 8.5 %collective-permute-start.1 = (bf16[2,272,128]{2,1,0:T(8,128)(2,1)}, bf16[2,272,128]{2,1,0:T(8,128)(2,1)S(1)}, u32[]{:S(2)}, u32[]{:S(2)}) collective-permute-start(bf16[2,272,128]{2,1,0:T(8,128)(2,1)} %get-tuple-element.24), channel_id=1, source_target_pairs={{0,2},{2,0},{4,6},{6,4},{8,10},{10,8},{12,14},{14,12},{1,3},{3,1},... | collective-permute-start | bytes 417800 | tf_op jit(solution)/shard_map/ppermute | solution.py:243
  10.7 8.7 %collective-permute-start.2 = (bf16[2,272,128]{2,1,0:T(8,128)(2,1)}, bf16[2,272,128]{2,1,0:T(8,128)(2,1)S(1)}, u32[]{:S(2)}, u32[]{:S(2)}) collective-permute-start(bf16[2,272,128]{2,1,0:T(8,128)(2,1)} %get-tuple-element.25), channel_id=1, source_target_pairs={{0,4},{2,6},{4,0},{6,2},{8,12},{10,14},{12,8},{14,10},{1,5},{3,7},... | collective-permute-start | bytes 417800 | tf_op jit(solution)/shard_map/ppermute | solution.py:243
  12.3 16.8 %collective-permute-start.3 = (bf16[2,272,128]{2,1,0:T(8,128)(2,1)}, bf16[2,272,128]{2,1,0:T(8,128)(2,1)S(1)}, u32[]{:S(2)}, u32[]{:S(2)}) collective-permute-start(bf16[2,272,128]{2,1,0:T(8,128)(2,1)} %get-tuple-element.26), channel_id=1, source_target_pairs={{0,6},{2,4},{4,2},{6,0},{8,14},{10,12},{12,10},{14,8},{1,7},{3,5},... | collective-permute-start | bytes 417800 | tf_op jit(solution)/shard_map/ppermute | solution.py:243
  12.7 17.1 %collective-permute-start.4 = (bf16[2,272,128]{2,1,0:T(8,128)(2,1)}, bf16[2,272,128]{2,1,0:T(8,128)(2,1)S(1)}, u32[]{:S(2)}, u32[]{:S(2)}) collective-permute-start(bf16[2,272,128]{2,1,0:T(8,128)(2,1)} %get-tuple-element.27), channel_id=1, source_target_pairs={{0,10},{2,8},{4,14},{6,12},{8,2},{10,0},{12,6},{14,4},{1,11},{3,9}... | collective-permute-start | bytes 417800 | tf_op jit(solution)/shard_map/ppermute | solution.py:243
  14.2 15.6 %collective-permute-start.5 = (bf16[2,272,128]{2,1,0:T(8,128)(2,1)}, bf16[2,272,128]{2,1,0:T(8,128)(2,1)S(1)}, u32[]{:S(2)}, u32[]{:S(2)}) collective-permute-start(bf16[2,272,128]{2,1,0:T(8,128)(2,1)} %get-tuple-element.28), channel_id=1, source_target_pairs={{0,12},{2,14},{4,8},{6,10},{8,4},{10,6},{12,0},{14,2},{1,13},{3,15... | collective-permute-start | bytes 417800 | tf_op jit(solution)/shard_map/ppermute | solution.py:243
  17.7 12.2 %collective-permute-start.6 = (bf16[2,272,128]{2,1,0:T(8,128)(2,1)}, bf16[2,272,128]{2,1,0:T(8,128)(2,1)S(1)}, u32[]{:S(2)}, u32[]{:S(2)}) collective-permute-start(bf16[2,272,128]{2,1,0:T(8,128)(2,1)} %get-tuple-element.29), channel_id=1, source_target_pairs={{0,14},{2,12},{4,10},{6,8},{8,6},{10,4},{12,2},{14,0},{1,15},{3,13... | collective-permute-start | bytes 417800 | tf_op jit(solution)/shard_map/ppermute | solution.py:243
  18.5 0.9 %copy-start.3 = (bf16[2,272,128]{2,1,0:T(8,128)(2,1)S(1)}, bf16[2,272,128]{2,1,0:T(8,128)(2,1)}, u32[]{:S(2)}) copy-start(bf16[2,272,128]{2,1,0:T(8,128)(2,1)} %get-tuple-element.30.chunk) | copy-start | bytes 417796
  30.9 10.1 %collective-permute-start.9 = (bf16[592,128]{1,0:T(8,128)(2,1)S(1)}, bf16[592,128]{1,0:T(8,128)(2,1)S(1)}, u32[]{:S(2)}, u32[]{:S(2)}) collective-permute-start(bf16[592,128]{1,0:T(8,128)(2,1)S(1)} %get-tuple-element.34), channel_id=1, source_target_pairs={{0,8},{2,10},{4,12},{6,14},{8,0},{10,2},{12,4},{14,6},{1,9},{3,11}... | collective-permute-start | bytes 454664 | tf_op jit(solution)/shard_map/ppermute | solution.py:243
  36.2 7.3 %collective-permute-start.10 = (bf16[528,128]{1,0:T(8,128)(2,1)S(1)}, bf16[528,128]{1,0:T(8,128)(2,1)S(1)}, u32[]{:S(2)}, u32[]{:S(2)}) collective-permute-start(bf16[528,128]{1,0:T(8,128)(2,1)S(1)} %get-tuple-element.35), channel_id=1, source_target_pairs={{0,2},{2,0},{4,6},{6,4},{8,10},{10,8},{12,14},{14,12},{1,3},{3,1},... | collective-permute-start | bytes 405512 | tf_op jit(solution)/shard_map/ppermute | solution.py:243
  37.2 12.8 %collective-permute-start.11 = (bf16[528,128]{1,0:T(8,128)(2,1)S(1)}, bf16[528,128]{1,0:T(8,128)(2,1)S(1)}, u32[]{:S(2)}, u32[]{:S(2)}) collective-permute-start(bf16[528,128]{1,0:T(8,128)(2,1)S(1)} %get-tuple-element.36), channel_id=1, source_target_pairs={{0,4},{2,6},{4,0},{6,2},{8,12},{10,14},{12,8},{14,10},{1,5},{3,7},... | collective-permute-start | bytes 405512 | tf_op jit(solution)/shard_map/ppermute | solution.py:243
  37.3 12.8 %collective-permute-start.12 = (bf16[528,128]{1,0:T(8,128)(2,1)S(1)}, bf16[528,128]{1,0:T(8,128)(2,1)S(1)}, u32[]{:S(2)}, u32[]{:S(2)}) collective-permute-start(bf16[528,128]{1,0:T(8,128)(2,1)S(1)} %get-tuple-element.37), channel_id=1, source_target_pairs={{0,6},{2,4},{4,2},{6,0},{8,14},{10,12},{12,10},{14,8},{1,7},{3,5},... | collective-permute-start | bytes 405512 | tf_op jit(solution)/shard_map/ppermute | solution.py:243
  39.7 14.2 %collective-permute-start.13 = (bf16[528,128]{1,0:T(8,128)(2,1)S(1)}, bf16[528,128]{1,0:T(8,128)(2,1)S(1)}, u32[]{:S(2)}, u32[]{:S(2)}) collective-permute-start(bf16[528,128]{1,0:T(8,128)(2,1)S(1)} %get-tuple-element.38), channel_id=1, source_target_pairs={{0,10},{2,8},{4,14},{6,12},{8,2},{10,0},{12,6},{14,4},{1,11},{3,9}... | collective-permute-start | bytes 405512 | tf_op jit(solution)/shard_map/ppermute | solution.py:243
  41.0 5.2 %collective-permute-start.14 = (bf16[128,128]{1,0:T(8,128)(2,1)S(1)}, bf16[128,128]{1,0:T(8,128)(2,1)S(1)}, u32[]{:S(2)}, u32[]{:S(2)}) collective-permute-start(bf16[128,128]{1,0:T(8,128)(2,1)S(1)} %shard_map.100.have), channel_id=1, source_target_pairs={{0,2},{2,0},{4,6},{6,4},{8,10},{10,8},{12,14},{14,12},{1,3},{3,1},... | collective-permute-start | bytes 98312 | tf_op jit(solution)/shard_map/ppermute | solution.py:243
  43.5 13.1 %collective-permute-start.7 = (bf16[528,128]{1,0:T(8,128)(2,1)S(1)}, bf16[528,128]{1,0:T(8,128)(2,1)S(1)}, u32[]{:S(2)}, u32[]{:S(2)}) collective-permute-start(bf16[528,128]{1,0:T(8,128)(2,1)S(1)} %get-tuple-element.31), channel_id=1, source_target_pairs={{0,12},{2,14},{4,8},{6,10},{8,4},{10,6},{12,0},{14,2},{1,13},{3,15... | collective-permute-start | bytes 405512 | tf_op jit(solution)/shard_map/ppermute | solution.py:243
  46.2 10.3 %collective-permute-start.8 = (bf16[528,128]{1,0:T(8,128)(2,1)S(1)}, bf16[528,128]{1,0:T(8,128)(2,1)S(1)}, u32[]{:S(2)}, u32[]{:S(2)}) collective-permute-start(bf16[528,128]{1,0:T(8,128)(2,1)S(1)} %get-tuple-element.32), channel_id=1, source_target_pairs={{0,14},{2,12},{4,10},{6,8},{8,6},{10,4},{12,2},{14,0},{1,15},{3,13... | collective-permute-start | bytes 405512 | tf_op jit(solution)/shard_map/ppermute | solution.py:243
  49.9 6.0 %collective-permute-start.15 = (bf16[256,128]{1,0:T(8,128)(2,1)S(1)}, bf16[256,128]{1,0:T(8,128)(2,1)S(1)}, u32[]{:S(2)}, u32[]{:S(2)}) collective-permute-start(bf16[256,128]{1,0:T(8,128)(2,1)S(1)} %shard_map.101), channel_id=1, source_target_pairs={{0,4},{2,6},{4,0},{6,2},{8,12},{10,14},{12,8},{14,10},{1,5},{3,7},... | collective-permute-start | bytes 196616 | tf_op jit(solution)/shard_map/ppermute | solution.py:243
  56.5 1.3 %collective-permute-start.16 = (f32[2,8,768]{2,1,0:T(8,128)S(1)}, f32[2,8,768]{2,1,0:T(8,128)S(1)}, u32[]{:S(2)}, u32[]{:S(2)}) collective-permute-start(f32[2,8,768]{2,1,0:T(8,128)S(1)} %get-tuple-element.43), channel_id=1, source_target_pairs={{0,1},{1,0},{2,3},{3,2},{4,5},{5,4},{6,7},{7,6},{8,9},{9,8},{10,11... | collective-permute-start | bytes 147464 | tf_op jit(solution)/shard_map/ppermute | solution.py:340

commit v8 on v7

--- a/solution.py
+++ b/solution.py
@@ -17,7 +17,7 @@
 KEPT = 8
 
 
-def params(limit=48):
+def params(limit=16):
     return pltpu.CompilerParams(vmem_limit_bytes=limit << 20)
 
 

time: 59.1 us -> 59.1 us (level)
  no operation moved by 1% of the time
where the time goes in v8:
time: 59.1 us; the launch traced here: 58.9 us
  starting transfers between devices  31.3 us (53%)
  waiting for transfers between devices  17.2 us (29%)
  Pallas kernels  8.54 us (14%)
  local copies, waits for them, and re-layouts  1.01 us (2%)
  between operations  0.79 us (1%)
    ppermute x16, starting transfers between devices, exchange(): lax.ppermute(chunk, 'beam', [(j, j ^ x) for j in range(n)])  31.2 us
    ppermute x16, waiting for transfers between devices, exchange(): lax.ppermute(chunk, 'beam', [(j, j ^ x) for j in range(n)])  16 us
    pallas_call x2, Pallas kernels, fast(): pl.pallas_call(functools.partial(pack_kernel, n, part), out_shape=[jax.Sh...  4.37 us
    pallas_call x2, Pallas kernels, finish(): pl.pallas_call(functools.partial(final_kernel, n, part, not before), out_...  2.63 us
    ppermute x1, waiting for transfers between devices, fast(): other = lax.ppermute(send, 'head', [(0, 1), (1, 0)])  1.2 us
  transfers between devices with their start and end apart: 17, of which 6 were waited for; matrix products, arithmetic and copies ran while one was open for 0% of the time, Pallas kernels for 8%

profile of v8, /device:TPU:0, one launch (start us, length us, event | category | flops | bytes accessed | tf_op | source)
XLA Modules:
  0.0 58.9 jit_solution(3061008856498502082)
XLA Ops:
  0.6 0.0 copy-start.4
  0.6 0.0 copy-start.5
  0.6 1.9 %shard_map.95 = bf16[2,272,128]{2,1,0:T(8,128)(2,1)} custom-call(f32[2,128,2048]{2,1,0:T(8,128)} %st_hbm.3, bf16[2,2,2048]{2,1,0:T(2,128)(2,1)} %q.3, bf16[2,2,2048]{2,1,0:T(2,128)(2,1)} %k.7, bf16[2,2,2048]{2,1,0:T(2,128)(2,1)} %v.7, bf16[2,2,2048]{2,1,0:T(2,128)(2,1)} %g.3), custom_call_target="tpu_custom_call" | custom-call | tf_op jit(solution)/shard_map/pallas_call | solution.py:250
  2.5 0.0 copy-start
  2.6 0.0 copy-start.1
  2.6 0.0 copy-start.2
  2.6 4.1 %collective-permute-start = (bf16[2,272,128]{2,1,0:T(8,128)(2,1)}, bf16[2,272,128]{2,1,0:T(8,128)(2,1)S(1)}, u32[]{:S(2)}, u32[]{:S(2)}) collective-permute-start(bf16[2,272,128]{2,1,0:T(8,128)(2,1)} %shard_map.95), channel_id=1, source_target_pairs={{0,8},{2,10},{4,12},{6,14},{8,0},{10,2},{12,4},{14,6},{1,9},{3,11}... | collective-permute-start | bytes 417800 | tf_op jit(solution)/shard_map/ppermute | solution.py:243
  6.7 2.5 %shard_map.96 = (bf16[2,272,128]{2,1,0:T(8,128)(2,1)}, bf16[2,272,128]{2,1,0:T(8,128)(2,1)}, bf16[2,272,128]{2,1,0:T(8,128)(2,1)}, bf16[2,272,128]{2,1,0:T(8,128...) custom-call(f32[2,128,2048]{2,1,0:T(8,128)} %st_hbm.3, ...), custom_call_target="tpu_custom_call" | custom-call | tf_op jit(solution)/shard_map/pallas_call | solution.py:250
  9.2 1.6 %collective-permute-start.1 = (bf16[2,272,128]{2,1,0:T(8,128)(2,1)}, bf16[2,272,128]{2,1,0:T(8,128)(2,1)S(1)}, u32[]{:S(2)}, u32[]{:S(2)}) collective-permute-start(bf16[2,272,128]{2,1,0:T(8,128)(2,1)} %get-tuple-element.24), channel_id=1, source_target_pairs={{0,2},{2,0},{4,6},{6,4},{8,10},{10,8},{12,14},{14,12},{1,3},{3,1},... | collective-permute-start | bytes 417800 | tf_op jit(solution)/shard_map/ppermute | solution.py:243
  10.7 1.6 %collective-permute-start.2 = (bf16[2,272,128]{2,1,0:T(8,128)(2,1)}, bf16[2,272,128]{2,1,0:T(8,128)(2,1)S(1)}, u32[]{:S(2)}, u32[]{:S(2)}) collective-permute-start(bf16[2,272,128]{2,1,0:T(8,128)(2,1)} %get-tuple-element.25), channel_id=1, source_target_pairs={{0,4},{2,6},{4,0},{6,2},{8,12},{10,14},{12,8},{14,10},{1,5},{3,7},... | collective-permute-start | bytes 417800 | tf_op jit(solution)/shard_map/ppermute | solution.py:243
  12.3 0.4 collective-permute-start.3
  12.7 1.5 %collective-permute-start.4 = (bf16[2,272,128]{2,1,0:T(8,128)(2,1)}, bf16[2,272,128]{2,1,0:T(8,128)(2,1)S(1)}, u32[]{:S(2)}, u32[]{:S(2)}) collective-permute-start(bf16[2,272,128]{2,1,0:T(8,128)(2,1)} %get-tuple-element.27), channel_id=1, source_target_pairs={{0,10},{2,8},{4,14},{6,12},{8,2},{10,0},{12,6},{14,4},{1,11},{3,9}... | collective-permute-start | bytes 417800 | tf_op jit(solution)/shard_map/ppermute | solution.py:243
  14.2 0.0 copy-done.4
  14.2 0.0 collective-permute-done.rest_0_
  14.2 3.5 %collective-permute-start.5 = (bf16[2,272,128]{2,1,0:T(8,128)(2,1)}, bf16[2,272,128]{2,1,0:T(8,128)(2,1)S(1)}, u32[]{:S(2)}, u32[]{:S(2)}) collective-permute-start(bf16[2,272,128]{2,1,0:T(8,128)(2,1)} %get-tuple-element.28), channel_id=1, source_target_pairs={{0,12},{2,14},{4,8},{6,10},{8,4},{10,6},{12,0},{14,2},{1,13},{3,15... | collective-permute-start | bytes 417800 | tf_op jit(solution)/shard_map/ppermute | solution.py:243
  17.7 0.0 collective-permute-done.1.rest_1_
  17.7 0.8 %collective-permute-start.6 = (bf16[2,272,128]{2,1,0:T(8,128)(2,1)}, bf16[2,272,128]{2,1,0:T(8,128)(2,1)S(1)}, u32[]{:S(2)}, u32[]{:S(2)}) collective-permute-start(bf16[2,272,128]{2,1,0:T(8,128)(2,1)} %get-tuple-element.29), channel_id=1, source_target_pairs={{0,14},{2,12},{4,10},{6,8},{8,6},{10,4},{12,2},{14,0},{1,15},{3,13... | collective-permute-start | bytes 417800 | tf_op jit(solution)/shard_map/ppermute | solution.py:243
  18.5 0.0 copy-done.5
  18.5 0.0 copy-start.3
  18.5 0.9 %copy-done.3 = bf16[2,272,128]{2,1,0:T(8,128)(2,1)S(1)} copy-done((bf16[2,272,128]{2,1,0:T(8,128)(2,1)S(1)}, bf16[2,272,128]{2,1,0:T(8,128)(2,1)}, u32[]{:S(2)}) %copy-start.3) | copy-done | bytes 139288
  19.4 0.0 collective-permute-done.2.rest_2_
  19.4 9.6 %collective-permute-done.3.rest_3_ = bf16[2,272,128]{2,1,0:T(8,128)(2,1)S(1)} collective-permute-done((bf16[2,272,128]{2,1,0:T(8,128)(2,1)}, bf16[2,272,128]{2,1,0:T(8,128)(2,1)S(1)}, u32[]{:S(2)}, u32[]{:S(2)}) %collective-permute-start.3) | collective-permute-done | bytes 139296 | tf_op jit(solution)/shard_map/ppermute | solution.py:243
  29.1 0.8 %collective-permute-done.4.rest_4_ = bf16[2,272,128]{2,1,0:T(8,128)(2,1)S(1)} collective-permute-done((bf16[2,272,128]{2,1,0:T(8,128)(2,1)}, bf16[2,272,128]{2,1,0:T(8,128)(2,1)S(1)}, u32[]{:S(2)}, u32[]{:S(2)}) %collective-permute-start.4) | collective-permute-done | bytes 139296 | tf_op jit(solution)/shard_map/ppermute | solution.py:243
  29.8 0.0 collective-permute-done.5.rest_5_
  29.8 0.0 collective-permute-done.6.rest_6_
  29.8 0.1 broadcast_in_dim.2.decay
  29.9 1.0 %shard_map.98 = (bf16[592,128]{1,0:T(8,128)(2,1)S(1)}, bf16[528,128]{1,0:T(8,128)(2,1)S(1)}, bf16[528,128]{1,0:T(8,128)(2,1)S(1)}, bf16[528,128]{1,0:T(8,128)(2,...) custom-call(s32[4,16]{1,0:T(4,128)S(1)} %pad_add_fusion.parents_hbm,, ...), custom_call_target="tpu_custom_call" | custom-call | tf_op jit(solution)/shard_map/pallas_call | solution.py:274
  30.9 5.3 %collective-permute-start.9 = (bf16[592,128]{1,0:T(8,128)(2,1)S(1)}, bf16[592,128]{1,0:T(8,128)(2,1)S(1)}, u32[]{:S(2)}, u32[]{:S(2)}) collective-permute-start(bf16[592,128]{1,0:T(8,128)(2,1)S(1)} %get-tuple-element.34), channel_id=1, source_target_pairs={{0,8},{2,10},{4,12},{6,14},{8,0},{10,2},{12,4},{14,6},{1,9},{3,11}... | collective-permute-start | bytes 454664 | tf_op jit(solution)/shard_map/ppermute | solution.py:243
  36.2 1.0 %collective-permute-start.10 = (bf16[528,128]{1,0:T(8,128)(2,1)S(1)}, bf16[528,128]{1,0:T(8,128)(2,1)S(1)}, u32[]{:S(2)}, u32[]{:S(2)}) collective-permute-start(bf16[528,128]{1,0:T(8,128)(2,1)S(1)} %get-tuple-element.35), channel_id=1, source_target_pairs={{0,2},{2,0},{4,6},{6,4},{8,10},{10,8},{12,14},{14,12},{1,3},{3,1},... | collective-permute-start | bytes 405512 | tf_op jit(solution)/shard_map/ppermute | solution.py:243
  37.2 0.1 collective-permute-start.11
  37.3 2.4 %collective-permute-start.12 = (bf16[528,128]{1,0:T(8,128)(2,1)S(1)}, bf16[528,128]{1,0:T(8,128)(2,1)S(1)}, u32[]{:S(2)}, u32[]{:S(2)}) collective-permute-start(bf16[528,128]{1,0:T(8,128)(2,1)S(1)} %get-tuple-element.37), channel_id=1, source_target_pairs={{0,6},{2,4},{4,2},{6,0},{8,14},{10,12},{12,10},{14,8},{1,7},{3,5},... | collective-permute-start | bytes 405512 | tf_op jit(solution)/shard_map/ppermute | solution.py:243
  39.7 1.3 %collective-permute-start.13 = (bf16[528,128]{1,0:T(8,128)(2,1)S(1)}, bf16[528,128]{1,0:T(8,128)(2,1)S(1)}, u32[]{:S(2)}, u32[]{:S(2)}) collective-permute-start(bf16[528,128]{1,0:T(8,128)(2,1)S(1)} %get-tuple-element.38), channel_id=1, source_target_pairs={{0,10},{2,8},{4,14},{6,12},{8,2},{10,0},{12,6},{14,4},{1,11},{3,9}... | collective-permute-start | bytes 405512 | tf_op jit(solution)/shard_map/ppermute | solution.py:243
  41.0 0.0 collective-permute-done.9.rest_2_.got
  41.0 1.2 %collective-permute-start.14 = (bf16[128,128]{1,0:T(8,128)(2,1)S(1)}, bf16[128,128]{1,0:T(8,128)(2,1)S(1)}, u32[]{:S(2)}, u32[]{:S(2)}) collective-permute-start(bf16[128,128]{1,0:T(8,128)(2,1)S(1)} %shard_map.100.have), channel_id=1, source_target_pairs={{0,2},{2,0},{4,6},{6,4},{8,10},{10,8},{12,14},{14,12},{1,3},{3,1},... | collective-permute-start | bytes 98312 | tf_op jit(solution)/shard_map/ppermute | solution.py:243
  42.2 1.2 %collective-permute-done.10.rest_3_ = bf16[528,128]{1,0:T(8,128)(2,1)S(1)} collective-permute-done((bf16[528,128]{1,0:T(8,128)(2,1)S(1)}, bf16[528,128]{1,0:T(8,128)(2,1)S(1)}, u32[]{:S(2)}, u32[]{:S(2)}) %collective-permute-start.10) | collective-permute-done | bytes 135200 | tf_op jit(solution)/shard_map/ppermute | solution.py:243
  43.5 2.8 %collective-permute-start.7 = (bf16[528,128]{1,0:T(8,128)(2,1)S(1)}, bf16[528,128]{1,0:T(8,128)(2,1)S(1)}, u32[]{:S(2)}, u32[]{:S(2)}) collective-permute-start(bf16[528,128]{1,0:T(8,128)(2,1)S(1)} %get-tuple-element.31), channel_id=1, source_target_pairs={{0,12},{2,14},{4,8},{6,10},{8,4},{10,6},{12,0},{14,2},{1,13},{3,15... | collective-permute-start | bytes 405512 | tf_op jit(solution)/shard_map/ppermute | solution.py:243
  46.2 0.0 collective-permute-done.14.got.rest_0_
  46.2 3.7 %collective-permute-start.8 = (bf16[528,128]{1,0:T(8,128)(2,1)S(1)}, bf16[528,128]{1,0:T(8,128)(2,1)S(1)}, u32[]{:S(2)}, u32[]{:S(2)}) collective-permute-start(bf16[528,128]{1,0:T(8,128)(2,1)S(1)} %get-tuple-element.32), channel_id=1, source_target_pairs={{0,14},{2,12},{4,10},{6,8},{8,6},{10,4},{12,2},{14,0},{1,15},{3,13... | collective-permute-start | bytes 405512 | tf_op jit(solution)/shard_map/ppermute | solution.py:243
  49.9 0.0 collective-permute-done.11.rest_4_
  49.9 0.1 collective-permute-start.15
  50.0 0.0 collective-permute-done.12.rest_5_
  50.0 3.8 %collective-permute-done.13.rest_6_ = bf16[528,128]{1,0:T(8,128)(2,1)S(1)} collective-permute-done((bf16[528,128]{1,0:T(8,128)(2,1)S(1)}, bf16[528,128]{1,0:T(8,128)(2,1)S(1)}, u32[]{:S(2)}, u32[]{:S(2)}) %collective-permute-start.13) | collective-permute-done | bytes 135200 | tf_op jit(solution)/shard_map/ppermute | solution.py:243
  53.8 0.0 copy-done
  53.9 0.0 copy-done.1
  53.9 0.0 copy-done.2
  53.9 1.5 %shard_map.99 = (f32[2,128,2048]{2,1,0:T(8,128)}, f32[32,768]{1,0:T(8,128)S(1)}) custom-call(f32[16,128]{1,0:T(8,128)S(1)} %broadcast_in_dim.2.decay, bf16[2,2,2048]{2,1,0:T(2,128)(2,1)S(1)} %copy-done.1, bf16[2,2,2048]{2,1,0:T(2,128)(2,1)S(1)} %copy-done.2, bf16[2048,768]{1,0:T(8,128)(2,1)S(1)} %copy-done, ...), custom_call_target="tpu_custom_call" | custom-call | tf_op jit(solution)/shard_map/pallas_call | solution.py:314
  55.4 0.6 collective-permute-done.15.rest_1_
  56.0 0.5 shard_map.102
  56.5 0.1 collective-permute-start.16
  56.6 0.0 collective-permute-done.7.rest_0_
  56.6 0.0 collective-permute-done.8.rest_1_
  56.6 1.2 %collective-permute-done.16.rest_4_ = f32[2,8,768]{2,1,0:T(8,128)S(1)} collective-permute-done((f32[2,8,768]{2,1,0:T(8,128)S(1)}, f32[2,8,768]{2,1,0:T(8,128)S(1)}, u32[]{:S(2)}, u32[]{:S(2)}) %collective-permute-start.16) | collective-permute-done | bytes 49184 | tf_op jit(solution)/shard_map/ppermute | solution.py:340
  57.8 1.1 %shard_map.103 = (f32[2,128,2048]{2,1,0:T(8,128)}, bf16[2,8,768]{2,1,0:T(8,128)(2,1)}) custom-call(f32[16,128]{1,0:T(8,128)S(1)} %broadcast_in_dim.2.decay, bf16[2,2,2048]{2,1,0:T(2,128)(2,1)S(1)} %copy-done.1, bf16[2,2,2048]{2,1,0:T(2,128)(2,1)S(1)} %copy-done.2, ...), custom_call_target="tpu_custom_call", output_to_operand_aliasing={{0}: (5, {})} | custom-call | tf_op jit(solution)/shard_map/pallas_call | solution.py:314
  (6 shorter events, 0.0 us)
Async XLA Ops:
  0.6 13.6 %copy-start.4 = (s32[2,16]{1,0:T(2,128)S(1)}, s32[2,16]{1,0:T(2,128)}, u32[]{:S(2)}) copy-start(s32[2,16]{1,0:T(2,128)} %param.14) | copy-start | bytes 388
  0.6 17.8 %copy-start.5 = (f32[16]{0:T(128)S(1)}, f32[16]{0:T(128)}, u32[]{:S(2)}) copy-start(f32[16]{0:T(128)} %param.9) | copy-start | bytes 196
  2.5 51.3 %copy-start = (bf16[2048,768]{1,0:T(8,128)(2,1)S(1)}, bf16[2048,768]{1,0:T(8,128)(2,1)}, u32[]{:S(2)}) copy-start(bf16[2048,768]{1,0:T(8,128)(2,1)} %weight.1) | copy-start | bytes 9437188
  2.6 51.3 %copy-start.1 = (bf16[2,2,2048]{2,1,0:T(2,128)(2,1)S(1)}, bf16[2,2,2048]{2,1,0:T(2,128)(2,1)}, u32[]{:S(2)}) copy-start(bf16[2,2,2048]{2,1,0:T(2,128)(2,1)} %k.7) | copy-start | bytes 49156
  2.6 51.3 %copy-start.2 = (bf16[2,2,2048]{2,1,0:T(2,128)(2,1)S(1)}, bf16[2,2,2048]{2,1,0:T(2,128)(2,1)}, u32[]{:S(2)}) copy-start(bf16[2,2,2048]{2,1,0:T(2,128)(2,1)} %v.7) | copy-start | bytes 49156
  2.6 11.6 %collective-permute-start = (bf16[2,272,128]{2,1,0:T(8,128)(2,1)}, bf16[2,272,128]{2,1,0:T(8,128)(2,1)S(1)}, u32[]{:S(2)}, u32[]{:S(2)}) collective-permute-start(bf16[2,272,128]{2,1,0:T(8,128)(2,1)} %shard_map.95), channel_id=1, source_target_pairs={{0,8},{2,10},{4,12},{6,14},{8,0},{10,2},{12,4},{14,6},{1,9},{3,11}... | collective-permute-start | bytes 417800 | tf_op jit(solution)/shard_map/ppermute | solution.py:243
  9.2 8.5 %collective-permute-start.1 = (bf16[2,272,128]{2,1,0:T(8,128)(2,1)}, bf16[2,272,128]{2,1,0:T(8,128)(2,1)S(1)}, u32[]{:S(2)}, u32[]{:S(2)}) collective-permute-start(bf16[2,272,128]{2,1,0:T(8,128)(2,1)} %get-tuple-element.24), channel_id=1, source_target_pairs={{0,2},{2,0},{4,6},{6,4},{8,10},{10,8},{12,14},{14,12},{1,3},{3,1},... | collective-permute-start | bytes 417800 | tf_op jit(solution)/shard_map/ppermute | solution.py:243
  10.7 8.7 %collective-permute-start.2 = (bf16[2,272,128]{2,1,0:T(8,128)(2,1)}, bf16[2,272,128]{2,1,0:T(8,128)(2,1)S(1)}, u32[]{:S(2)}, u32[]{:S(2)}) collective-permute-start(bf16[2,272,128]{2,1,0:T(8,128)(2,1)} %get-tuple-element.25), channel_id=1, source_target_pairs={{0,4},{2,6},{4,0},{6,2},{8,12},{10,14},{12,8},{14,10},{1,5},{3,7},... | collective-permute-start | bytes 417800 | tf_op jit(solution)/shard_map/ppermute | solution.py:243
  12.3 16.8 %collective-permute-start.3 = (bf16[2,272,128]{2,1,0:T(8,128)(2,1)}, bf16[2,272,128]{2,1,0:T(8,128)(2,1)S(1)}, u32[]{:S(2)}, u32[]{:S(2)}) collective-permute-start(bf16[2,272,128]{2,1,0:T(8,128)(2,1)} %get-tuple-element.26), channel_id=1, source_target_pairs={{0,6},{2,4},{4,2},{6,0},{8,14},{10,12},{12,10},{14,8},{1,7},{3,5},... | collective-permute-start | bytes 417800 | tf_op jit(solution)/shard_map/ppermute | solution.py:243
  12.7 17.1 %collective-permute-start.4 = (bf16[2,272,128]{2,1,0:T(8,128)(2,1)}, bf16[2,272,128]{2,1,0:T(8,128)(2,1)S(1)}, u32[]{:S(2)}, u32[]{:S(2)}) collective-permute-start(bf16[2,272,128]{2,1,0:T(8,128)(2,1)} %get-tuple-element.27), channel_id=1, source_target_pairs={{0,10},{2,8},{4,14},{6,12},{8,2},{10,0},{12,6},{14,4},{1,11},{3,9}... | collective-permute-start | bytes 417800 | tf_op jit(solution)/shard_map/ppermute | solution.py:243
  14.2 15.6 %collective-permute-start.5 = (bf16[2,272,128]{2,1,0:T(8,128)(2,1)}, bf16[2,272,128]{2,1,0:T(8,128)(2,1)S(1)}, u32[]{:S(2)}, u32[]{:S(2)}) collective-permute-start(bf16[2,272,128]{2,1,0:T(8,128)(2,1)} %get-tuple-element.28), channel_id=1, source_target_pairs={{0,12},{2,14},{4,8},{6,10},{8,4},{10,6},{12,0},{14,2},{1,13},{3,15... | collective-permute-start | bytes 417800 | tf_op jit(solution)/shard_map/ppermute | solution.py:243
  17.7 12.2 %collective-permute-start.6 = (bf16[2,272,128]{2,1,0:T(8,128)(2,1)}, bf16[2,272,128]{2,1,0:T(8,128)(2,1)S(1)}, u32[]{:S(2)}, u32[]{:S(2)}) collective-permute-start(bf16[2,272,128]{2,1,0:T(8,128)(2,1)} %get-tuple-element.29), channel_id=1, source_target_pairs={{0,14},{2,12},{4,10},{6,8},{8,6},{10,4},{12,2},{14,0},{1,15},{3,13... | collective-permute-start | bytes 417800 | tf_op jit(solution)/shard_map/ppermute | solution.py:243
  18.5 0.9 %copy-start.3 = (bf16[2,272,128]{2,1,0:T(8,128)(2,1)S(1)}, bf16[2,272,128]{2,1,0:T(8,128)(2,1)}, u32[]{:S(2)}) copy-start(bf16[2,272,128]{2,1,0:T(8,128)(2,1)} %get-tuple-element.30.chunk) | copy-start | bytes 417796
  30.9 10.1 %collective-permute-start.9 = (bf16[592,128]{1,0:T(8,128)(2,1)S(1)}, bf16[592,128]{1,0:T(8,128)(2,1)S(1)}, u32[]{:S(2)}, u32[]{:S(2)}) collective-permute-start(bf16[592,128]{1,0:T(8,128)(2,1)S(1)} %get-tuple-element.34), channel_id=1, source_target_pairs={{0,8},{2,10},{4,12},{6,14},{8,0},{10,2},{12,4},{14,6},{1,9},{3,11}... | collective-permute-start | bytes 454664 | tf_op jit(solution)/shard_map/ppermute | solution.py:243
  36.2 7.3 %collective-permute-start.10 = (bf16[528,128]{1,0:T(8,128)(2,1)S(1)}, bf16[528,128]{1,0:T(8,128)(2,1)S(1)}, u32[]{:S(2)}, u32[]{:S(2)}) collective-permute-start(bf16[528,128]{1,0:T(8,128)(2,1)S(1)} %get-tuple-element.35), channel_id=1, source_target_pairs={{0,2},{2,0},{4,6},{6,4},{8,10},{10,8},{12,14},{14,12},{1,3},{3,1},... | collective-permute-start | bytes 405512 | tf_op jit(solution)/shard_map/ppermute | solution.py:243
  37.2 12.8 %collective-permute-start.11 = (bf16[528,128]{1,0:T(8,128)(2,1)S(1)}, bf16[528,128]{1,0:T(8,128)(2,1)S(1)}, u32[]{:S(2)}, u32[]{:S(2)}) collective-permute-start(bf16[528,128]{1,0:T(8,128)(2,1)S(1)} %get-tuple-element.36), channel_id=1, source_target_pairs={{0,4},{2,6},{4,0},{6,2},{8,12},{10,14},{12,8},{14,10},{1,5},{3,7},... | collective-permute-start | bytes 405512 | tf_op jit(solution)/shard_map/ppermute | solution.py:243
  37.3 12.8 %collective-permute-start.12 = (bf16[528,128]{1,0:T(8,128)(2,1)S(1)}, bf16[528,128]{1,0:T(8,128)(2,1)S(1)}, u32[]{:S(2)}, u32[]{:S(2)}) collective-permute-start(bf16[528,128]{1,0:T(8,128)(2,1)S(1)} %get-tuple-element.37), channel_id=1, source_target_pairs={{0,6},{2,4},{4,2},{6,0},{8,14},{10,12},{12,10},{14,8},{1,7},{3,5},... | collective-permute-start | bytes 405512 | tf_op jit(solution)/shard_map/ppermute | solution.py:243
  39.7 14.2 %collective-permute-start.13 = (bf16[528,128]{1,0:T(8,128)(2,1)S(1)}, bf16[528,128]{1,0:T(8,128)(2,1)S(1)}, u32[]{:S(2)}, u32[]{:S(2)}) collective-permute-start(bf16[528,128]{1,0:T(8,128)(2,1)S(1)} %get-tuple-element.38), channel_id=1, source_target_pairs={{0,10},{2,8},{4,14},{6,12},{8,2},{10,0},{12,6},{14,4},{1,11},{3,9}... | collective-permute-start | bytes 405512 | tf_op jit(solution)/shard_map/ppermute | solution.py:243
  41.0 5.2 %collective-permute-start.14 = (bf16[128,128]{1,0:T(8,128)(2,1)S(1)}, bf16[128,128]{1,0:T(8,128)(2,1)S(1)}, u32[]{:S(2)}, u32[]{:S(2)}) collective-permute-start(bf16[128,128]{1,0:T(8,128)(2,1)S(1)} %shard_map.100.have), channel_id=1, source_target_pairs={{0,2},{2,0},{4,6},{6,4},{8,10},{10,8},{12,14},{14,12},{1,3},{3,1},... | collective-permute-start | bytes 98312 | tf_op jit(solution)/shard_map/ppermute | solution.py:243
  43.5 13.1 %collective-permute-start.7 = (bf16[528,128]{1,0:T(8,128)(2,1)S(1)}, bf16[528,128]{1,0:T(8,128)(2,1)S(1)}, u32[]{:S(2)}, u32[]{:S(2)}) collective-permute-start(bf16[528,128]{1,0:T(8,128)(2,1)S(1)} %get-tuple-element.31), channel_id=1, source_target_pairs={{0,12},{2,14},{4,8},{6,10},{8,4},{10,6},{12,0},{14,2},{1,13},{3,15... | collective-permute-start | bytes 405512 | tf_op jit(solution)/shard_map/ppermute | solution.py:243
  46.2 10.3 %collective-permute-start.8 = (bf16[528,128]{1,0:T(8,128)(2,1)S(1)}, bf16[528,128]{1,0:T(8,128)(2,1)S(1)}, u32[]{:S(2)}, u32[]{:S(2)}) collective-permute-start(bf16[528,128]{1,0:T(8,128)(2,1)S(1)} %get-tuple-element.32), channel_id=1, source_target_pairs={{0,14},{2,12},{4,10},{6,8},{8,6},{10,4},{12,2},{14,0},{1,15},{3,13... | collective-permute-start | bytes 405512 | tf_op jit(solution)/shard_map/ppermute | solution.py:243
  49.9 6.0 %collective-permute-start.15 = (bf16[256,128]{1,0:T(8,128)(2,1)S(1)}, bf16[256,128]{1,0:T(8,128)(2,1)S(1)}, u32[]{:S(2)}, u32[]{:S(2)}) collective-permute-start(bf16[256,128]{1,0:T(8,128)(2,1)S(1)} %shard_map.101), channel_id=1, source_target_pairs={{0,4},{2,6},{4,0},{6,2},{8,12},{10,14},{12,8},{14,10},{1,5},{3,7},... | collective-permute-start | bytes 196616 | tf_op jit(solution)/shard_map/ppermute | solution.py:243
  56.5 1.3 %collective-permute-start.16 = (f32[2,8,768]{2,1,0:T(8,128)S(1)}, f32[2,8,768]{2,1,0:T(8,128)S(1)}, u32[]{:S(2)}, u32[]{:S(2)}) collective-permute-start(f32[2,8,768]{2,1,0:T(8,128)S(1)} %get-tuple-element.43), channel_id=1, source_target_pairs={{0,1},{1,0},{2,3},{3,2},{4,5},{5,4},{6,7},{7,6},{8,9},{9,8},{10,11... | collective-permute-start | bytes 147464 | tf_op jit(solution)/shard_map/ppermute | solution.py:340
